TPU v7x, 32 devices: a whole 2x2x4 slice. The times are simulated.
32 devices in a mesh: rows: 32 (over z, y, x, core).
Axes of the slice: x: 2, y: 2, z: 4, core: 2. Of those that a mesh axis runs over, the one named last changes fastest.
Arguments:
- covariates: float32 [65536, 128], P('rows'), may hold values from -6 to 6
- outcome: float32 [65536], P('rows'), may hold values from 0 to 3
- predictor: float32 [65536], P('rows'), may hold values from -1.5 to 1.5
- firm_id: int32 [65536], P('rows'), may hold values from 0 to 127
- dy_id: int32 [65536], P('rows'), may hold values from 0 to 2047
- pd_owner: int32 [65536, 1], P('rows'), may hold values from 0 to 31; in each aligned block of 2048 rows (0 to 2047, 2048 to 4095, ...) at most 128 rows name the same one
- pd_local: int32 [65536], P('rows'), may hold values from 0 to 15
Outputs:
- x_tilde: float32 [65536, 128], P('rows')
- z_tilde: float32 [65536], P('rows')
- gram: float32 [128, 128], P('rows')
- rhs: float32 [128], P('rows')
Inputs may be any that keep to these rules, and one draw needn't show every extreme that they name: `pd_owner`: among the rows of one device no owner is named more than 128 times, a bound that some block reaches.
All inputs are finite; a program needn't handle non-finite values.
Results may differ from a plain program's by a relative error of at most 0.0003.
Values sent between devices are 32-bit elements; how exact they have to be, the bound alone decides.
No kernel may reach another device: no remote copies, remote signals or barrier semaphores. Data moves between devices by JAX's collectives and lax.ppermute only.
A program may use at most 64 MiB of HBM per device.

v0:
```python
import math

import jax
import jax.numpy as jnp
from jax import lax
from jax.sharding import PartitionSpec as P

DY = 2048
FIRM_DEV = 128
PD_DEV = 16


def block_length(rows, segments):
    target = max(128, 1048576 // segments)
    return math.gcd(rows, target)


def onehot_sums(values, groups, segments):
    rows = values.shape[0]
    columns = values.shape[1]
    step = block_length(rows, segments)
    blocks = rows // step
    value_blocks = values.reshape(blocks, step, columns)
    group_blocks = groups.reshape(blocks, step)
    labels = jnp.arange(segments, dtype=jnp.int32)

    def accumulate(total, pair):
        block_values, block_groups = pair
        table = (block_groups[:, None] == labels[None, :]).astype(jnp.float32)
        added = jnp.dot(
            table.T,
            block_values,
            precision=lax.Precision.HIGHEST,
            preferred_element_type=jnp.float32,
        )
        return (total + added, None)

    start = jnp.zeros((segments, columns), jnp.float32)
    total, unused = lax.scan(accumulate, start, (value_blocks, group_blocks))
    return total


def onehot_pick(table, groups):
    rows = groups.shape[0]
    segments = table.shape[0]
    columns = table.shape[1]
    step = block_length(rows, segments)
    blocks = rows // step
    group_blocks = groups.reshape(blocks, step)
    labels = jnp.arange(segments, dtype=jnp.int32)

    def pick(carry, block_groups):
        selector = (block_groups[:, None] == labels[None, :]).astype(jnp.float32)
        picked = jnp.dot(
            selector, table, precision=lax.Precision.HIGHEST, preferred_element_type=jnp.float32
        )
        return (carry, picked)

    unused, picked = lax.scan(pick, jnp.int32(0), group_blocks)
    return picked.reshape(rows, columns)


def weighted_columns(covariates, working, weight):
    return jnp.concatenate(
        [weight[:, None] * covariates, (weight * working)[:, None], weight[:, None]], axis=1
    )


def split_sums(sums, width):
    return (sums[:, :width], sums[:, width], sums[:, width + 1])


def group_means(sum_x, sum_z, sum_w):
    denominator = jnp.where(sum_w > 0.0, sum_w, jnp.float32(1.0))
    return (sum_x / denominator[:, None], sum_z / denominator)


def subtract_means(covariates, working, mean_x, mean_z, groups):
    table = jnp.concatenate([mean_x, mean_z[:, None]], axis=1)
    picked = onehot_pick(table, groups)
    width = covariates.shape[1]
    return (covariates - picked[:, :width], working - picked[:, width])


def shards(covariates, outcome, predictor, firm_id, dy_id, pd_owner, pd_local):
    rows_dev = covariates.shape[0]
    width = covariates.shape[1]
    devices = lax.axis_size("rows")
    weight = jnp.exp(predictor)
    working = predictor + outcome / weight - 1.0
    sums = onehot_sums(weighted_columns(covariates, working, weight), firm_id, FIRM_DEV)
    mean_x, mean_z = group_means(*split_sums(sums, width))
    covariates, working = subtract_means(covariates, working, mean_x, mean_z, firm_id)
    sums = onehot_sums(weighted_columns(covariates, working, weight), dy_id, DY)
    sum_x, sum_z, sum_w = split_sums(sums, width)
    sum_x, sum_z, sum_w = lax.psum((sum_x, sum_z, sum_w), "rows")
    mean_x, mean_z = group_means(sum_x, sum_z, sum_w)
    covariates, working = subtract_means(covariates, working, mean_x, mean_z, dy_id)
    owners = pd_owner[:, 0]
    global_ids = owners * PD_DEV + pd_local
    sums = onehot_sums(weighted_columns(covariates, working, weight), global_ids, devices * PD_DEV)
    sum_x, sum_z, sum_w = split_sums(sums, width)
    sum_x, sum_z, sum_w = (
        lax.psum_scatter(sum_x, "rows", scatter_dimension=0, tiled=True),
        lax.psum_scatter(sum_z, "rows", scatter_dimension=0, tiled=True),
        lax.psum_scatter(sum_w, "rows", scatter_dimension=0, tiled=True),
    )
    mean_x, mean_z = group_means(sum_x, sum_z, sum_w)
    table_x, table_z = (
        lax.all_gather(mean_x, "rows", axis=0, tiled=True),
        lax.all_gather(mean_z, "rows", axis=0, tiled=True),
    )
    covariates, working = subtract_means(covariates, working, table_x, table_z, global_ids)
    scaled = weight[:, None] * covariates
    gram_term = jnp.dot(scaled.T, covariates, precision=lax.Precision.HIGHEST)
    rhs_term = jnp.dot(scaled.T, working, precision=lax.Precision.HIGHEST)
    total_rows = rows_dev * devices
    gram_all, rhs_all = lax.psum((gram_term, rhs_term), "rows")
    share = width // devices
    first_row = lax.axis_index("rows") * share
    gram_part = lax.dynamic_slice_in_dim(gram_all, first_row, share, 0)
    rhs_part = lax.dynamic_slice_in_dim(rhs_all, first_row, share, 0)
    return (covariates, working, gram_part / total_rows, rhs_part / total_rows)


def solution(mesh):
    in_specs = (
        P("rows", None),
        P("rows"),
        P("rows"),
        P("rows"),
        P("rows"),
        P("rows", None),
        P("rows"),
    )
    out_specs = (P("rows", None), P("rows"), P("rows", None), P("rows"))
    return jax.shard_map(shards, mesh=mesh, in_specs=in_specs, out_specs=out_specs, check_vma=False)
```

profile of v0, /device:TPU:0, one launch (start us, length us, event | category | flops | bytes accessed | tf_op | source)
XLA Modules:
  0.0 554.6 jit_solution(292329155089993818)
XLA Ops:
  7.2 1.6 copy.45
  8.9 0.6 copy-done.7
  9.5 0.8 fusion.19
  10.4 0.9 fusion.26
  11.3 1.3 broadcast_multiply_fusion.1
  12.6 0.9 concatenate.35
  13.5 2.6 copy.54
  16.1 1.9 concatenate.34
  17.9 3.2 pad_maximum_fusion
  21.2 11.9 %while.7 = (s32[]{:T(128)}, f32[2048,130]{0,1:T(8,128)S(1)}, s32[4,512]{1,0:T(4,128)S(1)}, f32[4,512,130]{2,1,0:T(8,128)}, s32[]{:T(128)}, /*index=5*/s32[]{:T(128)}) while((s32[]{:T(128)}, f32[2048,130]{0,1:T(8,128)S(1)}, s32[4,512]{1,0:T(4,128)S(1)}, f32[4,512,130]{2,1,0:T(8,128)}, s32[]{:T(128)}, /*index=5*/s32[]{:T(128)}) %tuple.66), condition=%wide.region_1.2_spmd.clone, body=%wide.region_0.1_spmd.clone.sunk | while | flops 1637359616 | bytes 2660947 | solution.py:39
  21.2 2.9 fusion.59
  24.1 2.9 fusion.59
  27.1 2.9 fusion.59
  30.1 2.9 fusion.59
  33.1 1.0 slice.50
  34.3 42.5 %all-reduce.4 = (f32[2048]{0:T(1024)S(1)}, f32[2048]{0:T(1024)S(1)}) all-reduce(f32[2048]{0:T(1024)S(1)} %bitcast.68, f32[2048]{0:T(1024)S(1)} %bitcast.67), channel_id=1, replica_groups=mesh['rows'=32] {'rows'}, use_global_device_ids=true, to_apply=%region_4.5 | all-reduce | flops 4096 | bytes 32768 | tf_op jit(solution)/shard_map/psum | solution.py:96
  76.8 90.3 %all-reduce.8.cloned.1.call-done = f32[2048,128]{0,1:T(8,128)} async-done(((f32[2048,128]{0,1:T(8,128)}), f32[2048,128]{0,1:T(8,128)}) %all-reduce.8.cloned.1.call-update) | async-done | bytes 1048592 | tf_op jit(solution)/shard_map/psum | solution.py:96
  167.0 1.3 broadcast_divide_fusion
  168.4 1.1 pad_maximum_fusion.5
  169.5 1.7 copy.49
  171.2 37.0 %while.6 = (s32[]{:T(128)}, f32[4,512,129]{1,0,2:T(4,128)}, s32[4,512]{1,0:T(4,128)S(1)}, f32[2048,129]{1,0:T(8,128)S(1)}, s32[]{:T(128)}, /*index=5*/s32[]{:T(128)}) while((s32[]{:T(128)}, f32[4,512,129]{1,0,2:T(4,128)}, s32[4,512]{1,0:T(4,128)S(1)}, f32[2048,129]{1,0:T(8,128)S(1)}, s32[]{:T(128)}, /*index=5*/s32[]{:T(128)}) %tuple.78), condition=%wide.region_6.7_spmd.clone, body=%wide.region_5.6_spmd.clone.sunk | while | flops 1624244224 | bytes 2383949 | solution.py:59
  171.3 2.5 fusion.57
  174.1 6.4 %dynamic_update_slice.11 = f32[4,512,129]{1,0,2:T(4,128)} dynamic-update-slice(f32[4,512,129]{1,0,2:T(4,128)} %get-tuple-element.294, f32[1,512,129]{1,0,2:T(1,128)S(1)} %copy.61, s32[]{:T(128)} %get-tuple-element.293, s32[]{:T(128)} %constant.48.clone.1..sunk, s32[]{:T(128)} %constant.48.clone.1..sunk) | dynamic-update-slice | bytes 528388 | tf_op jit(solution)/shard_map/while/body/jit(dynamic_update_index_in_dim)/dynamic_update_slice | solution.py:59
  180.5 2.5 fusion.57
  183.3 6.4 %dynamic_update_slice.11 = f32[4,512,129]{1,0,2:T(4,128)} dynamic-update-slice(f32[4,512,129]{1,0,2:T(4,128)} %get-tuple-element.294, f32[1,512,129]{1,0,2:T(1,128)S(1)} %copy.61, s32[]{:T(128)} %get-tuple-element.293, s32[]{:T(128)} %constant.48.clone.1..sunk, s32[]{:T(128)} %constant.48.clone.1..sunk) | dynamic-update-slice | bytes 528388 | tf_op jit(solution)/shard_map/while/body/jit(dynamic_update_index_in_dim)/dynamic_update_slice | solution.py:59
  189.8 2.5 fusion.57
  192.6 6.4 %dynamic_update_slice.11 = f32[4,512,129]{1,0,2:T(4,128)} dynamic-update-slice(f32[4,512,129]{1,0,2:T(4,128)} %get-tuple-element.294, f32[1,512,129]{1,0,2:T(1,128)S(1)} %copy.61, s32[]{:T(128)} %get-tuple-element.293, s32[]{:T(128)} %constant.48.clone.1..sunk, s32[]{:T(128)} %constant.48.clone.1..sunk) | dynamic-update-slice | bytes 528388 | tf_op jit(solution)/shard_map/while/body/jit(dynamic_update_index_in_dim)/dynamic_update_slice | solution.py:59
  199.0 2.5 fusion.57
  201.8 6.4 %dynamic_update_slice.11 = f32[4,512,129]{1,0,2:T(4,128)} dynamic-update-slice(f32[4,512,129]{1,0,2:T(4,128)} %get-tuple-element.294, f32[1,512,129]{1,0,2:T(1,128)S(1)} %copy.61, s32[]{:T(128)} %get-tuple-element.293, s32[]{:T(128)} %constant.48.clone.1..sunk, s32[]{:T(128)} %constant.48.clone.1..sunk) | dynamic-update-slice | bytes 528388 | tf_op jit(solution)/shard_map/while/body/jit(dynamic_update_index_in_dim)/dynamic_update_slice | solution.py:59
  208.3 1.4 pad.15
  209.7 0.4 copy.59
  210.1 0.8 copy-done.1
  211.2 1.7 fusion.14
  212.9 0.8 copy.55
  213.9 39.2 %all-reduce.3 = (f32[512]{0:T(512)S(1)}, f32[512]{0:T(512)S(1)}) all-reduce(f32[512]{0:T(512)S(1)} %bitcast.72, f32[512]{0:T(512)S(1)} %bitcast.71), channel_id=4, replica_groups=mesh['rows'=32] {'rows'}, use_global_device_ids=true, to_apply=%region_9.10.clone | all-reduce | flops 1024 | bytes 8192
  253.3 40.0 %all-reduce = f32[512]{0:T(512)S(1)} all-reduce(f32[512]{0:T(512)S(1)} %get-tuple-element.218), channel_id=1, replica_groups=mesh['rows'=32] {'rows'}, use_global_device_ids=true, to_apply=%add | all-reduce | flops 512 | bytes 4096
  293.4 53.4 %reduce-scatter.4.cloned.1.call-done = f32[16,128]{1,0:T(8,128)} async-done(((f32[512,128]{1,0:T(8,128)}), f32[16,128]{1,0:T(8,128)}) %reduce-scatter.4.cloned.1.call-update) | async-done | bytes 8208 | tf_op jit(solution)/shard_map/reduce_scatter | solution.py:104
  346.8 0.8 broadcast_divide_fusion.1
  347.5 37.2 %all_gather.6 = f32[512,128]{1,0:T(8,128)S(1)} all-gather(f32[16,128]{1,0:T(8,128)S(1)} %broadcast_divide_fusion.1), channel_id=1, replica_groups=mesh['rows'=32] {'rows'}, dimensions={0}, use_global_device_ids=true | all-gather | bytes 270336 | tf_op jit(solution)/shard_map/all_gather | solution.py:110
  384.8 2.6 fusion.13
  387.4 0.3 slice_subtract_fusion
  387.8 1.7 fusion.17
  389.4 0.9 convolution_bitcast_fusion
  390.3 37.2 %psum.39 = f32[128]{0:T(128)S(1)} all-reduce(f32[128]{0:T(128)S(1)} %convolution_bitcast_fusion), channel_id=1, replica_groups=mesh['rows'=32] {'rows'}, use_global_device_ids=true, to_apply=%region_11.12 | all-reduce | flops 128 | bytes 1024 | tf_op jit(solution)/shard_map/psum | solution.py:118
  427.6 0.6 dynamic-slice_multiply_fusion.1
  428.2 1.3 copy.53
  429.5 117.3 %all-reduce.10.cloned.1.call-done = f32[128,128]{1,0:T(8,128)} async-done(((f32[128,128]{1,0:T(8,128)}), f32[128,128]{1,0:T(8,128)}) %all-reduce.10.cloned.1.call-update) | async-done | bytes 65552 | tf_op jit(solution)/shard_map/psum | solution.py:118
  546.8 1.3 dynamic-slice_multiply_fusion
  (61 shorter events, 2.3 us)
Async XLA Ops:
  7.2 1.6 copy-start.5
  7.2 1.6 copy-start.4
  7.2 159.9 %all-reduce.8.cloned.1.call-start = ((), (), s32[]{:S(2)}) async-start(), calls=%async_computation.1 | async-start | bytes 2097152 | tf_op jit(solution)/shard_map/psum | solution.py:96
  8.8 0.7 copy-start.7
  11.3 1.3 copy-start
  13.5 4.4 copy-start.9
  33.0 1.2 copy-start.10
  33.1 1.2 copy-start.8
  34.1 312.6 %reduce-scatter.4.cloned.1.call-start = ((), (), s32[]{:S(2)}) async-start(), calls=%async_computation.3 | async-start | bytes 270336 | tf_op jit(solution)/shard_map/reduce_scatter | solution.py:104
  209.7 1.2 copy-start.1
  210.1 1.1 copy-start.2
  213.8 333.0 %all-reduce.10.cloned.1.call-start = ((), (), s32[]{:S(2)}) async-start(), calls=%async_computation.2 | async-start | bytes 131072 | tf_op jit(solution)/shard_map/psum | solution.py:118
  384.8 2.6 copy-start.3
  387.8 2.6 copy-start.6
Sparse Core Ops, SparseCore 0:
  34.2 132.7 all-reduce.7
  213.9 132.7 reduce-scatter.3
  427.7 119.0 all-reduce.9
where the time goes:
time: 557 us; the launch traced here: 555 us
  waiting for transfers between devices  261 us (47%)
  blocking collectives  196 us (35%)
  local copies, waits for them, and re-layouts  42.2 us (8%)
  matrix products  30.3 us (5%)
  between operations  14.1 us (3%)
  other arithmetic  10.5 us (2%)
    psum x1, waiting for transfers between devices, shards(): gram_all, rhs_all = lax.psum((gram_term, rhs_term), 'rows')  117 us
    psum x1, waiting for transfers between devices, shards(): sum_x, sum_z, sum_w = lax.psum((sum_x, sum_z, sum_w), 'rows')  90.3 us
    unnamed x2, blocking collectives  79.2 us
    reduce_scatter x1, waiting for transfers between devices, shards(): lax.psum_scatter(sum_x, 'rows', scatter_dimension=0, tiled=True)  53.4 us
    psum x1, blocking collectives, shards(): sum_x, sum_z, sum_w = lax.psum((sum_x, sum_z, sum_w), 'rows')  42.5 us
    all_gather x1, blocking collectives, shards(): lax.all_gather(mean_x, 'rows', axis=0, tiled=True)  37.2 us
    psum x1, blocking collectives, shards(): gram_all, rhs_all = lax.psum((gram_term, rhs_term), 'rows')  37.2 us
    dynamic_update_slice x8, local copies, waits for them, and re-layouts, onehot_pick(): unused, picked = lax.scan(pick, jnp.int32(0), group_blocks)  26.8 us
  transfers between devices with their start and end apart: 3, of which 3 were waited for; matrix products, arithmetic and copies ran while one was open for 0% of the time, Pallas kernels for 0%

commit v1 on v0

v1 whole, which is shorter than its diff:
```python
import functools
import math

import jax
import jax.numpy as jnp
from jax import lax
from jax.experimental import pallas as pl
from jax.experimental.pallas import tpu as pltpu
from jax.sharding import PartitionSpec as P

DY = 2048
FIRM_DEV = 128
PD_DEV = 16
LANES = 128
TILE = 8
VMEM_LIMIT = 48 * 1024 * 1024

BF16 = jnp.bfloat16
F32 = jnp.float32
I32 = jnp.int32


def iota(shape, dim):
    return lax.broadcasted_iota(I32, shape, dim)


def dot(a, b):
    return jnp.dot(a, b, preferred_element_type=F32)


def dot_exact(a, b):
    return jnp.dot(a, b, precision=lax.Precision.HIGHEST, preferred_element_type=F32)


def onehot(mask):
    return jnp.where(mask, 1.0, 0.0).astype(BF16)


def pieces(value, count):
    parts = []
    for _ in range(count):
        part = value.astype(BF16)
        parts.append(part)
        value = value - part.astype(F32)
    return parts


def pair(value):
    return jnp.concatenate(pieces(value, 2), axis=1)


def unpair(value):
    return value[:, :LANES] + value[:, LANES:]


def row_block(a):
    return slice(a * LANES, (a + 1) * LANES)


def weights_of(predictor, outcome):
    weight = jnp.exp(predictor)
    return weight, predictor + outcome / weight - 1.0


def scatter_half(ids, ids_t, weight, working, pairs_ref, base, blocks, width, out_ref, sums_ref):
    rows = ids.shape[0] * LANES
    count = blocks * width
    step = math.gcd(count, 256)
    for first in range(0, count, step):
        labels = iota((step, LANES), 0) + (base + first)
        table = jnp.concatenate(
            [onehot(labels == ids[a : a + 1, :]) for a in range(rows // LANES)], axis=1
        )
        sums = unpair(dot(table, pairs_ref[...]))
        out_ref[first // width : (first + step) // width, :width, :] = sums.reshape(
            step // width, width, LANES
        )
    block = lax.div(ids, I32(width))
    place = lax.rem(ids_t, I32(width))
    labels = iota((blocks, LANES), 0) + lax.div(base, I32(width))
    parts = pieces(weight, 3) + pieces(weight * working, 3)
    left = []
    for a in range(rows // LANES):
        mask = labels == block[a : a + 1, :]
        left.append(
            jnp.concatenate(
                [jnp.where(mask, part[a : a + 1, :].astype(F32), 0.0) for part in parts], axis=0
            ).astype(BF16)
        )
    right = jnp.concatenate(
        [onehot(iota((LANES, LANES), 1) == place[:, a : a + 1]) for a in range(rows // LANES)], axis=0
    )
    sums = dot(jnp.concatenate(left, axis=1), right)
    sums = [sums[i * blocks : (i + 1) * blocks, :] for i in range(6)]
    sum_w = sums[0] + sums[1] + sums[2]
    sum_z = sums[3] + sums[4] + sums[5]
    sum_z = pltpu.roll(sum_z, width, 1)
    out_ref[:, width, :] = jnp.where(iota((blocks, LANES), 1) < width, sum_w, sum_z)


def gather_half(ids, ids_t, means_ref, base, blocks, width, x_of, z, step=256):
    rows = ids.shape[0] * LANES
    count = blocks * width
    table = pair(means_ref[:, :width, :].reshape(count, LANES))
    x_new = []
    for a in range(rows // LANES):
        labels = iota((LANES, count), 1) + base
        picked = unpair(dot(onehot(labels == ids_t[:, a : a + 1]), table))
        x_new.append(x_of(a) - picked)
    mean_z = pltpu.roll(means_ref[:, width, :], LANES - width, 1)
    parts = jnp.concatenate([part.astype(F32) for part in pieces(mean_z, 3)], axis=0)
    left = jnp.transpose(parts)[:width, :].astype(BF16)
    block = lax.div(ids, I32(width)) - lax.div(base, I32(width))
    place = lax.rem(ids, I32(width))
    z_new = []
    for a in range(rows // LANES):
        mask = onehot(iota((blocks, LANES), 0) == block[a : a + 1, :])
        candidates = dot(left, jnp.concatenate([mask, mask, mask], axis=0))
        chosen = jnp.where(iota((width, LANES), 0) == place[a : a + 1, :], candidates, 0.0)
        z_new.append(z[a : a + 1, :] - jnp.sum(chosen, axis=0, keepdims=True))
    return x_new, jnp.concatenate(z_new, axis=0)


def firm_kernel(
    blocks, width, base_ref, x_ref, outcome_ref, predictor_ref, firm_ref, dy_ref,
    x1_ref, z1_ref, pairs_ref, out_ref,
):
    count = firm_ref.shape[0]
    firm = firm_ref[...]
    weight, working = weights_of(predictor_ref[...], outcome_ref[...])
    weight_t = jnp.transpose(weight)
    firm_t = jnp.transpose(firm)
    for a in range(count):
        pairs_ref[row_block(a), :] = pair(x_ref[row_block(a), :] * weight_t[:, a : a + 1])
    masks = [iota((FIRM_DEV, LANES), 0) == firm[a : a + 1, :] for a in range(count)]
    table = jnp.concatenate([onehot(mask) for mask in masks], axis=1)
    sum_x = unpair(dot(table, pairs_ref[...]))
    spread_w = jnp.zeros((FIRM_DEV, LANES), F32)
    spread_z = jnp.zeros((FIRM_DEV, LANES), F32)
    weighted = weight * working
    for a in range(count):
        spread_w += jnp.where(masks[a], weight[a : a + 1, :], 0.0)
        spread_z += jnp.where(masks[a], weighted[a : a + 1, :], 0.0)
    sum_w = jnp.sum(spread_w, axis=1, keepdims=True)
    sum_z = jnp.sum(spread_z, axis=1, keepdims=True)
    denominator = jnp.where(sum_w > 0.0, sum_w, 1.0)
    mean_x = pair(sum_x / denominator)
    mean_z = sum_z / denominator
    z1 = []
    for a in range(count):
        selector = onehot(iota((LANES, FIRM_DEV), 1) == firm_t[:, a : a + 1])
        x1 = x_ref[row_block(a), :] - unpair(dot(selector, mean_x))
        x1_ref[row_block(a), :] = x1
        pairs_ref[row_block(a), :] = pair(x1 * weight_t[:, a : a + 1])
        picked = jnp.sum(jnp.where(masks[a], mean_z, 0.0), axis=0, keepdims=True)
        z1.append(working[a : a + 1, :] - picked)
    z1 = jnp.concatenate(z1, axis=0)
    z1_ref[...] = z1
    dy = dy_ref[...]
    scatter_half(dy, jnp.transpose(dy), weight, z1, pairs_ref, base_ref[0], blocks, width, out_ref, None)


def sums_kernel(blocks, width, base_ref, pairs_ref, z1_ref, predictor_ref, dy_ref, out_ref):
    dy = dy_ref[...]
    weight = jnp.exp(predictor_ref[...])
    scatter_half(dy, jnp.transpose(dy), weight, z1_ref[...], pairs_ref, base_ref[0], blocks, width, out_ref, None)


def means_of(total, width):
    line = total[width : width + 1, :]
    diagonal = iota((width, LANES), 0) == iota((width, LANES), 1)
    sum_w = jnp.sum(jnp.where(diagonal, line, 0.0), axis=1, keepdims=True)
    mean_x = total[:width, :] / jnp.where(sum_w > 0.0, sum_w, 1.0)
    lane = iota((1, LANES), 1)
    divisor = pltpu.roll(jnp.where(lane < width, line, 1.0), width, 1)
    divisor = jnp.where(divisor > 0.0, divisor, 1.0)
    in_z = (lane >= width) & (lane < 2 * width)
    return mean_x, jnp.where(in_z, line / divisor, line)


def means_kernel(width, in_ref, out_ref):
    blocks, height = in_ref.shape[0], in_ref.shape[1]
    total = in_ref[0]
    for j in range(1, blocks):
        total = total + in_ref[j]
    mean_x, line = means_of(total, width)
    rest = jnp.zeros((height - width - 1, LANES), F32)
    result = jnp.concatenate([mean_x, line, rest], axis=0)
    for j in range(blocks):
        out_ref[j] = result


def gather_kernel(blocks, width, base_ref, x_ref, z_ref, means_ref, dy_ref, x_out, z_out):
    dy = dy_ref[...]
    x_new, z_new = gather_half(
        dy, jnp.transpose(dy), means_ref, base_ref[0], blocks, width, lambda a: x_ref[row_block(a), :], z_ref[...]
    )
    for a, value in enumerate(x_new):
        x_out[row_block(a), :] = value
    z_out[...] = z_new


def effect_kernel(
    blocks, width, pd_width, share, base_ref, x_ref, z_ref, means_ref, dy_ref, predictor_ref, owner_ref, local_ref,
    x2_ref, z2_ref, keep_ref, send_ref, weighted_ref, plain_ref,
):
    dy = dy_ref[...]
    weight = jnp.exp(predictor_ref[...])
    weight_t = jnp.transpose(weight)
    x_new, z2 = gather_half(
        dy, jnp.transpose(dy), means_ref, base_ref[0], blocks, width, lambda a: x_ref[row_block(a), :], z_ref[...]
    )
    for a, value in enumerate(x_new):
        x2_ref[row_block(a), :] = value
        plain_ref[row_block(a), :] = pair(value)
        weighted_ref[row_block(a), :] = pair(value * weight_t[:, a : a + 1])
    z2_ref[...] = z2
    effect = owner_ref[...] * PD_DEV + local_ref[...]
    effect_t = jnp.transpose(effect)
    for index, out_ref in ((1, keep_ref), (2, send_ref)):
        scatter_half(effect, effect_t, weight, z2, weighted_ref, base_ref[index], blocks, pd_width, out_ref, None)
    gram = lax.dot_general(
        weighted_ref[...], plain_ref[...], (((0,), (0,)), ((), ())), preferred_element_type=F32
    )
    gram = unpair(gram[:LANES, :] + gram[LANES:, :])
    left = [part.astype(F32) for part in pieces(weight * z2, 3)]
    rhs = jnp.zeros((TILE, 2 * LANES), F32)
    for a in range(dy.shape[0]):
        rows = jnp.concatenate([part[a : a + 1, :] for part in left] + [jnp.zeros((TILE - 3, LANES), F32)], axis=0)
        rhs += dot(rows.astype(BF16), plain_ref[row_block(a), :])
    rhs = unpair(jnp.sum(rhs, axis=0, keepdims=True))
    core = base_ref[3]
    spare = jnp.zeros((keep_ref.shape[1] - pd_width - 2 - share, LANES), F32)
    for j in range(blocks):
        even = gram[2 * j * share : (2 * j + 1) * share, :]
        odd = gram[(2 * j + 1) * share : (2 * j + 2) * share, :]
        keep_ref[j, pd_width + 1 :, :] = jnp.concatenate([jnp.where(core == 0, even, odd), rhs, spare], axis=0)
        send_ref[j, pd_width + 1 :, :] = jnp.concatenate([jnp.where(core == 0, odd, even), rhs, spare], axis=0)


def final_means_kernel(width, in_ref, out_ref, total_ref):
    blocks, height = in_ref.shape[0], in_ref.shape[1]
    total = in_ref[0]
    for j in range(1, blocks):
        total = total + in_ref[j]
    mean_x, line = means_of(total, width)
    rest = jnp.zeros((height - width - 1, LANES), F32)
    result = jnp.concatenate([mean_x, line, rest], axis=0)
    for j in range(blocks):
        out_ref[j] = result
    total_ref[...] = total


def last_kernel(
    blocks, width, share, total_rows, base_ref, x_ref, z_ref, own_ref, other_ref, total_ref, owner_ref, local_ref,
    x_out, z_out, gram_out, rhs_out,
):
    effect = owner_ref[...] * PD_DEV + local_ref[...]
    effect_t = jnp.transpose(effect)
    x_new, z_new = gather_half(
        effect, effect_t, own_ref, base_ref[1], blocks, width, lambda a: x_ref[row_block(a), :], z_ref[...]
    )
    x_new, z_new = gather_half(
        effect, effect_t, other_ref, base_ref[2], blocks, width, lambda a: x_new[a], z_new
    )
    for a, value in enumerate(x_new):
        x_out[row_block(a), :] = value
    z_out[...] = z_new
    first = base_ref[4]
    pick = jnp.where(iota((TILE, LANES), 1) == iota((TILE, LANES), 0) + first, 1.0, 0.0)
    gram_less = jnp.zeros((TILE, LANES), F32)
    rhs_less = jnp.zeros((1, LANES), F32)
    for ref in (own_ref, other_ref):
        mean_x = ref[:, :width, :]
        line = ref[:, width, :][:, None, :]
        lane = iota((blocks, width, LANES), 2)
        place = iota((blocks, width, LANES), 1)
        sum_w = jnp.sum(jnp.where(lane == place, line, 0.0), axis=2, keepdims=True)
        mean_z = jnp.sum(jnp.where(lane == place + width, line, 0.0), axis=2, keepdims=True)
        sum_x = (sum_w * mean_x).reshape(blocks * width, LANES)
        mean_x = mean_x.reshape(blocks * width, LANES)
        mean_z = mean_z.reshape(blocks * width, 1)
        columns = lax.dot_general(
            pick, sum_x, (((1,), (1,)), ((), ())), precision=lax.Precision.HIGHEST, preferred_element_type=F32
        )
        gram_less += dot_exact(columns, mean_x)
        rhs_less += jnp.sum(sum_x * mean_z, axis=0, keepdims=True)
    total = total_ref[...]
    scale = 1.0 / total_rows
    gram_out[...] = (total[width + 1 : width + 1 + share, :] - gram_less[:share, :]) * scale
    rhs = (total[width + 1 + share : width + 2 + share, :] - rhs_less) * scale
    rhs_out[...] = pltpu.roll(rhs, LANES - first, 1)[:, :share]


def call(kernel, outs, args, scratch=(), flops=0):
    size = sum(math.prod(v.shape) * v.dtype.itemsize for v in list(args) + list(outs))
    specs = [pl.BlockSpec(memory_space=pltpu.VMEM)] * len(args)
    if args[0].ndim == 1:
        specs[0] = pl.BlockSpec(memory_space=pltpu.SMEM)
    return pl.pallas_call(
        kernel,
        out_shape=tuple(outs),
        in_specs=specs,
        out_specs=tuple(pl.BlockSpec(memory_space=pltpu.VMEM) for _ in outs),
        scratch_shapes=scratch,
        cost_estimate=pl.CostEstimate(flops=flops, bytes_accessed=size, transcendentals=0),
        compiler_params=pltpu.CompilerParams(vmem_limit_bytes=VMEM_LIMIT),
    )(*args)


def shaped(*shape, dtype=F32):
    return jax.ShapeDtypeStruct(shape, dtype)


def shards(covariates, outcome, predictor, firm_id, dy_id, pd_owner, pd_local):
    rows, width = covariates.shape
    devices = lax.axis_size("rows")
    blocks = devices // 2
    share = width // devices
    total_rows = rows * devices
    dy_width, pd_width = DY // devices, PD_DEV
    dy_high, pd_high = dy_width + TILE, pd_width + TILE
    lines = rows // LANES
    me = lax.axis_index("rows")
    core = lax.rem(me, 2)
    groups = [[core_of + 2 * chip for chip in range(blocks)] for core_of in range(2)]
    partner = [(i, i ^ 1) for i in range(devices)]
    outcome, predictor, firm, dy, owner, local = (
        v.reshape(lines, LANES) for v in (outcome, predictor, firm_id, dy_id, pd_owner, pd_local)
    )
    dy_half, pd_half = blocks * dy_width, blocks * pd_width
    zero = jnp.zeros((), I32)

    def table(*values):
        return jnp.stack([jnp.asarray(v, I32) for v in values])

    keep_base = table(core * dy_half)
    send_base = table((1 - core) * dy_half)
    pd_base = table((1 - core) * dy_half, core * pd_half, (1 - core) * pd_half, core, me * share)

    def exchange(v):
        return lax.ppermute(v, "rows", partner)

    def across(v):
        return lax.all_to_all(v, "rows", 0, 0, axis_index_groups=groups)

    wide = 4 * rows * LANES
    x1, z1, pairs, send = call(
        functools.partial(firm_kernel, blocks, dy_width),
        (
            shaped(rows, width),
            shaped(lines, LANES),
            shaped(rows, 2 * LANES, dtype=BF16),
            shaped(blocks, dy_high, LANES),
        ),
        (send_base, covariates, outcome, predictor, firm, dy),
        flops=wide * (dy_half + 2 * FIRM_DEV),
    )
    got = exchange(send)
    (keep,) = call(
        functools.partial(sums_kernel, blocks, dy_width),
        (shaped(blocks, dy_high, LANES),),
        (keep_base, pairs, z1, predictor, dy),
        flops=wide * dy_half,
    )
    sums = across(keep + got)
    (means,) = call(
        functools.partial(means_kernel, dy_width),
        (shaped(blocks, dy_high, LANES),),
        (sums,),
    )
    means = across(means)
    other = exchange(means)
    x1, z1 = call(
        functools.partial(gather_kernel, blocks, dy_width),
        (shaped(rows, width), shaped(lines, LANES)),
        (keep_base, x1, z1, means, dy),
        flops=wide * dy_half,
    )
    x2, z2, keep, send = call(
        functools.partial(effect_kernel, blocks, dy_width, pd_width, share),
        (
            shaped(rows, width),
            shaped(lines, LANES),
            shaped(blocks, pd_high, LANES),
            shaped(blocks, pd_high, LANES),
        ),
        (pd_base, x1, z1, other, dy, predictor, owner, local),
        scratch=(pltpu.VMEM((rows, 2 * LANES), BF16), pltpu.VMEM((rows, 2 * LANES), BF16)),
        flops=wide * (dy_half + 2 * pd_half + 2 * LANES),
    )
    sums = across(keep + exchange(send))
    means, total = call(
        functools.partial(final_means_kernel, pd_width),
        (shaped(blocks, pd_high, LANES), shaped(pd_high, LANES)),
        (sums,),
    )
    means = across(means)
    other = exchange(means)
    x3, z3, gram, rhs = call(
        functools.partial(last_kernel, blocks, pd_width, share, total_rows),
        (shaped(rows, width), shaped(lines, LANES), shaped(share, LANES), shaped(1, share)),
        (pd_base, x2, z2, means, other, total, owner, local),
        flops=wide * 2 * pd_half,
    )
    return x3, z3.reshape(rows), gram, rhs.reshape(share)


def solution(mesh):
    in_specs = (
        P("rows", None),
        P("rows"),
        P("rows"),
        P("rows"),
        P("rows"),
        P("rows", None),
        P("rows"),
    )
    out_specs = (P("rows", None), P("rows"), P("rows", None), P("rows"))
    return jax.shard_map(shards, mesh=mesh, in_specs=in_specs, out_specs=out_specs, check_vma=False)
```

time: 557 us -> 89.2 us (0.16)
  waiting for transfers between devices: 261 us -> 3.17 us
  blocking collectives: 196 us -> 68.8 us
  local copies, waits for them, and re-layouts: 42.2 us -> 2.89 us
  matrix products: 30.3 us -> 0 us
  between operations: 14.1 us -> 0.72 us
  Pallas kernels: 0 us -> 12.3 us
  other arithmetic: 10.5 us -> 0.11 us
    psum x2 -> x0, waiting for transfers between devices: 208 us -> none  [the longest x1 117 us: shards(): gram_all, rhs_all = lax.psum((gram_term, rhs_term), 'rows')]
    psum x2 -> x0, blocking collectives: 79.7 us -> none  [the longest x1 42.5 us: shards(): sum_x, sum_z, sum_w = lax.psum((sum_x, sum_z, sum_w), 'rows')]
    unnamed x2 -> x0, blocking collectives: 79.2 us -> none
    all_to_all x0 -> x4, blocking collectives: none -> 68.8 us  [across(): return lax.all_to_all(v, 'rows', 0, 0, axis_index_groups=groups)]
    reduce_scatter x1 -> x0, waiting for transfers between devices: 53.4 us -> none  [shards(): lax.psum_scatter(sum_x, 'rows', scatter_dimension=0, tiled=True)]
    all_gather x1 -> x0, blocking collectives: 37.2 us -> none  [shards(): lax.all_gather(mean_x, 'rows', axis=0, tiled=True)]
    dot_general x14 -> x0, matrix products: 30.3 us -> none  [the longest x6 14.2 us: accumulate(): jnp.dot(table.T, block_values, precision=lax.Precision.HIGHEST, preferred...]
    dynamic_update_slice x8 -> x0, local copies, waits for them, and re-layouts: 26.8 us -> none  [onehot_pick(): unused, picked = lax.scan(pick, jnp.int32(0), group_blocks)]
  transfers between devices with their start and end apart: 3 -> 4, of which waited for: 3 -> 3; matrix products, arithmetic and copies ran while one was open for 0% -> 0% of each run, Pallas kernels for 0% -> 3%
where the time goes in v1:
time: 89.2 us; the launch traced here: 88.7 us
  blocking collectives  68.8 us (77%)
  Pallas kernels  12.3 us (14%)
  waiting for transfers between devices  3.17 us (4%)
  local copies, waits for them, and re-layouts  2.89 us (3%)
    all_to_all x4, blocking collectives, across(): return lax.all_to_all(v, 'rows', 0, 0, axis_index_groups=groups)  68.8 us
    pallas_call x7, Pallas kernels, call(): pl.pallas_call(kernel, out_shape=tuple(outs), in_specs=specs, out_specs=t...  12.3 us
    ppermute x4, waiting for transfers between devices, exchange(): return lax.ppermute(v, 'rows', partner)  3.17 us
    unnamed x16, local copies, waits for them, and re-layouts  2.81 us
  transfers between devices with their start and end apart: 4, of which 3 were waited for; matrix products, arithmetic and copies ran while one was open for 0% of the time, Pallas kernels for 3%

profile of v1, /device:TPU:0, one launch (start us, length us, event | category | flops | bytes accessed | tf_op | source)
XLA Modules:
  0.0 88.7 jit_solution(10854757526320462319)
XLA Ops:
  0.6 0.0 copy-start.3
  0.6 0.0 copy-start.2
  0.7 0.0 copy-start.1
  0.7 0.7 copy-done.3
  1.3 0.0 copy-done.2
  1.4 0.0 copy-done.1
  1.4 0.0 copy-start
  1.4 1.2 %copy-done = f32[2048,128]{1,0:T(8,128)S(1)} copy-done((f32[2048,128]{1,0:T(8,128)S(1)}, f32[2048,128]{1,0:T(8,128)}, u32[]{:S(2)}) %copy-start) | copy-done | bytes 1048600
  2.6 0.0 copy-start.4
  2.6 0.7 copy-done.4
  3.3 2.7 %shard_map.102 = (f32[2048,128]{1,0:T(8,128)S(1)}, f32[16,128]{1,0:T(8,128)S(1)}, bf16[2048,256]{1,0:T(8,128)(2,1)S(1)}, f32[16,72,128]{2,1,0:T(8,128)S(1)}) custom-call(s32[1]{0:T(128)} %bitcast.base_ref, f32[2048,128]{1,0:T(8,128)S(1)} %copy-done, f32[16,128]{1,0:T(8,128)S(1)} %bitcast.14, f32[16,128]{1,0:T(8,128)S(1)} %bitcast.16, ...), custom_call_target="tpu_custom_call" | custom-call | flops 1342177280 | bytes 3776516 | tf_op jit(solution)/shard_map/pallas_call | solution.py:300
  6.0 0.0 copy-start.5
  6.0 0.5 collective-permute-start
  6.6 0.2 copy-done.5
  6.7 1.4 %shard_map.103 = f32[16,72,128]{2,1,0:T(8,128)S(1)} custom-call(s32[1]{0:T(128)} %bitcast.5.base_ref, bf16[2048,256]{1,0:T(8,128)(2,1)S(1)} %get-tuple-element.22.pairs_ref, f32[16,128]{1,0:T(8,128)S(1)} %get-tuple-element.21.z1_ref.z_ref, f32[16,128]{1,0:T(8,128)S(1)} %bitcast.17, s32[16,128]{1,0:T(8,128)S(1)} %bitcast.20), custom_call_target="tpu_custom_call" | custom-call | flops 1073741824 | bytes 1662980 | tf_op jit(solution)/shard_map/pallas_call | solution.py:300
  8.2 0.0 collective-permute-done
  8.2 0.1 add.6
  8.3 25.8 %all_to_all.20.in_ref = f32[16,72,128]{2,1,0:T(8,128)S(1)} all-to-all(f32[16,72,128]{2,1,0:T(8,128)S(1)} %add.6), channel_id=1, replica_groups={{0,2,4,6,8,10,12,14,16,18,20,22,24,26,28,30},{1,3,5,7,9,11,13,15,17,19,..., dimensions={0} | all-to-all | bytes 1179648 | tf_op jit(solution)/shard_map/all_to_all | solution.py:345
  34.1 0.1 shard_map.104
  34.2 20.0 %all_to_all.21.means_ref = f32[16,72,128]{2,1,0:T(8,128)S(1)} all-to-all(f32[16,72,128]{2,1,0:T(8,128)S(1)} %shard_map.104), channel_id=1, replica_groups={{0,2,4,6,8,10,12,14,16,18,20,22,24,26,28,30},{1,3,5,7,9,11,13,15,17,19,..., dimensions={0} | all-to-all | bytes 1179648 | tf_op jit(solution)/shard_map/all_to_all | solution.py:345
  54.2 0.0 collective-permute-start.1
  54.2 0.1 stack.27.base_ref
  54.3 0.0 copy-start.6
  54.3 0.0 copy-start.7
  54.3 1.5 %shard_map.105 = (f32[2048,128]{1,0:T(8,128)S(1)}, f32[16,128]{1,0:T(8,128)S(1)}) custom-call(s32[1]{0:T(128)} %bitcast.5.base_ref, f32[2048,128]{1,0:T(8,128)S(1)} %get-tuple-element.20.x_ref, f32[16,128]{1,0:T(8,128)S(1)} %get-tuple-element.21.z1_ref.z_ref, f32[16,72,128]{2,1,0:T(8,128)S(1)} %all_to_all.21.means_ref, s32[16,128]{1,0:T(8,128)S(1)} %bitcast.21), custom_call_target="tpu_custom_call" | custom-call | flops 1073741824 | bytes 2711556 | tf_op jit(solution)/shard_map/pallas_call | solution.py:300
  55.8 0.4 collective-permute-done.1.means_ref
  56.2 0.0 copy-done.6
  56.2 0.0 copy-done.7
  56.2 3.6 %shard_map.106 = (f32[2048,128]{1,0:T(8,128)S(1)}, f32[16,128]{1,0:T(8,128)S(1)}, f32[16,24,128]{2,1,0:T(8,128)S(1)}, f32[16,24,128]{2,1,0:T(8,128)S(1)}) custom-call(s32[5]{0:T(128)S(1)} %stack.27.base_ref, f32[2048,128]{1,0:T(8,128)S(1)} %get-tuple-element.24.x_ref, f32[16,128]{1,0:T(8,128)S(1)} %get-tuple-element.25.z_ref, ...), custom_call_target="tpu_custom_call" | custom-call | flops 1879048192 | bytes 3129364 | tf_op jit(solution)/shard_map/pallas_call | solution.py:300
  59.8 0.2 collective-permute-start.2
  60.0 1.3 %collective-permute-done.2 = f32[16,24,128]{2,1,0:T(8,128)S(1)} collective-permute-done((f32[16,24,128]{2,1,0:T(8,128)S(1)}, f32[16,24,128]{2,1,0:T(8,128)S(1)}, u32[]{:S(2)}, u32[]{:S(2)}) %collective-permute-start.2) | collective-permute-done | bytes 196640 | tf_op jit(solution)/shard_map/ppermute | solution.py:342
  61.3 11.5 %all_to_all.22.in_ref = f32[16,24,128]{2,1,0:T(8,128)S(1)} all-to-all(f32[16,24,128]{2,1,0:T(8,128)S(1)} %add.7), channel_id=1, replica_groups={{0,2,4,6,8,10,12,14,16,18,20,22,24,26,28,30},{1,3,5,7,9,11,13,15,17,19,..., dimensions={0} | all-to-all | bytes 393216 | tf_op jit(solution)/shard_map/all_to_all | solution.py:345
  72.8 0.1 shard_map.107
  72.9 11.5 %all_to_all.23.own_ref = f32[16,24,128]{2,1,0:T(8,128)S(1)} all-to-all(f32[16,24,128]{2,1,0:T(8,128)S(1)} %get-tuple-element.30), channel_id=1, replica_groups={{0,2,4,6,8,10,12,14,16,18,20,22,24,26,28,30},{1,3,5,7,9,11,13,15,17,19,..., dimensions={0} | all-to-all | bytes 393216 | tf_op jit(solution)/shard_map/all_to_all | solution.py:345
  84.5 0.0 collective-permute-start.3
  84.5 1.4 %collective-permute-done.3.other_ref = f32[16,24,128]{2,1,0:T(8,128)S(1)} collective-permute-done((f32[16,24,128]{2,1,0:T(8,128)S(1)}, f32[16,24,128]{2,1,0:T(8,128)S(1)}, u32[]{:S(2)}, u32[]{:S(2)}) %collective-permute-start.3) | collective-permute-done | bytes 196640 | tf_op jit(solution)/shard_map/ppermute | solution.py:342
  85.9 2.8 %shard_map.108 = (f32[2048,128]{1,0:T(8,128)}, f32[16,128]{1,0:T(8,128)}, f32[4,128]{1,0:T(4,128)}, f32[1,4]{1,0:T(1,128)}) custom-call(s32[5]{0:T(128)S(1)} %stack.27.base_ref, f32[2048,128]{1,0:T(8,128)S(1)} %get-tuple-element.26.x_ref, f32[16,128]{1,0:T(8,128)S(1)} %get-tuple-element.27.z_ref, f32[16,24,128]{2,1,0:T(8,128)S(1)} %all_to_all.23.own_ref, ...), custom_call_target="tpu_custom_call" | custom-call | flops 536870912 | bytes 2537508 | tf_op jit(solution)/shard_map/pallas_call | solution.py:300
  (1 shorter events, 0.0 us)
Async XLA Ops:
  0.6 0.7 copy-start.3
  0.6 0.7 copy-start.2
  0.7 0.7 copy-start.1
  1.4 1.2 %copy-start = (f32[2048,128]{1,0:T(8,128)S(1)}, f32[2048,128]{1,0:T(8,128)}, u32[]{:S(2)}) copy-start(f32[2048,128]{1,0:T(8,128)} %x_ref.1) | copy-start | bytes 3145732
  2.6 0.7 copy-start.4
  6.0 0.7 copy-start.5
  6.0 2.1 %collective-permute-start = (f32[16,72,128]{2,1,0:T(8,128)S(1)}, f32[16,72,128]{2,1,0:T(8,128)S(1)}, u32[]{:S(2)}, u32[]{:S(2)}) collective-permute-start(f32[16,72,128]{2,1,0:T(8,128)S(1)} %get-tuple-element.23), channel_id=1, source_target_pairs={{0,1},{1,0},{2,3},{3,2},{4,5},{5,4},{6,7},{7,6},{8,9},{9,8},{10,11... | collective-permute-start | bytes 1769480 | tf_op jit(solution)/shard_map/ppermute | solution.py:342
  54.2 2.0 %collective-permute-start.1 = (f32[16,72,128]{2,1,0:T(8,128)S(1)}, f32[16,72,128]{2,1,0:T(8,128)S(1)}, u32[]{:S(2)}, u32[]{:S(2)}) collective-permute-start(f32[16,72,128]{2,1,0:T(8,128)S(1)} %all_to_all.21.means_ref), channel_id=1, source_target_pairs={{0,1},{1,0},{2,3},{3,2},{4,5},{5,4},{6,7},{7,6},{8,9},{9,8},{10,11... | collective-permute-start | bytes 1769480 | tf_op jit(solution)/shard_map/ppermute | solution.py:342
  54.3 1.9 %copy-start.6 = (s32[2048,1]{0,1:T(1,128)S(1)}, s32[2048,1]{0,1:T(1,128)}, u32[]{:S(2)}) copy-start(s32[2048,1]{0,1:T(1,128)} %param.12) | copy-start | bytes 24580
  54.3 1.9 %copy-start.7 = (s32[2048]{0:T(1024)S(1)}, s32[2048]{0:T(1024)}, u32[]{:S(2)}) copy-start(s32[2048]{0:T(1024)} %param.13) | copy-start | bytes 24580
  59.8 1.5 %collective-permute-start.2 = (f32[16,24,128]{2,1,0:T(8,128)S(1)}, f32[16,24,128]{2,1,0:T(8,128)S(1)}, u32[]{:S(2)}, u32[]{:S(2)}) collective-permute-start(f32[16,24,128]{2,1,0:T(8,128)S(1)} %get-tuple-element.29), channel_id=1, source_target_pairs={{0,1},{1,0},{2,3},{3,2},{4,5},{5,4},{6,7},{7,6},{8,9},{9,8},{10,11... | collective-permute-start | bytes 589832 | tf_op jit(solution)/shard_map/ppermute | solution.py:342
  84.5 1.4 %collective-permute-start.3 = (f32[16,24,128]{2,1,0:T(8,128)S(1)}, f32[16,24,128]{2,1,0:T(8,128)S(1)}, u32[]{:S(2)}, u32[]{:S(2)}) collective-permute-start(f32[16,24,128]{2,1,0:T(8,128)S(1)} %all_to_all.23.own_ref), channel_id=1, source_target_pairs={{0,1},{1,0},{2,3},{3,2},{4,5},{5,4},{6,7},{7,6},{8,9},{9,8},{10,11... | collective-permute-start | bytes 589832 | tf_op jit(solution)/shard_map/ppermute | solution.py:342

commit v2 on v1

v2 whole, which is shorter than its diff:
```python
import functools
import math

import jax
import jax.numpy as jnp
from jax import lax
from jax.experimental import pallas as pl
from jax.experimental.pallas import tpu as pltpu
from jax.sharding import PartitionSpec as P

DY = 2048
FIRM_DEV = 128
PD_DEV = 16
LANES = 128
TILE = 8
VMEM_LIMIT = 48 * 1024 * 1024

BF16 = jnp.bfloat16
F32 = jnp.float32
I32 = jnp.int32


def iota(shape, dim):
    return lax.broadcasted_iota(I32, shape, dim)


def dot(a, b):
    return jnp.dot(a, b, preferred_element_type=F32)


def dot_exact(a, b):
    return jnp.dot(a, b, precision=lax.Precision.HIGHEST, preferred_element_type=F32)


def onehot(mask):
    return jnp.where(mask, 1.0, 0.0).astype(BF16)


def pieces(value, count):
    parts = []
    for _ in range(count):
        part = value.astype(BF16)
        parts.append(part)
        value = value - part.astype(F32)
    return parts


def pair(value):
    return jnp.concatenate(pieces(value, 2), axis=1)


def unpair(value):
    return value[:, :LANES] + value[:, LANES:]


def row_block(a):
    return slice(a * LANES, (a + 1) * LANES)


def weights_of(predictor, outcome):
    weight = jnp.exp(predictor)
    return weight, predictor + outcome / weight - 1.0


def scatter_half(ids, ids_t, weight, working, pairs_ref, base, blocks, width, out_ref):
    lines = ids.shape[0]
    count = blocks * width
    step = math.gcd(count, 256)
    for first in range(0, count, step):
        labels = iota((step, LANES), 0) + (base + first)
        table = jnp.concatenate([onehot(labels == ids[a : a + 1, :]) for a in range(lines)], axis=1)
        sums = unpair(dot(table, pairs_ref[...]))
        out_ref[first // width : (first + step) // width, :width, :] = sums.reshape(
            step // width, width, LANES
        )
    block = lax.div(ids, I32(width))
    place = lax.rem(ids_t, I32(width))
    labels = iota((blocks, LANES), 0) + lax.div(base, I32(width))
    parts = [part.astype(F32) for part in pieces(weight, 3) + pieces(weight * working, 3)]
    left = []
    for a in range(lines):
        mask = labels == block[a : a + 1, :]
        left.append(jnp.concatenate([jnp.where(mask, part[a : a + 1, :], 0.0) for part in parts], axis=0))
    left = jnp.concatenate(left, axis=1).astype(BF16)
    right = jnp.concatenate(
        [onehot(iota((LANES, LANES), 1) == place[:, a : a + 1]) for a in range(lines)], axis=0
    )
    sums = dot(left, right)
    sums = [sums[i * blocks : (i + 1) * blocks, :] for i in range(6)]
    out_ref[:, width, :] = sums[0] + sums[1] + sums[2]
    out_ref[:, width + 1, :] = sums[3] + sums[4] + sums[5]
    spare = out_ref.shape[1] - width - 2
    if spare:
        out_ref[:, width + 2 :, :] = jnp.zeros((blocks, spare, LANES), F32)


def gather_half(ids, ids_t, means_ref, base, blocks, width, x_of, z):
    lines = ids.shape[0]
    count = blocks * width
    table = pair(means_ref[:, :width, :].reshape(count, LANES))
    x_new = []
    for a in range(lines):
        labels = iota((LANES, count), 1) + base
        picked = unpair(dot(onehot(labels == ids_t[:, a : a + 1]), table))
        x_new.append(x_of(a) - picked)
    parts = jnp.concatenate([part.astype(F32) for part in pieces(means_ref[:, width + 1, :], 3)], axis=0)
    left = jnp.transpose(parts)[:width, :].astype(BF16)
    block = lax.div(ids, I32(width)) - lax.div(base, I32(width))
    place = lax.rem(ids, I32(width))
    z_new = []
    for a in range(lines):
        mask = onehot(iota((blocks, LANES), 0) == block[a : a + 1, :])
        candidates = dot(left, jnp.concatenate([mask, mask, mask], axis=0))
        chosen = jnp.where(iota((width, LANES), 0) == place[a : a + 1, :], candidates, 0.0)
        z_new.append(z[a : a + 1, :] - jnp.sum(chosen, axis=0, keepdims=True))
    return x_new, jnp.concatenate(z_new, axis=0)


def firm_kernel(
    blocks, width, base_ref, x_hbm, outcome_hbm, predictor_hbm, firm_hbm, dy_hbm,
    x1_ref, z1_ref, pairs_ref, out_ref, x_ref, outcome_ref, predictor_ref, firm_ref, dy_ref, sems,
):
    small = [(firm_hbm, firm_ref), (predictor_hbm, predictor_ref), (outcome_hbm, outcome_ref), (dy_hbm, dy_ref)]
    copies = [pltpu.make_async_copy(src, dst, sems.at[i]) for i, (src, dst) in enumerate(small)]
    count = firm_ref.shape[0]
    chunk = max(1, count // 4)
    starts = list(range(0, count, chunk))
    for i, a in enumerate(starts):
        span = slice(a * LANES, (a + chunk) * LANES)
        copies.append(pltpu.make_async_copy(x_hbm.at[span, :], x_ref.at[span, :], sems.at[len(small) + i]))
    for copy in copies:
        copy.start()
    for copy in copies[: len(small)]:
        copy.wait()
    firm = firm_ref[...]
    weight, working = weights_of(predictor_ref[...], outcome_ref[...])
    weight_t = jnp.transpose(weight)
    firm_t = jnp.transpose(firm)
    masks = [iota((FIRM_DEV, LANES), 0) == firm[a : a + 1, :] for a in range(count)]
    spread_w = jnp.zeros((FIRM_DEV, LANES), F32)
    spread_z = jnp.zeros((FIRM_DEV, LANES), F32)
    weighted = weight * working
    for a in range(count):
        spread_w += jnp.where(masks[a], weight[a : a + 1, :], 0.0)
        spread_z += jnp.where(masks[a], weighted[a : a + 1, :], 0.0)
    sum_w = jnp.sum(spread_w, axis=1, keepdims=True)
    sum_z = jnp.sum(spread_z, axis=1, keepdims=True)
    denominator = jnp.where(sum_w > 0.0, sum_w, 1.0)
    mean_z = sum_z / denominator
    table = jnp.concatenate([onehot(mask) for mask in masks], axis=1)
    for i, a in enumerate(starts):
        copies[len(small) + i].wait()
        for b in range(a, a + chunk):
            pairs_ref[row_block(b), :] = pair(x_ref[row_block(b), :] * weight_t[:, b : b + 1])
    mean_x = pair(unpair(dot(table, pairs_ref[...])) / denominator)
    z1 = []
    for a in range(count):
        selector = onehot(iota((LANES, FIRM_DEV), 1) == firm_t[:, a : a + 1])
        x1 = x_ref[row_block(a), :] - unpair(dot(selector, mean_x))
        x1_ref[row_block(a), :] = x1
        pairs_ref[row_block(a), :] = pair(x1 * weight_t[:, a : a + 1])
        picked = jnp.sum(jnp.where(masks[a], mean_z, 0.0), axis=0, keepdims=True)
        z1.append(working[a : a + 1, :] - picked)
    z1 = jnp.concatenate(z1, axis=0)
    z1_ref[...] = z1
    dy = dy_ref[...]
    scatter_half(dy, jnp.transpose(dy), weight, z1, pairs_ref, base_ref[0], blocks, width, out_ref)


def sums_kernel(blocks, width, base_ref, pairs_ref, z1_ref, predictor_ref, dy_ref, out_ref):
    dy = dy_ref[...]
    weight = jnp.exp(predictor_ref[...])
    scatter_half(dy, jnp.transpose(dy), weight, z1_ref[...], pairs_ref, base_ref[0], blocks, width, out_ref)


def total_kernel(in_ref, out_ref):
    total = in_ref[0]
    for j in range(1, in_ref.shape[0]):
        total = total + in_ref[j]
    out_ref[...] = total


def means_kernel(width, mine_ref, got_ref, out_ref, *rest_ref):
    total = mine_ref[...] + got_ref[...]
    line_w = total[width : width + 1, :]
    line_z = total[width + 1 : width + 2, :]
    diagonal = iota((width, LANES), 0) == iota((width, LANES), 1)
    sum_w = jnp.sum(jnp.where(diagonal, line_w, 0.0), axis=1, keepdims=True)
    mean_x = total[:width, :] / jnp.where(sum_w > 0.0, sum_w, 1.0)
    mean_z = line_z / jnp.where(line_w > 0.0, line_w, 1.0)
    height = out_ref.shape[1]
    rest = jnp.zeros((height - width - 2, LANES), F32)
    result = jnp.concatenate([mean_x, line_w, mean_z, rest], axis=0)
    for j in range(out_ref.shape[0]):
        out_ref[j] = result
    if rest_ref:
        rest_ref[0][...] = total[height:, :]


def gather_kernel(blocks, width, base_ref, x_ref, z_ref, means_ref, dy_ref, x_out, z_out):
    dy = dy_ref[...]
    x_new, z_new = gather_half(
        dy, jnp.transpose(dy), means_ref, base_ref[0], blocks, width, lambda a: x_ref[row_block(a), :], z_ref[...]
    )
    for a, value in enumerate(x_new):
        x_out[row_block(a), :] = value
    z_out[...] = z_new


def effect_kernel(
    blocks, width, pd_width, base_ref, x_ref, z_ref, means_ref, dy_ref, predictor_ref, owner_ref, local_ref,
    x2_ref, z2_ref, weighted_ref, send_ref,
):
    dy = dy_ref[...]
    weight = jnp.exp(predictor_ref[...])
    weight_t = jnp.transpose(weight)
    x_new, z2 = gather_half(
        dy, jnp.transpose(dy), means_ref, base_ref[0], blocks, width, lambda a: x_ref[row_block(a), :], z_ref[...]
    )
    for a, value in enumerate(x_new):
        x2_ref[row_block(a), :] = value
        weighted_ref[row_block(a), :] = pair(value * weight_t[:, a : a + 1])
    z2_ref[...] = z2
    effect = owner_ref[...] * PD_DEV + local_ref[...]
    scatter_half(
        effect, jnp.transpose(effect), weight, z2, weighted_ref, base_ref[2], blocks, pd_width, send_ref
    )


def gram_kernel(
    blocks, pd_width, share, base_ref, x2_ref, z2_ref, weighted_ref, predictor_ref, owner_ref, local_ref,
    keep_ref, gram_ref, plain_ref,
):
    weight = jnp.exp(predictor_ref[...])
    z2 = z2_ref[...]
    lines = z2.shape[0]
    effect = owner_ref[...] * PD_DEV + local_ref[...]
    scatter_half(
        effect, jnp.transpose(effect), weight, z2, weighted_ref, base_ref[1], blocks, pd_width, keep_ref
    )
    for a in range(lines):
        plain_ref[row_block(a), :] = pair(x2_ref[row_block(a), :])
    gram = lax.dot_general(
        weighted_ref[...], plain_ref[...], (((0,), (0,)), ((), ())), preferred_element_type=F32
    )
    gram = unpair(gram[:LANES, :] + gram[LANES:, :])
    left = [part.astype(F32) for part in pieces(weight * z2, 3)]
    none = jnp.zeros((TILE - 3, LANES), F32)
    left = jnp.concatenate(
        [jnp.concatenate([part[a : a + 1, :] for part in left] + [none], axis=0) for a in range(lines)], axis=1
    )
    rhs = unpair(jnp.sum(dot(left.astype(BF16), plain_ref[...]), axis=0, keepdims=True))
    spare = jnp.zeros((gram_ref.shape[1] - 4 * share - 1, LANES), F32)
    half = blocks * 2 * share
    for j in range(blocks):
        low = gram[2 * j * share : 2 * (j + 1) * share, :]
        high = gram[half + 2 * j * share : half + 2 * (j + 1) * share, :]
        gram_ref[j] = jnp.concatenate([low, high, rhs, spare], axis=0)


def last_kernel(
    blocks, width, share, total_rows, base_ref, x_ref, z_ref, own_ref, other_ref, mine_ref, got_ref, owner_ref,
    local_ref, x_hbm, z_out, gram_out, rhs_out, x_out, sems,
):
    effect = owner_ref[...] * PD_DEV + local_ref[...]
    effect_t = jnp.transpose(effect)
    x_new, z_new = gather_half(
        effect, effect_t, own_ref, base_ref[1], blocks, width, lambda a: x_ref[row_block(a), :], z_ref[...]
    )
    x_new, z_new = gather_half(
        effect, effect_t, other_ref, base_ref[2], blocks, width, lambda a: x_new[a], z_new
    )
    copies = []
    count = len(x_new)
    chunk = max(1, count // 4)
    for a, value in enumerate(x_new):
        x_out[row_block(a), :] = value
        if a % chunk == chunk - 1:
            span = slice((a + 1 - chunk) * LANES, (a + 1) * LANES)
            copies.append(pltpu.make_async_copy(x_out.at[span, :], x_hbm.at[span, :], sems.at[a // chunk]))
            copies[-1].start()
    z_out[...] = z_new
    me, core, high = base_ref[4], base_ref[3], base_ref[5]
    first = me * share
    pick = jnp.where(iota((TILE, LANES), 1) == iota((TILE, LANES), 0) + first, 1.0, 0.0)
    gram_less = jnp.zeros((TILE, LANES), F32)
    rhs_less = jnp.zeros((1, LANES), F32)
    for ref in (own_ref, other_ref):
        mean_x = ref[:, :width, :]
        diagonal = iota((blocks, width, LANES), 2) == iota((blocks, width, LANES), 1)
        sum_w = jnp.sum(jnp.where(diagonal, ref[:, width, :][:, None, :], 0.0), axis=2, keepdims=True)
        mean_z = jnp.sum(jnp.where(diagonal, ref[:, width + 1, :][:, None, :], 0.0), axis=2, keepdims=True)
        sum_x = (sum_w * mean_x).reshape(blocks * width, LANES)
        mean_x = mean_x.reshape(blocks * width, LANES)
        mean_z = mean_z.reshape(blocks * width, 1)
        columns = lax.dot_general(
            pick, sum_x, (((1,), (1,)), ((), ())), precision=lax.Precision.HIGHEST, preferred_element_type=F32
        )
        gram_less += dot_exact(columns, mean_x)
        rhs_less += jnp.sum(sum_x * mean_z, axis=0, keepdims=True)
    total = mine_ref[...] + got_ref[...]
    gram = jnp.zeros((share, LANES), F32)
    for place in range(4):
        here = (high == place // 2) & (core == place % 2)
        gram = jnp.where(here, total[place * share : (place + 1) * share, :], gram)
    scale = 1.0 / total_rows
    gram_out[...] = (gram - gram_less[:share, :]) * scale
    rhs = (total[4 * share : 4 * share + 1, :] - rhs_less) * scale
    rhs_out[...] = pltpu.roll(rhs, LANES - first, 1)[:, :share]
    for copy in copies:
        copy.wait()


VMEM = pl.BlockSpec(memory_space=pltpu.VMEM)
SMEM = pl.BlockSpec(memory_space=pltpu.SMEM)
HBM = pl.BlockSpec(memory_space=pltpu.HBM)


def call(kernel, outs, args, scratch=(), flops=0, in_specs=None, out_specs=None):
    size = sum(math.prod(v.shape) * v.dtype.itemsize for v in list(args) + list(outs))
    return pl.pallas_call(
        kernel,
        out_shape=tuple(outs),
        in_specs=in_specs or [SMEM if v.ndim == 1 else VMEM for v in args],
        out_specs=tuple(out_specs or [VMEM] * len(outs)),
        scratch_shapes=scratch,
        cost_estimate=pl.CostEstimate(flops=flops, bytes_accessed=size, transcendentals=0),
        compiler_params=pltpu.CompilerParams(vmem_limit_bytes=VMEM_LIMIT),
    )(*args)


def shaped(*shape, dtype=F32):
    return jax.ShapeDtypeStruct(shape, dtype)


def rounded(rows):
    return -(-rows // TILE) * TILE


def shards(covariates, outcome, predictor, firm_id, dy_id, pd_owner, pd_local):
    rows, width = covariates.shape
    devices = lax.axis_size("rows")
    blocks = devices // 4
    share = width // devices
    total_rows = rows * devices
    dy_width, pd_width = DY // (2 * blocks), devices * PD_DEV // (2 * blocks)
    dy_high, pd_high = rounded(dy_width + 2), rounded(pd_width + 2)
    gram_high = rounded(4 * share + 1)
    lines = rows // LANES
    me = lax.axis_index("rows")
    core = lax.rem(me, 2)
    high = lax.div(me, devices // 2)
    groups = [
        [half * (devices // 2) + core_of + 2 * chip for chip in range(blocks)]
        for half in range(2)
        for core_of in range(2)
    ]
    partner = [(i, i ^ 1) for i in range(devices)]
    opposite = [(i, (i + devices // 2) % devices) for i in range(devices)]
    outcome, predictor, firm, dy, owner, local = (
        v.reshape(lines, LANES) for v in (outcome, predictor, firm_id, dy_id, pd_owner, pd_local)
    )
    dy_half, pd_half = blocks * dy_width, blocks * pd_width

    def table(*values):
        return jnp.stack([jnp.asarray(v, I32) for v in values])

    keep_base = table(core * dy_half)
    send_base = table((1 - core) * dy_half)
    pd_base = table((1 - core) * dy_half, core * pd_half, (1 - core) * pd_half, core, me, high)

    def to_core(v):
        return lax.ppermute(v, "rows", partner)

    def to_half(v):
        return lax.ppermute(v, "rows", opposite)

    def across(v):
        return lax.all_to_all(v, "rows", 0, 0, axis_index_groups=groups)

    def total_of(v):
        return call(total_kernel, (shaped(*v.shape[1:]),), (v,))[0]

    wide = 4 * rows * LANES
    count = min(4, lines)
    x1, z1, pairs, send = call(
        functools.partial(firm_kernel, blocks, dy_width),
        (
            shaped(rows, width),
            shaped(lines, LANES),
            shaped(rows, 2 * LANES, dtype=BF16),
            shaped(blocks, dy_high, LANES),
        ),
        (send_base, covariates, outcome, predictor, firm, dy),
        scratch=(
            pltpu.VMEM((rows, width), F32),
            pltpu.VMEM((lines, LANES), F32),
            pltpu.VMEM((lines, LANES), F32),
            pltpu.VMEM((lines, LANES), I32),
            pltpu.VMEM((lines, LANES), I32),
            pltpu.SemaphoreType.DMA((4 + count,)),
        ),
        flops=wide * (dy_half + 2 * FIRM_DEV),
        in_specs=[SMEM] + [HBM] * 5,
    )
    got = to_core(send)
    (keep,) = call(
        functools.partial(sums_kernel, blocks, dy_width),
        (shaped(blocks, dy_high, LANES),),
        (keep_base, pairs, z1, predictor, dy),
        flops=wide * dy_half,
    )
    mine = total_of(across(keep + got))
    (means,) = call(
        functools.partial(means_kernel, dy_width), (shaped(blocks, dy_high, LANES),), (mine, to_half(mine))
    )
    means = across(means)
    other = to_core(means)
    x1, z1 = call(
        functools.partial(gather_kernel, blocks, dy_width),
        (shaped(rows, width), shaped(lines, LANES)),
        (keep_base, x1, z1, means, dy),
        flops=wide * dy_half,
    )
    x2, z2, pairs, send = call(
        functools.partial(effect_kernel, blocks, dy_width, pd_width),
        (
            shaped(rows, width),
            shaped(lines, LANES),
            shaped(rows, 2 * LANES, dtype=BF16),
            shaped(blocks, pd_high, LANES),
        ),
        (pd_base, x1, z1, other, dy, predictor, owner, local),
        flops=wide * (dy_half + pd_half),
    )
    got = to_core(send)
    keep, gram = call(
        functools.partial(gram_kernel, blocks, pd_width, share),
        (shaped(blocks, pd_high, LANES), shaped(blocks, gram_high, LANES)),
        (pd_base, x2, z2, pairs, predictor, owner, local),
        scratch=(pltpu.VMEM((rows, 2 * LANES), BF16),),
        flops=wide * (pd_half + 2 * LANES),
    )
    mine = total_of(across(jnp.concatenate([keep + got, gram], axis=1)))
    means, gram = call(
        functools.partial(means_kernel, pd_width),
        (shaped(blocks, pd_high, LANES), shaped(gram_high, LANES)),
        (mine, to_half(mine)),
    )
    got = to_core(gram)
    means = across(means)
    other = to_core(means)
    x3, z3, gram, rhs = call(
        functools.partial(last_kernel, blocks, pd_width, share, total_rows),
        (shaped(rows, width), shaped(lines, LANES), shaped(share, LANES), shaped(1, share)),
        (pd_base, x2, z2, means, other, gram, got, owner, local),
        scratch=(pltpu.VMEM((rows, width), F32), pltpu.SemaphoreType.DMA((count,))),
        flops=wide * 2 * pd_half,
        out_specs=[HBM, VMEM, VMEM, VMEM],
    )
    return x3, z3.reshape(rows), gram, rhs.reshape(share)


def solution(mesh):
    in_specs = (
        P("rows", None),
        P("rows"),
        P("rows"),
        P("rows"),
        P("rows"),
        P("rows", None),
        P("rows"),
    )
    out_specs = (P("rows", None), P("rows"), P("rows", None), P("rows"))
    return jax.shard_map(shards, mesh=mesh, in_specs=in_specs, out_specs=out_specs, check_vma=False)
```

time: 89.2 us -> 78.5 us (0.88)
  blocking collectives: 68.8 us -> 45.5 us
  starting transfers between devices: 0.73 us -> 6.75 us
  waiting for transfers between devices: 3.17 us -> 6.89 us
  Pallas kernels: 12.3 us -> 14 us
  other arithmetic: 0.11 us -> 1.18 us
    all_to_all x4, blocking collectives: 68.8 us -> 45.5 us  [across(): return lax.all_to_all(v, 'rows', 0, 0, axis_index_groups=groups)]
    ppermute x4 -> x7, starting transfers between devices: 0.73 us -> 6.75 us  [the longest x2 5.42 us: to_half(): return lax.ppermute(v, 'rows', opposite)]
    ppermute x4 -> x7, waiting for transfers between devices: 3.17 us -> 6.89 us  [the longest x2 5.49 us: to_half(): return lax.ppermute(v, 'rows', opposite)]
    pallas_call x7 -> x10, Pallas kernels: 12.3 us -> 14 us  [call(): pl.pallas_call(kernel, out_shape=tuple(outs), in_specs=in_specs or [SMEM...]
    add x2, other arithmetic: 0.11 us -> 1.16 us  [the longest x1 1.13 us: shards(): mine = total_of(across(keep + got))]
  transfers between devices with their start and end apart: 4 -> 7, of which waited for: 3 -> 5; matrix products, arithmetic and copies ran while one was open for 0% -> 0% of each run, Pallas kernels for 3% -> 6%
where the time goes in v2:
time: 78.5 us; the launch traced here: 78 us
  blocking collectives  45.5 us (58%)
  Pallas kernels  14 us (18%)
  waiting for transfers between devices  6.89 us (9%)
  starting transfers between devices  6.75 us (9%)
  local copies, waits for them, and re-layouts  2.89 us (4%)
  other arithmetic  1.18 us (2%)
    all_to_all x4, blocking collectives, across(): return lax.all_to_all(v, 'rows', 0, 0, axis_index_groups=groups)  45.5 us
    pallas_call x10, Pallas kernels, call(): pl.pallas_call(kernel, out_shape=tuple(outs), in_specs=in_specs or [SMEM...  14 us
    ppermute x2, waiting for transfers between devices, to_half(): return lax.ppermute(v, 'rows', opposite)  5.49 us
    ppermute x2, starting transfers between devices, to_half(): return lax.ppermute(v, 'rows', opposite)  5.42 us
    unnamed x16, local copies, waits for them, and re-layouts  2.81 us
  transfers between devices with their start and end apart: 7, of which 5 were waited for; matrix products, arithmetic and copies ran while one was open for 0% of the time, Pallas kernels for 6%

profile of v2, /device:TPU:0, one launch (start us, length us, event | category | flops | bytes accessed | tf_op | source)
XLA Modules:
  0.0 78.0 jit_solution(17244649736215848014)
XLA Ops:
  0.6 0.0 copy-start.5
  0.6 0.0 copy-start.4
  0.7 0.0 copy-start
  0.7 0.7 copy-done.5
  1.3 0.0 copy-done.4
  1.4 0.0 copy-done
  1.4 0.0 copy-start.3
  1.4 1.2 %copy-done.3 = f32[2048,128]{1,0:T(8,128)S(1)} copy-done((f32[2048,128]{1,0:T(8,128)S(1)}, f32[2048,128]{1,0:T(8,128)}, u32[]{:S(2)}) %copy-start.3) | copy-done | bytes 1048600
  2.6 0.0 copy-start.6
  2.6 0.7 copy-done.6
  3.3 3.3 %shard_map.102 = (f32[2048,128]{1,0:T(8,128)S(1)}, f32[16,128]{1,0:T(8,128)S(1)}, bf16[2048,256]{1,0:T(8,128)(2,1)S(1)}, f32[8,136,128]{2,1,0:T(8,128)S(1)}) custom-call(s32[1]{0:T(128)} %bitcast.base_ref, f32[2048,128]{1,0:T(8,128)S(1)} %copy-done.3, f32[16,128]{1,0:T(8,128)S(1)} %bitcast.25, f32[16,128]{1,0:T(8,128)S(1)} %bitcast.15, ...), custom_call_target="tpu_custom_call" | custom-call | flops 1342177280 | bytes 3743748 | tf_op jit(solution)/shard_map/pallas_call | solution.py:321
  6.6 0.0 copy-start.7
  6.6 0.5 collective-permute-start
  7.1 0.2 copy-done.7
  7.3 1.3 %shard_map.103 = f32[8,136,128]{2,1,0:T(8,128)S(1)} custom-call(s32[1]{0:T(128)} %bitcast.6.base_ref, bf16[2048,256]{1,0:T(8,128)(2,1)S(1)} %get-tuple-element.24.pairs_ref, f32[16,128]{1,0:T(8,128)S(1)} %get-tuple-element.23.z1_ref.z_ref, f32[16,128]{1,0:T(8,128)S(1)} %bitcast.16, s32[16,128]{1,0:T(8,128)S(1)} %bitcast.28), custom_call_target="tpu_custom_call" | custom-call | flops 1073741824 | bytes 1630212 | tf_op jit(solution)/shard_map/pallas_call | solution.py:321
  8.6 0.2 collective-permute-done
  8.8 1.1 %add.6 = f32[8,136,128]{2,1,0:T(8,128)S(1)} add(f32[8,136,128]{2,1,0:T(8,128)S(1)} %shard_map.103, f32[8,136,128]{2,1,0:T(8,128)} %collective-permute-done) | non-fusion elementwise | flops 139264 | bytes 1671168 | tf_op jit(solution)/shard_map/add | solution.py:413
  10.0 16.3 %all_to_all.20.in_ref = f32[8,136,128]{2,1,0:T(8,128)S(1)} all-to-all(f32[8,136,128]{2,1,0:T(8,128)S(1)} %add.6), channel_id=1, replica_groups={{0,2,4,6,8,10,12,14},{1,3,5,7,9,11,13,15},{16,18,20,22,24,26,28,30},{17..., dimensions={0} | all-to-all | bytes 1114112 | tf_op jit(solution)/shard_map/all_to_all | solution.py:379
  26.3 2.7 %collective-permute-start.1 = (f32[136,128]{1,0:T(8,128)S(1)}, f32[136,128]{1,0:T(8,128)S(1)}, u32[]{:S(2)}, u32[]{:S(2)}) collective-permute-start(f32[136,128]{1,0:T(8,128)S(1)} %shard_map.104.mine_ref), channel_id=1, source_target_pairs={{0,16},{1,17},{2,18},{3,19},{4,20},{5,21},{6,22},{7,23},{8,24},{9,... | collective-permute-start | bytes 208904 | tf_op jit(solution)/shard_map/ppermute | solution.py:376
  29.0 3.4 %collective-permute-done.1.got_ref = f32[136,128]{1,0:T(8,128)S(1)} collective-permute-done((f32[136,128]{1,0:T(8,128)S(1)}, f32[136,128]{1,0:T(8,128)S(1)}, u32[]{:S(2)}, u32[]{:S(2)}) %collective-permute-start.1) | collective-permute-done | bytes 69664 | tf_op jit(solution)/shard_map/ppermute | solution.py:376
  32.3 0.1 shard_map.105
  32.4 10.9 %all_to_all.21.means_ref = f32[8,136,128]{2,1,0:T(8,128)S(1)} all-to-all(f32[8,136,128]{2,1,0:T(8,128)S(1)} %shard_map.105), channel_id=1, replica_groups={{0,2,4,6,8,10,12,14},{1,3,5,7,9,11,13,15},{16,18,20,22,24,26,28,30},{17..., dimensions={0} | all-to-all | bytes 1114112 | tf_op jit(solution)/shard_map/all_to_all | solution.py:379
  43.3 0.0 collective-permute-start.2
  43.3 0.1 stack.31.base_ref
  43.4 0.0 copy-start.1
  43.4 0.0 copy-start.2
  43.4 1.6 %shard_map.106 = (f32[2048,128]{1,0:T(8,128)S(1)}, f32[16,128]{1,0:T(8,128)S(1)}) custom-call(s32[1]{0:T(128)} %bitcast.6.base_ref, f32[2048,128]{1,0:T(8,128)S(1)} %get-tuple-element.22.x_ref, f32[16,128]{1,0:T(8,128)S(1)} %get-tuple-element.23.z1_ref.z_ref, f32[8,136,128]{2,1,0:T(8,128)S(1)} %all_to_all.21.means_ref, s32[16,128]{1,0:T(8,128)S(1)} %bitcast.29), custom_call_target="tpu_custom_call" | custom-call | flops 1073741824 | bytes 2678788 | tf_op jit(solution)/shard_map/pallas_call | solution.py:321
  45.0 0.3 collective-permute-done.2.means_ref
  45.3 0.0 copy-done.1
  45.3 0.0 copy-done.2
  45.3 2.6 %shard_map.107 = (f32[2048,128]{1,0:T(8,128)S(1)}, f32[16,128]{1,0:T(8,128)S(1)}, bf16[2048,256]{1,0:T(8,128)(2,1)S(1)}, f32[8,40,128]{2,1,0:T(8,128)S(1)}) custom-call(s32[6]{0:T(128)S(1)} %stack.31.base_ref, f32[2048,128]{1,0:T(8,128)S(1)} %get-tuple-element.26.x_ref, f32[16,128]{1,0:T(8,128)S(1)} %get-tuple-element.27.z_ref, ...), custom_call_target="tpu_custom_call" | custom-call | flops 1342177280 | bytes 3915800 | tf_op jit(solution)/shard_map/pallas_call | solution.py:321
  47.9 0.3 collective-permute-start.3
  48.2 1.9 %shard_map.108 = (f32[8,40,128]{2,1,0:T(8,128)S(1)}, f32[8,24,128]{2,1,0:T(8,128)S(1)}) custom-call(s32[6]{0:T(128)S(1)} %stack.31.base_ref, f32[2048,128]{1,0:T(8,128)S(1)} %get-tuple-element.28.x2_ref.x_ref, f32[16,128]{1,0:T(8,128)S(1)} %get-tuple-element.29.z2_ref.z_ref, bf16[2048,256]{1,0:T(8,128)(2,1)S(1)} %get-tuple-element.30.weighted_ref, ...), custom_call_target="tpu_custom_call" | custom-call | flops 536870912 | bytes 2392088 | tf_op jit(solution)/shard_map/pallas_call | solution.py:321
  50.1 0.0 collective-permute-done.3
  50.1 9.7 %all_to_all.22.in_ref = f32[8,64,128]{2,1,0:T(8,128)S(1)} all-to-all(f32[8,64,128]{2,1,0:T(8,128)S(1)} %pad_maximum_fusion), channel_id=1, replica_groups={{0,2,4,6,8,10,12,14},{1,3,5,7,9,11,13,15},{16,18,20,22,24,26,28,30},{17..., dimensions={0} | all-to-all | bytes 524288 | tf_op jit(solution)/shard_map/all_to_all | solution.py:379
  59.9 2.8 %collective-permute-start.4 = (f32[64,128]{1,0:T(8,128)S(1)}, f32[64,128]{1,0:T(8,128)S(1)}, u32[]{:S(2)}, u32[]{:S(2)}) collective-permute-start(f32[64,128]{1,0:T(8,128)S(1)} %shard_map.109.mine_ref), channel_id=1, source_target_pairs={{0,16},{1,17},{2,18},{3,19},{4,20},{5,21},{6,22},{7,23},{8,24},{9,... | collective-permute-start | bytes 98312 | tf_op jit(solution)/shard_map/ppermute | solution.py:376
  62.6 2.1 %collective-permute-done.4.got_ref = f32[64,128]{1,0:T(8,128)S(1)} collective-permute-done((f32[64,128]{1,0:T(8,128)S(1)}, f32[64,128]{1,0:T(8,128)S(1)}, u32[]{:S(2)}, u32[]{:S(2)}) %collective-permute-start.4) | collective-permute-done | bytes 32800 | tf_op jit(solution)/shard_map/ppermute | solution.py:376
  64.8 0.1 shard_map.110
  64.9 8.6 %all_to_all.23.own_ref = f32[8,40,128]{2,1,0:T(8,128)S(1)} all-to-all(f32[8,40,128]{2,1,0:T(8,128)S(1)} %get-tuple-element.34), channel_id=1, replica_groups={{0,2,4,6,8,10,12,14},{1,3,5,7,9,11,13,15},{16,18,20,22,24,26,28,30},{17..., dimensions={0} | all-to-all | bytes 327680 | tf_op jit(solution)/shard_map/all_to_all | solution.py:379
  73.5 0.0 collective-permute-start.5
  73.5 0.5 collective-permute-start.6
  74.0 0.9 %collective-permute-done.6.got_ref = f32[24,128]{1,0:T(8,128)S(1)} collective-permute-done((f32[24,128]{1,0:T(8,128)S(1)}, f32[24,128]{1,0:T(8,128)S(1)}, u32[]{:S(2)}, u32[]{:S(2)}) %collective-permute-start.6) | collective-permute-done | bytes 12320 | tf_op jit(solution)/shard_map/ppermute | solution.py:373
  74.9 0.0 collective-permute-done.5.other_ref
  74.9 3.1 %shard_map.111 = (f32[2048,128]{1,0:T(8,128)}, f32[16,128]{1,0:T(8,128)}, f32[4,128]{1,0:T(4,128)}, f32[1,4]{1,0:T(1,128)}) custom-call(s32[6]{0:T(128)S(1)} %stack.31.base_ref, f32[2048,128]{1,0:T(8,128)S(1)} %get-tuple-element.28.x2_ref.x_ref, f32[16,128]{1,0:T(8,128)S(1)} %get-tuple-element.29.z2_ref.z_ref, f32[8,40,128]{2,1,0:T(8,128)S(1)} %all_to_all.23.own_ref, ...), custom_call_target="tpu_custom_call" | custom-call | flops 536870912 | bytes 2484264 | tf_op jit(solution)/shard_map/pallas_call | solution.py:321
  (4 shorter events, 0.1 us)
Async XLA Ops:
  0.6 0.7 copy-start.5
  0.6 0.7 copy-start.4
  0.7 0.7 copy-start
  1.4 1.2 %copy-start.3 = (f32[2048,128]{1,0:T(8,128)S(1)}, f32[2048,128]{1,0:T(8,128)}, u32[]{:S(2)}) copy-start(f32[2048,128]{1,0:T(8,128)} %x_hbm.1) | copy-start | bytes 3145732
  2.6 0.7 copy-start.6
  6.6 0.7 copy-start.7
  6.6 2.2 %collective-permute-start = (f32[8,136,128]{2,1,0:T(8,128)S(1)}, f32[8,136,128]{2,1,0:T(8,128)}, u32[]{:S(2)}, u32[]{:S(2)}) collective-permute-start(f32[8,136,128]{2,1,0:T(8,128)S(1)} %get-tuple-element.25), channel_id=1, source_target_pairs={{0,1},{1,0},{2,3},{3,2},{4,5},{5,4},{6,7},{7,6},{8,9},{9,8},{10,11... | collective-permute-start | bytes 1671176 | tf_op jit(solution)/shard_map/ppermute | solution.py:373
  26.3 6.0 %collective-permute-start.1 = (f32[136,128]{1,0:T(8,128)S(1)}, f32[136,128]{1,0:T(8,128)S(1)}, u32[]{:S(2)}, u32[]{:S(2)}) collective-permute-start(f32[136,128]{1,0:T(8,128)S(1)} %shard_map.104.mine_ref), channel_id=1, source_target_pairs={{0,16},{1,17},{2,18},{3,19},{4,20},{5,21},{6,22},{7,23},{8,24},{9,... | collective-permute-start | bytes 208904 | tf_op jit(solution)/shard_map/ppermute | solution.py:376
  43.3 2.0 %collective-permute-start.2 = (f32[8,136,128]{2,1,0:T(8,128)S(1)}, f32[8,136,128]{2,1,0:T(8,128)S(1)}, u32[]{:S(2)}, u32[]{:S(2)}) collective-permute-start(f32[8,136,128]{2,1,0:T(8,128)S(1)} %all_to_all.21.means_ref), channel_id=1, source_target_pairs={{0,1},{1,0},{2,3},{3,2},{4,5},{5,4},{6,7},{7,6},{8,9},{9,8},{10,11... | collective-permute-start | bytes 1671176 | tf_op jit(solution)/shard_map/ppermute | solution.py:373
  43.4 1.9 %copy-start.1 = (s32[2048,1]{0,1:T(1,128)S(1)}, s32[2048,1]{0,1:T(1,128)}, u32[]{:S(2)}) copy-start(s32[2048,1]{0,1:T(1,128)} %param.12) | copy-start | bytes 24580
  43.4 1.9 %copy-start.2 = (s32[2048]{0:T(1024)S(1)}, s32[2048]{0:T(1024)}, u32[]{:S(2)}) copy-start(s32[2048]{0:T(1024)} %param.13) | copy-start | bytes 24580
  47.9 2.2 %collective-permute-start.3 = (f32[8,40,128]{2,1,0:T(8,128)S(1)}, f32[8,40,128]{2,1,0:T(8,128)S(1)}, u32[]{:S(2)}, u32[]{:S(2)}) collective-permute-start(f32[8,40,128]{2,1,0:T(8,128)S(1)} %get-tuple-element.32), channel_id=1, source_target_pairs={{0,1},{1,0},{2,3},{3,2},{4,5},{5,4},{6,7},{7,6},{8,9},{9,8},{10,11... | collective-permute-start | bytes 491528 | tf_op jit(solution)/shard_map/ppermute | solution.py:373
  59.9 4.9 %collective-permute-start.4 = (f32[64,128]{1,0:T(8,128)S(1)}, f32[64,128]{1,0:T(8,128)S(1)}, u32[]{:S(2)}, u32[]{:S(2)}) collective-permute-start(f32[64,128]{1,0:T(8,128)S(1)} %shard_map.109.mine_ref), channel_id=1, source_target_pairs={{0,16},{1,17},{2,18},{3,19},{4,20},{5,21},{6,22},{7,23},{8,24},{9,... | collective-permute-start | bytes 98312 | tf_op jit(solution)/shard_map/ppermute | solution.py:376
  73.5 1.4 %collective-permute-start.5 = (f32[8,40,128]{2,1,0:T(8,128)S(1)}, f32[8,40,128]{2,1,0:T(8,128)S(1)}, u32[]{:S(2)}, u32[]{:S(2)}) collective-permute-start(f32[8,40,128]{2,1,0:T(8,128)S(1)} %all_to_all.23.own_ref), channel_id=1, source_target_pairs={{0,1},{1,0},{2,3},{3,2},{4,5},{5,4},{6,7},{7,6},{8,9},{9,8},{10,11... | collective-permute-start | bytes 491528 | tf_op jit(solution)/shard_map/ppermute | solution.py:373
  73.5 1.4 %collective-permute-start.6 = (f32[24,128]{1,0:T(8,128)S(1)}, f32[24,128]{1,0:T(8,128)S(1)}, u32[]{:S(2)}, u32[]{:S(2)}) collective-permute-start(f32[24,128]{1,0:T(8,128)S(1)} %get-tuple-element.35.mine_ref), channel_id=1, source_target_pairs={{0,1},{1,0},{2,3},{3,2},{4,5},{5,4},{6,7},{7,6},{8,9},{9,8},{10,11... | collective-permute-start | bytes 36872 | tf_op jit(solution)/shard_map/ppermute | solution.py:373

commit v3 on v2

--- a/solution.py
+++ b/solution.py
@@ -13,11 +13,16 @@
 PD_DEV = 16
 LANES = 128
 TILE = 8
-VMEM_LIMIT = 48 * 1024 * 1024
+AXIS = "rows"
+VMEM_LIMIT = 32 * 1024 * 1024
 
 BF16 = jnp.bfloat16
 F32 = jnp.float32
 I32 = jnp.int32
+
+
+def core_index():
+    return lax.rem(lax.axis_index(AXIS), 2)
 
 
 def iota(shape, dim):
@@ -117,8 +122,8 @@
 
 
 def firm_kernel(
-    blocks, width, base_ref, x_hbm, outcome_hbm, predictor_hbm, firm_hbm, dy_hbm,
-    x1_ref, z1_ref, pairs_ref, out_ref, x_ref, outcome_ref, predictor_ref, firm_ref, dy_ref, sems,
+    blocks, width, x_hbm, outcome_hbm, predictor_hbm, firm_hbm, dy_hbm,
+    x1_ref, z1_ref, weight_ref, dy_ref, pairs_ref, out_ref, x_ref, outcome_ref, predictor_ref, firm_ref, sems,
 ):
     small = [(firm_hbm, firm_ref), (predictor_hbm, predictor_ref), (outcome_hbm, outcome_ref), (dy_hbm, dy_ref)]
     copies = [pltpu.make_async_copy(src, dst, sems.at[i]) for i, (src, dst) in enumerate(small)]
@@ -134,6 +139,7 @@
         copy.wait()
     firm = firm_ref[...]
     weight, working = weights_of(predictor_ref[...], outcome_ref[...])
+    weight_ref[...] = weight
     weight_t = jnp.transpose(weight)
     firm_t = jnp.transpose(firm)
     masks = [iota((FIRM_DEV, LANES), 0) == firm[a : a + 1, :] for a in range(count)]
@@ -164,13 +170,12 @@
     z1 = jnp.concatenate(z1, axis=0)
     z1_ref[...] = z1
     dy = dy_ref[...]
-    scatter_half(dy, jnp.transpose(dy), weight, z1, pairs_ref, base_ref[0], blocks, width, out_ref)
-
-
-def sums_kernel(blocks, width, base_ref, pairs_ref, z1_ref, predictor_ref, dy_ref, out_ref):
+    scatter_half(dy, jnp.transpose(dy), weight, z1, pairs_ref, (1 - core_index()) * (blocks * width), blocks, width, out_ref)
+
+
+def sums_kernel(blocks, width, pairs_ref, z1_ref, weight_ref, dy_ref, out_ref):
     dy = dy_ref[...]
-    weight = jnp.exp(predictor_ref[...])
-    scatter_half(dy, jnp.transpose(dy), weight, z1_ref[...], pairs_ref, base_ref[0], blocks, width, out_ref)
+    scatter_half(dy, jnp.transpose(dy), weight_ref[...], z1_ref[...], pairs_ref, core_index() * (blocks * width), blocks, width, out_ref)
 
 
 def total_kernel(in_ref, out_ref):
@@ -197,10 +202,10 @@
         rest_ref[0][...] = total[height:, :]
 
 
-def gather_kernel(blocks, width, base_ref, x_ref, z_ref, means_ref, dy_ref, x_out, z_out):
+def gather_kernel(blocks, width, x_ref, z_ref, means_ref, dy_ref, x_out, z_out):
     dy = dy_ref[...]
     x_new, z_new = gather_half(
-        dy, jnp.transpose(dy), means_ref, base_ref[0], blocks, width, lambda a: x_ref[row_block(a), :], z_ref[...]
+        dy, jnp.transpose(dy), means_ref, core_index() * (blocks * width), blocks, width, lambda a: x_ref[row_block(a), :], z_ref[...]
     )
     for a, value in enumerate(x_new):
         x_out[row_block(a), :] = value
@@ -208,14 +213,14 @@
 
 
 def effect_kernel(
-    blocks, width, pd_width, base_ref, x_ref, z_ref, means_ref, dy_ref, predictor_ref, owner_ref, local_ref,
+    blocks, width, pd_width, x_ref, z_ref, means_ref, dy_ref, weight_ref, owner_ref, local_ref,
     x2_ref, z2_ref, weighted_ref, send_ref,
 ):
     dy = dy_ref[...]
-    weight = jnp.exp(predictor_ref[...])
+    weight = weight_ref[...]
     weight_t = jnp.transpose(weight)
     x_new, z2 = gather_half(
-        dy, jnp.transpose(dy), means_ref, base_ref[0], blocks, width, lambda a: x_ref[row_block(a), :], z_ref[...]
+        dy, jnp.transpose(dy), means_ref, (1 - core_index()) * (blocks * width), blocks, width, lambda a: x_ref[row_block(a), :], z_ref[...]
     )
     for a, value in enumerate(x_new):
         x2_ref[row_block(a), :] = value
@@ -223,20 +228,20 @@
     z2_ref[...] = z2
     effect = owner_ref[...] * PD_DEV + local_ref[...]
     scatter_half(
-        effect, jnp.transpose(effect), weight, z2, weighted_ref, base_ref[2], blocks, pd_width, send_ref
+        effect, jnp.transpose(effect), weight, z2, weighted_ref, (1 - core_index()) * (blocks * pd_width), blocks, pd_width, send_ref
     )
 
 
 def gram_kernel(
-    blocks, pd_width, share, base_ref, x2_ref, z2_ref, weighted_ref, predictor_ref, owner_ref, local_ref,
+    blocks, pd_width, share, x2_ref, z2_ref, weighted_ref, weight_ref, owner_ref, local_ref,
     keep_ref, gram_ref, plain_ref,
 ):
-    weight = jnp.exp(predictor_ref[...])
+    weight = weight_ref[...]
     z2 = z2_ref[...]
     lines = z2.shape[0]
     effect = owner_ref[...] * PD_DEV + local_ref[...]
     scatter_half(
-        effect, jnp.transpose(effect), weight, z2, weighted_ref, base_ref[1], blocks, pd_width, keep_ref
+        effect, jnp.transpose(effect), weight, z2, weighted_ref, core_index() * (blocks * pd_width), blocks, pd_width, keep_ref
     )
     for a in range(lines):
         plain_ref[row_block(a), :] = pair(x2_ref[row_block(a), :])
@@ -258,21 +263,46 @@
         gram_ref[j] = jnp.concatenate([low, high, rhs, spare], axis=0)
 
 
+def gram_less(means_ref, blocks, width, first):
+    mean_x = means_ref[:, :width, :]
+    diagonal = iota((blocks, width, LANES), 2) == iota((blocks, width, LANES), 1)
+    sum_w = jnp.sum(jnp.where(diagonal, means_ref[:, width, :][:, None, :], 0.0), axis=2, keepdims=True)
+    mean_z = jnp.sum(jnp.where(diagonal, means_ref[:, width + 1, :][:, None, :], 0.0), axis=2, keepdims=True)
+    sum_x = (sum_w * mean_x).reshape(blocks * width, LANES)
+    pick = jnp.where(iota((TILE, LANES), 1) == iota((TILE, LANES), 0) + first, 1.0, 0.0)
+    columns = lax.dot_general(
+        pick, sum_x, (((1,), (1,)), ((), ())), precision=lax.Precision.HIGHEST, preferred_element_type=F32
+    )
+    rhs = jnp.sum(sum_x * mean_z.reshape(blocks * width, 1), axis=0, keepdims=True)
+    return dot_exact(columns, mean_x.reshape(blocks * width, LANES)), rhs
+
+
+def own_kernel(
+    blocks, width, share, x_ref, z_ref, means_ref, owner_ref, local_ref, x_out, z_out, less_ref
+):
+    effect = owner_ref[...] * PD_DEV + local_ref[...]
+    x_new, z_new = gather_half(
+        effect, jnp.transpose(effect), means_ref, core_index() * (blocks * width), blocks, width, lambda a: x_ref[row_block(a), :],
+        z_ref[...],
+    )
+    for a, value in enumerate(x_new):
+        x_out[row_block(a), :] = value
+    z_out[...] = z_new
+    gram, rhs = gram_less(means_ref, blocks, width, lax.axis_index(AXIS) * share)
+    less_ref[...] = jnp.concatenate([gram, rhs, jnp.zeros((TILE - 1, LANES), F32)], axis=0)
+
+
 def last_kernel(
-    blocks, width, share, total_rows, base_ref, x_ref, z_ref, own_ref, other_ref, mine_ref, got_ref, owner_ref,
+    blocks, width, share, total_rows, x_ref, z_ref, means_ref, less_ref, mine_ref, got_ref, owner_ref,
     local_ref, x_hbm, z_out, gram_out, rhs_out, x_out, sems,
 ):
     effect = owner_ref[...] * PD_DEV + local_ref[...]
-    effect_t = jnp.transpose(effect)
     x_new, z_new = gather_half(
-        effect, effect_t, own_ref, base_ref[1], blocks, width, lambda a: x_ref[row_block(a), :], z_ref[...]
-    )
-    x_new, z_new = gather_half(
-        effect, effect_t, other_ref, base_ref[2], blocks, width, lambda a: x_new[a], z_new
+        effect, jnp.transpose(effect), means_ref, (1 - core_index()) * (blocks * width), blocks, width, lambda a: x_ref[row_block(a), :],
+        z_ref[...],
     )
     copies = []
-    count = len(x_new)
-    chunk = max(1, count // 4)
+    chunk = max(1, len(x_new) // 4)
     for a, value in enumerate(x_new):
         x_out[row_block(a), :] = value
         if a % chunk == chunk - 1:
@@ -280,39 +310,24 @@
             copies.append(pltpu.make_async_copy(x_out.at[span, :], x_hbm.at[span, :], sems.at[a // chunk]))
             copies[-1].start()
     z_out[...] = z_new
-    me, core, high = base_ref[4], base_ref[3], base_ref[5]
+    me = lax.axis_index(AXIS)
+    core, high = core_index(), lax.div(me, 2 * blocks)
     first = me * share
-    pick = jnp.where(iota((TILE, LANES), 1) == iota((TILE, LANES), 0) + first, 1.0, 0.0)
-    gram_less = jnp.zeros((TILE, LANES), F32)
-    rhs_less = jnp.zeros((1, LANES), F32)
-    for ref in (own_ref, other_ref):
-        mean_x = ref[:, :width, :]
-        diagonal = iota((blocks, width, LANES), 2) == iota((blocks, width, LANES), 1)
-        sum_w = jnp.sum(jnp.where(diagonal, ref[:, width, :][:, None, :], 0.0), axis=2, keepdims=True)
-        mean_z = jnp.sum(jnp.where(diagonal, ref[:, width + 1, :][:, None, :], 0.0), axis=2, keepdims=True)
-        sum_x = (sum_w * mean_x).reshape(blocks * width, LANES)
-        mean_x = mean_x.reshape(blocks * width, LANES)
-        mean_z = mean_z.reshape(blocks * width, 1)
-        columns = lax.dot_general(
-            pick, sum_x, (((1,), (1,)), ((), ())), precision=lax.Precision.HIGHEST, preferred_element_type=F32
-        )
-        gram_less += dot_exact(columns, mean_x)
-        rhs_less += jnp.sum(sum_x * mean_z, axis=0, keepdims=True)
+    gram_part, rhs_part = gram_less(means_ref, blocks, width, first)
     total = mine_ref[...] + got_ref[...]
     gram = jnp.zeros((share, LANES), F32)
     for place in range(4):
         here = (high == place // 2) & (core == place % 2)
         gram = jnp.where(here, total[place * share : (place + 1) * share, :], gram)
     scale = 1.0 / total_rows
-    gram_out[...] = (gram - gram_less[:share, :]) * scale
-    rhs = (total[4 * share : 4 * share + 1, :] - rhs_less) * scale
+    gram_out[...] = (gram - (gram_part[:share, :] + less_ref[:share, :])) * scale
+    rhs = (total[4 * share : 4 * share + 1, :] - (rhs_part + less_ref[TILE : TILE + 1, :])) * scale
     rhs_out[...] = pltpu.roll(rhs, LANES - first, 1)[:, :share]
     for copy in copies:
         copy.wait()
 
 
 VMEM = pl.BlockSpec(memory_space=pltpu.VMEM)
-SMEM = pl.BlockSpec(memory_space=pltpu.SMEM)
 HBM = pl.BlockSpec(memory_space=pltpu.HBM)
 
 
@@ -321,7 +336,7 @@
     return pl.pallas_call(
         kernel,
         out_shape=tuple(outs),
-        in_specs=in_specs or [SMEM if v.ndim == 1 else VMEM for v in args],
+        in_specs=in_specs or [VMEM] * len(args),
         out_specs=tuple(out_specs or [VMEM] * len(outs)),
         scratch_shapes=scratch,
         cost_estimate=pl.CostEstimate(flops=flops, bytes_accessed=size, transcendentals=0),
@@ -329,6 +344,10 @@
     )(*args)
 
 
+def in_hbm(v):
+    return pltpu.with_memory_space_constraint(v, pltpu.HBM)
+
+
 def shaped(*shape, dtype=F32):
     return jax.ShapeDtypeStruct(shape, dtype)
 
@@ -339,7 +358,7 @@
 
 def shards(covariates, outcome, predictor, firm_id, dy_id, pd_owner, pd_local):
     rows, width = covariates.shape
-    devices = lax.axis_size("rows")
+    devices = lax.axis_size(AXIS)
     blocks = devices // 4
     share = width // devices
     total_rows = rows * devices
@@ -347,9 +366,6 @@
     dy_high, pd_high = rounded(dy_width + 2), rounded(pd_width + 2)
     gram_high = rounded(4 * share + 1)
     lines = rows // LANES
-    me = lax.axis_index("rows")
-    core = lax.rem(me, 2)
-    high = lax.div(me, devices // 2)
     groups = [
         [half * (devices // 2) + core_of + 2 * chip for chip in range(blocks)]
         for half in range(2)
@@ -362,52 +378,46 @@
     )
     dy_half, pd_half = blocks * dy_width, blocks * pd_width
 
-    def table(*values):
-        return jnp.stack([jnp.asarray(v, I32) for v in values])
-
-    keep_base = table(core * dy_half)
-    send_base = table((1 - core) * dy_half)
-    pd_base = table((1 - core) * dy_half, core * pd_half, (1 - core) * pd_half, core, me, high)
-
     def to_core(v):
-        return lax.ppermute(v, "rows", partner)
+        return lax.ppermute(v, AXIS, partner)
 
     def to_half(v):
-        return lax.ppermute(v, "rows", opposite)
+        return lax.ppermute(v, AXIS, opposite)
 
     def across(v):
-        return lax.all_to_all(v, "rows", 0, 0, axis_index_groups=groups)
+        return lax.all_to_all(v, AXIS, 0, 0, axis_index_groups=groups)
 
     def total_of(v):
         return call(total_kernel, (shaped(*v.shape[1:]),), (v,))[0]
 
     wide = 4 * rows * LANES
     count = min(4, lines)
-    x1, z1, pairs, send = call(
+    x1, z1, weight, dy, pairs, send = call(
         functools.partial(firm_kernel, blocks, dy_width),
         (
             shaped(rows, width),
             shaped(lines, LANES),
+            shaped(lines, LANES),
+            shaped(lines, LANES, dtype=I32),
             shaped(rows, 2 * LANES, dtype=BF16),
             shaped(blocks, dy_high, LANES),
         ),
-        (send_base, covariates, outcome, predictor, firm, dy),
+        tuple(in_hbm(v) for v in (covariates, outcome, predictor, firm, dy)),
         scratch=(
             pltpu.VMEM((rows, width), F32),
             pltpu.VMEM((lines, LANES), F32),
             pltpu.VMEM((lines, LANES), F32),
             pltpu.VMEM((lines, LANES), I32),
-            pltpu.VMEM((lines, LANES), I32),
             pltpu.SemaphoreType.DMA((4 + count,)),
         ),
         flops=wide * (dy_half + 2 * FIRM_DEV),
-        in_specs=[SMEM] + [HBM] * 5,
+        in_specs=[HBM] * 5,
     )
     got = to_core(send)
     (keep,) = call(
         functools.partial(sums_kernel, blocks, dy_width),
         (shaped(blocks, dy_high, LANES),),
-        (keep_base, pairs, z1, predictor, dy),
+        (pairs, z1, weight, dy),
         flops=wide * dy_half,
     )
     mine = total_of(across(keep + got))
@@ -419,7 +429,7 @@
     x1, z1 = call(
         functools.partial(gather_kernel, blocks, dy_width),
         (shaped(rows, width), shaped(lines, LANES)),
-        (keep_base, x1, z1, means, dy),
+        (x1, z1, means, dy),
         flops=wide * dy_half,
     )
     x2, z2, pairs, send = call(
@@ -430,14 +440,14 @@
             shaped(rows, 2 * LANES, dtype=BF16),
             shaped(blocks, pd_high, LANES),
         ),
-        (pd_base, x1, z1, other, dy, predictor, owner, local),
+        (x1, z1, other, dy, weight, owner, local),
         flops=wide * (dy_half + pd_half),
     )
     got = to_core(send)
     keep, gram = call(
         functools.partial(gram_kernel, blocks, pd_width, share),
         (shaped(blocks, pd_high, LANES), shaped(blocks, gram_high, LANES)),
-        (pd_base, x2, z2, pairs, predictor, owner, local),
+        (x2, z2, pairs, weight, owner, local),
         scratch=(pltpu.VMEM((rows, 2 * LANES), BF16),),
         flops=wide * (pd_half + 2 * LANES),
     )
@@ -450,12 +460,18 @@
     got = to_core(gram)
     means = across(means)
     other = to_core(means)
+    x3, z3, less = call(
+        functools.partial(own_kernel, blocks, pd_width, share),
+        (shaped(rows, width), shaped(lines, LANES), shaped(2 * TILE, LANES)),
+        (x2, z2, means, owner, local),
+        flops=wide * pd_half,
+    )
     x3, z3, gram, rhs = call(
         functools.partial(last_kernel, blocks, pd_width, share, total_rows),
         (shaped(rows, width), shaped(lines, LANES), shaped(share, LANES), shaped(1, share)),
-        (pd_base, x2, z2, means, other, gram, got, owner, local),
+        (x3, z3, other, less, gram, got, owner, local),
         scratch=(pltpu.VMEM((rows, width), F32), pltpu.SemaphoreType.DMA((count,))),
-        flops=wide * 2 * pd_half,
+        flops=wide * pd_half,
         out_specs=[HBM, VMEM, VMEM, VMEM],
     )
     return x3, z3.reshape(rows), gram, rhs.reshape(share)

time: 78.5 us -> 73.3 us (0.934)
  local copies, waits for them, and re-layouts: 2.89 us -> 0.01 us
  other arithmetic: 1.18 us -> 0.11 us
    unnamed x16 -> x4, local copies, waits for them, and re-layouts: 2.81 us -> 0.01 us
    add x1, other arithmetic: 1.13 us -> 0.07 us  [shards(): mine = total_of(across(keep + got))]
    pallas_call x10 -> x11, Pallas kernels: 14 us -> 13.7 us  [call(): pl.pallas_call(kernel, out_shape=tuple(outs), in_specs=in_specs or [VMEM]...]
  transfers between devices with their start and end apart: 7 -> 7, of which waited for: 5 -> 4; matrix products, arithmetic and copies ran while one was open for 0% -> 0% of each run, Pallas kernels for 6% -> 7%
where the time goes in v3:
time: 73.3 us; the launch traced here: 73 us
  blocking collectives  45.6 us (62%)
  Pallas kernels  13.7 us (19%)
  starting transfers between devices  6.65 us (9%)
  waiting for transfers between devices  6.12 us (8%)
    all_to_all x4, blocking collectives, across(): return lax.all_to_all(v, AXIS, 0, 0, axis_index_groups=groups)  45.6 us
    pallas_call x11, Pallas kernels, call(): pl.pallas_call(kernel, out_shape=tuple(outs), in_specs=in_specs or [VMEM]...  13.7 us
    ppermute x2, waiting for transfers between devices, to_half(): return lax.ppermute(v, AXIS, opposite)  5.5 us
    ppermute x2, starting transfers between devices, to_half(): return lax.ppermute(v, AXIS, opposite)  5.41 us
  transfers between devices with their start and end apart: 7, of which 4 were waited for; matrix products, arithmetic and copies ran while one was open for 0% of the time, Pallas kernels for 7%

profile of v3, /device:TPU:0, one launch (start us, length us, event | category | flops | bytes accessed | tf_op | source)
XLA Modules:
  0.0 73.0 jit_solution(9661014460216850659)
XLA Ops:
  0.6 4.0 %shard_map.102 = (f32[2048,128]{1,0:T(8,128)S(1)}, f32[16,128]{1,0:T(8,128)S(1)}, f32[16,128]{1,0:T(8,128)S(1)}, s32[16,128]{1,0:T(8,128)S(1)}, bf16[2048,256]{1...) custom-call(f32[2048,128]{1,0:T(8,128)} %x_hbm.1, f32[16,128]{1,0:T(8,128)} %bitcast.16, f32[16,128]{1,0:T(8,128)} %bitcast.17, ...), custom_call_target="tpu_custom_call" | custom-call | flops 1342177280 | bytes 3760128 | tf_op jit(solution)/shard_map/pallas_call | solution.py:336
  4.6 0.5 collective-permute-start
  5.1 1.3 %shard_map.103 = f32[8,136,128]{2,1,0:T(8,128)S(1)} custom-call(bf16[2048,256]{1,0:T(8,128)(2,1)S(1)} %get-tuple-element.29.pairs_ref, f32[16,128]{1,0:T(8,128)S(1)} %get-tuple-element.28.z1_ref.z_ref, f32[16,128]{1,0:T(8,128)S(1)} %get-tuple-element.30.weight_ref, s32[16,128]{1,0:T(8,128)S(1)} %get-tuple-element.31.dy_ref), custom_call_target="tpu_custom_call" | custom-call | flops 1073741824 | bytes 1630208 | tf_op jit(solution)/shard_map/pallas_call | solution.py:336
  6.5 0.2 collective-permute-done
  6.7 0.1 add.6
  6.8 16.3 %all_to_all.20.in_ref = f32[8,136,128]{2,1,0:T(8,128)S(1)} all-to-all(f32[8,136,128]{2,1,0:T(8,128)S(1)} %add.6), channel_id=1, replica_groups={{0,2,4,6,8,10,12,14},{1,3,5,7,9,11,13,15},{16,18,20,22,24,26,28,30},{17..., dimensions={0} | all-to-all | bytes 1114112 | tf_op jit(solution)/shard_map/all_to_all | solution.py:388
  23.1 2.7 %collective-permute-start.1 = (f32[136,128]{1,0:T(8,128)S(1)}, f32[136,128]{1,0:T(8,128)S(1)}, u32[]{:S(2)}, u32[]{:S(2)}) collective-permute-start(f32[136,128]{1,0:T(8,128)S(1)} %shard_map.104.mine_ref), channel_id=1, source_target_pairs={{0,16},{1,17},{2,18},{3,19},{4,20},{5,21},{6,22},{7,23},{8,24},{9,... | collective-permute-start | bytes 208904 | tf_op jit(solution)/shard_map/ppermute | solution.py:385
  25.7 3.4 %collective-permute-done.1.got_ref = f32[136,128]{1,0:T(8,128)S(1)} collective-permute-done((f32[136,128]{1,0:T(8,128)S(1)}, f32[136,128]{1,0:T(8,128)S(1)}, u32[]{:S(2)}, u32[]{:S(2)}) %collective-permute-start.1) | collective-permute-done | bytes 69664 | tf_op jit(solution)/shard_map/ppermute | solution.py:385
  29.1 0.1 shard_map.105
  29.2 10.9 %all_to_all.21.means_ref = f32[8,136,128]{2,1,0:T(8,128)S(1)} all-to-all(f32[8,136,128]{2,1,0:T(8,128)S(1)} %shard_map.105), channel_id=1, replica_groups={{0,2,4,6,8,10,12,14},{1,3,5,7,9,11,13,15},{16,18,20,22,24,26,28,30},{17..., dimensions={0} | all-to-all | bytes 1114112 | tf_op jit(solution)/shard_map/all_to_all | solution.py:388
  40.1 0.0 collective-permute-start.2
  40.1 0.0 copy-start
  40.1 0.0 copy-start.1
  40.1 1.6 %shard_map.106 = (f32[2048,128]{1,0:T(8,128)S(1)}, f32[16,128]{1,0:T(8,128)S(1)}) custom-call(f32[2048,128]{1,0:T(8,128)S(1)} %get-tuple-element.27.x_ref, f32[16,128]{1,0:T(8,128)S(1)} %get-tuple-element.28.z1_ref.z_ref, f32[8,136,128]{2,1,0:T(8,128)S(1)} %all_to_all.21.means_ref, s32[16,128]{1,0:T(8,128)S(1)} %get-tuple-element.31.dy_ref), custom_call_target="tpu_custom_call" | custom-call | flops 1073741824 | bytes 2678784 | tf_op jit(solution)/shard_map/pallas_call | solution.py:336
  41.7 0.4 collective-permute-done.2.means_ref
  42.1 0.0 copy-done
  42.1 0.0 copy-done.1
  42.1 2.0 %shard_map.107 = (f32[2048,128]{1,0:T(8,128)S(1)}, f32[16,128]{1,0:T(8,128)S(1)}, bf16[2048,256]{1,0:T(8,128)(2,1)S(1)}, f32[8,40,128]{2,1,0:T(8,128)S(1)}) custom-call(f32[2048,128]{1,0:T(8,128)S(1)} %get-tuple-element.33.x_ref, f32[16,128]{1,0:T(8,128)S(1)} %get-tuple-element.34.z_ref, f32[8,136,128]{2,1,0:T(8,128)S(1)} %collective-permute-done.2.means_ref, ...), custom_call_target="tpu_custom_call" | custom-call | flops 1342177280 | bytes 3915776 | tf_op jit(solution)/shard_map/pallas_call | solution.py:336
  44.1 0.2 collective-permute-start.3
  44.4 1.3 %shard_map.108 = (f32[8,40,128]{2,1,0:T(8,128)S(1)}, f32[8,24,128]{2,1,0:T(8,128)S(1)}) custom-call(f32[2048,128]{1,0:T(8,128)S(1)} %get-tuple-element.35.x2_ref.x_ref, f32[16,128]{1,0:T(8,128)S(1)} %get-tuple-element.36.z2_ref.z_ref, bf16[2048,256]{1,0:T(8,128)(2,1)S(1)} %get-tuple-element.37.weighted_ref, f32[16,128]{1,0:T(8,128)S(1)} %get-tuple-element.30.weight_ref, ...), custom_call_target="tpu_custom_call" | custom-call | flops 536870912 | bytes 2392064 | tf_op jit(solution)/shard_map/pallas_call | solution.py:336
  45.7 0.0 collective-permute-done.3
  45.7 9.8 %all_to_all.22.in_ref = f32[8,64,128]{2,1,0:T(8,128)S(1)} all-to-all(f32[8,64,128]{2,1,0:T(8,128)S(1)} %pad_maximum_fusion), channel_id=1, replica_groups={{0,2,4,6,8,10,12,14},{1,3,5,7,9,11,13,15},{16,18,20,22,24,26,28,30},{17..., dimensions={0} | all-to-all | bytes 524288 | tf_op jit(solution)/shard_map/all_to_all | solution.py:388
  55.6 2.8 %collective-permute-start.4 = (f32[64,128]{1,0:T(8,128)S(1)}, f32[64,128]{1,0:T(8,128)S(1)}, u32[]{:S(2)}, u32[]{:S(2)}) collective-permute-start(f32[64,128]{1,0:T(8,128)S(1)} %shard_map.109.mine_ref), channel_id=1, source_target_pairs={{0,16},{1,17},{2,18},{3,19},{4,20},{5,21},{6,22},{7,23},{8,24},{9,... | collective-permute-start | bytes 98312 | tf_op jit(solution)/shard_map/ppermute | solution.py:385
  58.4 2.1 %collective-permute-done.4.got_ref = f32[64,128]{1,0:T(8,128)S(1)} collective-permute-done((f32[64,128]{1,0:T(8,128)S(1)}, f32[64,128]{1,0:T(8,128)S(1)}, u32[]{:S(2)}, u32[]{:S(2)}) %collective-permute-start.4) | collective-permute-done | bytes 32800 | tf_op jit(solution)/shard_map/ppermute | solution.py:385
  60.5 0.1 shard_map.110
  60.6 8.6 %all_to_all.23.means_ref = f32[8,40,128]{2,1,0:T(8,128)S(1)} all-to-all(f32[8,40,128]{2,1,0:T(8,128)S(1)} %get-tuple-element.41), channel_id=1, replica_groups={{0,2,4,6,8,10,12,14},{1,3,5,7,9,11,13,15},{16,18,20,22,24,26,28,30},{17..., dimensions={0} | all-to-all | bytes 327680 | tf_op jit(solution)/shard_map/all_to_all | solution.py:388
  69.2 0.0 collective-permute-start.5
  69.2 0.5 collective-permute-start.6
  69.7 1.0 %shard_map.111 = (f32[2048,128]{1,0:T(8,128)S(1)}, f32[16,128]{1,0:T(8,128)S(1)}, f32[16,128]{1,0:T(8,128)S(1)}) custom-call(f32[2048,128]{1,0:T(8,128)S(1)} %get-tuple-element.35.x2_ref.x_ref, f32[16,128]{1,0:T(8,128)S(1)} %get-tuple-element.36.z2_ref.z_ref, f32[8,40,128]{2,1,0:T(8,128)S(1)} %all_to_all.23.means_ref, s32[16,128]{1,0:T(8,128)S(1)} %bitcast.10, ...), custom_call_target="tpu_custom_call" | custom-call | flops 268435456 | bytes 2301952 | tf_op jit(solution)/shard_map/pallas_call | solution.py:336
  70.7 0.0 collective-permute-done.6.got_ref
  70.7 0.0 collective-permute-done.5.means_ref
  70.7 2.3 %shard_map.112 = (f32[2048,128]{1,0:T(8,128)}, f32[16,128]{1,0:T(8,128)}, f32[4,128]{1,0:T(4,128)}, f32[1,4]{1,0:T(1,128)}) custom-call(f32[2048,128]{1,0:T(8,128)S(1)} %get-tuple-element.42.x_ref, f32[16,128]{1,0:T(8,128)S(1)} %get-tuple-element.43.z_ref, f32[8,40,128]{2,1,0:T(8,128)S(1)} %collective-permute-done.5.means_ref, ...), custom_call_target="tpu_custom_call" | custom-call | flops 268435456 | bytes 2328592 | tf_op jit(solution)/shard_map/pallas_call | solution.py:336
  (4 shorter events, 0.1 us)
Async XLA Ops:
  4.6 2.1 %collective-permute-start = (f32[8,136,128]{2,1,0:T(8,128)S(1)}, f32[8,136,128]{2,1,0:T(8,128)S(1)}, u32[]{:S(2)}, u32[]{:S(2)}) collective-permute-start(f32[8,136,128]{2,1,0:T(8,128)S(1)} %get-tuple-element.32), channel_id=1, source_target_pairs={{0,1},{1,0},{2,3},{3,2},{4,5},{5,4},{6,7},{7,6},{8,9},{9,8},{10,11... | collective-permute-start | bytes 1671176 | tf_op jit(solution)/shard_map/ppermute | solution.py:382
  23.1 6.0 %collective-permute-start.1 = (f32[136,128]{1,0:T(8,128)S(1)}, f32[136,128]{1,0:T(8,128)S(1)}, u32[]{:S(2)}, u32[]{:S(2)}) collective-permute-start(f32[136,128]{1,0:T(8,128)S(1)} %shard_map.104.mine_ref), channel_id=1, source_target_pairs={{0,16},{1,17},{2,18},{3,19},{4,20},{5,21},{6,22},{7,23},{8,24},{9,... | collective-permute-start | bytes 208904 | tf_op jit(solution)/shard_map/ppermute | solution.py:385
  40.1 2.0 %collective-permute-start.2 = (f32[8,136,128]{2,1,0:T(8,128)S(1)}, f32[8,136,128]{2,1,0:T(8,128)S(1)}, u32[]{:S(2)}, u32[]{:S(2)}) collective-permute-start(f32[8,136,128]{2,1,0:T(8,128)S(1)} %all_to_all.21.means_ref), channel_id=1, source_target_pairs={{0,1},{1,0},{2,3},{3,2},{4,5},{5,4},{6,7},{7,6},{8,9},{9,8},{10,11... | collective-permute-start | bytes 1671176 | tf_op jit(solution)/shard_map/ppermute | solution.py:382
  40.1 2.0 %copy-start = (s32[2048,1]{0,1:T(1,128)S(1)}, s32[2048,1]{0,1:T(1,128)}, u32[]{:S(2)}) copy-start(s32[2048,1]{0,1:T(1,128)} %param.12) | copy-start | bytes 24580
  40.1 2.0 %copy-start.1 = (s32[2048]{0:T(1024)S(1)}, s32[2048]{0:T(1024)}, u32[]{:S(2)}) copy-start(s32[2048]{0:T(1024)} %param.13) | copy-start | bytes 24580
  44.1 1.5 %collective-permute-start.3 = (f32[8,40,128]{2,1,0:T(8,128)S(1)}, f32[8,40,128]{2,1,0:T(8,128)S(1)}, u32[]{:S(2)}, u32[]{:S(2)}) collective-permute-start(f32[8,40,128]{2,1,0:T(8,128)S(1)} %get-tuple-element.39), channel_id=1, source_target_pairs={{0,1},{1,0},{2,3},{3,2},{4,5},{5,4},{6,7},{7,6},{8,9},{9,8},{10,11... | collective-permute-start | bytes 491528 | tf_op jit(solution)/shard_map/ppermute | solution.py:382
  55.6 4.9 %collective-permute-start.4 = (f32[64,128]{1,0:T(8,128)S(1)}, f32[64,128]{1,0:T(8,128)S(1)}, u32[]{:S(2)}, u32[]{:S(2)}) collective-permute-start(f32[64,128]{1,0:T(8,128)S(1)} %shard_map.109.mine_ref), channel_id=1, source_target_pairs={{0,16},{1,17},{2,18},{3,19},{4,20},{5,21},{6,22},{7,23},{8,24},{9,... | collective-permute-start | bytes 98312 | tf_op jit(solution)/shard_map/ppermute | solution.py:385
  69.2 1.5 %collective-permute-start.5 = (f32[8,40,128]{2,1,0:T(8,128)S(1)}, f32[8,40,128]{2,1,0:T(8,128)S(1)}, u32[]{:S(2)}, u32[]{:S(2)}) collective-permute-start(f32[8,40,128]{2,1,0:T(8,128)S(1)} %all_to_all.23.means_ref), channel_id=1, source_target_pairs={{0,1},{1,0},{2,3},{3,2},{4,5},{5,4},{6,7},{7,6},{8,9},{9,8},{10,11... | collective-permute-start | bytes 491528 | tf_op jit(solution)/shard_map/ppermute | solution.py:382
  69.2 1.5 %collective-permute-start.6 = (f32[24,128]{1,0:T(8,128)S(1)}, f32[24,128]{1,0:T(8,128)S(1)}, u32[]{:S(2)}, u32[]{:S(2)}) collective-permute-start(f32[24,128]{1,0:T(8,128)S(1)} %get-tuple-element.45.mine_ref), channel_id=1, source_target_pairs={{0,1},{1,0},{2,3},{3,2},{4,5},{5,4},{6,7},{7,6},{8,9},{9,8},{10,11... | collective-permute-start | bytes 36872 | tf_op jit(solution)/shard_map/ppermute | solution.py:382

commit v4 on v3

--- a/solution.py
+++ b/solution.py
@@ -33,8 +33,8 @@
     return jnp.dot(a, b, preferred_element_type=F32)
 
 
-def dot_exact(a, b):
-    return jnp.dot(a, b, precision=lax.Precision.HIGHEST, preferred_element_type=F32)
+def dot_first(a, b):
+    return lax.dot_general(a, b, (((0,), (0,)), ((), ())), preferred_element_type=F32)
 
 
 def onehot(mask):
@@ -67,7 +67,7 @@
     return weight, predictor + outcome / weight - 1.0
 
 
-def scatter_half(ids, ids_t, weight, working, pairs_ref, base, blocks, width, out_ref):
+def scatter_half(ids, weight, working, pairs_ref, base, blocks, width, out_ref, group=16):
     lines = ids.shape[0]
     count = blocks * width
     step = math.gcd(count, 256)
@@ -79,46 +79,49 @@
             step // width, width, LANES
         )
     block = lax.div(ids, I32(width))
-    place = lax.rem(ids_t, I32(width))
+    place = lax.rem(ids, I32(width))
     labels = iota((blocks, LANES), 0) + lax.div(base, I32(width))
     parts = [part.astype(F32) for part in pieces(weight, 3) + pieces(weight * working, 3)]
-    left = []
-    for a in range(lines):
-        mask = labels == block[a : a + 1, :]
-        left.append(jnp.concatenate([jnp.where(mask, part[a : a + 1, :], 0.0) for part in parts], axis=0))
-    left = jnp.concatenate(left, axis=1).astype(BF16)
-    right = jnp.concatenate(
-        [onehot(iota((LANES, LANES), 1) == place[:, a : a + 1]) for a in range(lines)], axis=0
-    )
-    sums = dot(left, right)
+    sums = jnp.zeros((6 * blocks, width), F32)
+    for a in range(0, lines, group):
+        left, right = [], []
+        for b in range(a, min(a + group, lines)):
+            mask = labels == block[b : b + 1, :]
+            left.append(jnp.concatenate([jnp.where(mask, part[b : b + 1, :], 0.0) for part in parts], axis=0))
+            right.append(onehot(iota((width, LANES), 0) == place[b : b + 1, :]))
+        left = jnp.concatenate(left, axis=1).astype(BF16)
+        right = jnp.concatenate(right, axis=1)
+        sums += lax.dot_general(left, right, (((1,), (1,)), ((), ())), preferred_element_type=F32)
     sums = [sums[i * blocks : (i + 1) * blocks, :] for i in range(6)]
-    out_ref[:, width, :] = sums[0] + sums[1] + sums[2]
-    out_ref[:, width + 1, :] = sums[3] + sums[4] + sums[5]
+    out_ref[:, width, :width] = sums[0] + sums[1] + sums[2]
+    out_ref[:, width + 1, :width] = sums[3] + sums[4] + sums[5]
     spare = out_ref.shape[1] - width - 2
     if spare:
         out_ref[:, width + 2 :, :] = jnp.zeros((blocks, spare, LANES), F32)
 
 
-def gather_half(ids, ids_t, means_ref, base, blocks, width, x_of, z):
+def gather_half(ids, means_ref, base, blocks, width, z, emit):
     lines = ids.shape[0]
     count = blocks * width
-    table = pair(means_ref[:, :width, :].reshape(count, LANES))
-    x_new = []
-    for a in range(lines):
-        labels = iota((LANES, count), 1) + base
-        picked = unpair(dot(onehot(labels == ids_t[:, a : a + 1]), table))
-        x_new.append(x_of(a) - picked)
+    group = math.gcd(lines, 4)
     parts = jnp.concatenate([part.astype(F32) for part in pieces(means_ref[:, width + 1, :], 3)], axis=0)
     left = jnp.transpose(parts)[:width, :].astype(BF16)
     block = lax.div(ids, I32(width)) - lax.div(base, I32(width))
     place = lax.rem(ids, I32(width))
+    table = pair(means_ref[:, :width, :].reshape(count, LANES))
+    labels = iota((count, LANES), 0) + base
     z_new = []
-    for a in range(lines):
-        mask = onehot(iota((blocks, LANES), 0) == block[a : a + 1, :])
-        candidates = dot(left, jnp.concatenate([mask, mask, mask], axis=0))
-        chosen = jnp.where(iota((width, LANES), 0) == place[a : a + 1, :], candidates, 0.0)
-        z_new.append(z[a : a + 1, :] - jnp.sum(chosen, axis=0, keepdims=True))
-    return x_new, jnp.concatenate(z_new, axis=0)
+    for a in range(0, lines, group):
+        for b in range(a, a + group):
+            mask = onehot(iota((blocks, LANES), 0) == block[b : b + 1, :])
+            candidates = dot(left, jnp.concatenate([mask, mask, mask], axis=0))
+            chosen = jnp.where(iota((width, LANES), 0) == place[b : b + 1, :], candidates, 0.0)
+            z_new.append(z[b : b + 1, :] - jnp.sum(chosen, axis=0, keepdims=True))
+        mask = jnp.concatenate([onehot(labels == ids[b : b + 1, :]) for b in range(a, a + group)], axis=1)
+        picked = unpair(dot_first(mask, table))
+        for b in range(group):
+            emit(a + b, picked[row_block(b), :])
+    return jnp.concatenate(z_new, axis=0)
 
 
 def firm_kernel(
@@ -141,7 +144,7 @@
     weight, working = weights_of(predictor_ref[...], outcome_ref[...])
     weight_ref[...] = weight
     weight_t = jnp.transpose(weight)
-    firm_t = jnp.transpose(firm)
+    group = math.gcd(count, 4)
     masks = [iota((FIRM_DEV, LANES), 0) == firm[a : a + 1, :] for a in range(count)]
     spread_w = jnp.zeros((FIRM_DEV, LANES), F32)
     spread_z = jnp.zeros((FIRM_DEV, LANES), F32)
@@ -154,28 +157,32 @@
     denominator = jnp.where(sum_w > 0.0, sum_w, 1.0)
     mean_z = sum_z / denominator
     table = jnp.concatenate([onehot(mask) for mask in masks], axis=1)
+    sum_x = jnp.zeros((FIRM_DEV, 2 * LANES), F32)
     for i, a in enumerate(starts):
         copies[len(small) + i].wait()
+        span = slice(a * LANES, (a + chunk) * LANES)
         for b in range(a, a + chunk):
             pairs_ref[row_block(b), :] = pair(x_ref[row_block(b), :] * weight_t[:, b : b + 1])
-    mean_x = pair(unpair(dot(table, pairs_ref[...])) / denominator)
+        sum_x += dot(table[:, span], pairs_ref[span, :])
+    mean_x = pair(unpair(sum_x) / denominator)
     z1 = []
     for a in range(count):
-        selector = onehot(iota((LANES, FIRM_DEV), 1) == firm_t[:, a : a + 1])
-        x1 = x_ref[row_block(a), :] - unpair(dot(selector, mean_x))
+        if a % group == 0:
+            picked = unpair(dot_first(table[:, a * LANES : (a + group) * LANES], mean_x))
+        x1 = x_ref[row_block(a), :] - picked[row_block(a % group), :]
         x1_ref[row_block(a), :] = x1
         pairs_ref[row_block(a), :] = pair(x1 * weight_t[:, a : a + 1])
-        picked = jnp.sum(jnp.where(masks[a], mean_z, 0.0), axis=0, keepdims=True)
-        z1.append(working[a : a + 1, :] - picked)
+        picked_z = jnp.sum(jnp.where(masks[a], mean_z, 0.0), axis=0, keepdims=True)
+        z1.append(working[a : a + 1, :] - picked_z)
     z1 = jnp.concatenate(z1, axis=0)
     z1_ref[...] = z1
     dy = dy_ref[...]
-    scatter_half(dy, jnp.transpose(dy), weight, z1, pairs_ref, (1 - core_index()) * (blocks * width), blocks, width, out_ref)
+    scatter_half(dy, weight, z1, pairs_ref, (1 - core_index()) * (blocks * width), blocks, width, out_ref)
 
 
 def sums_kernel(blocks, width, pairs_ref, z1_ref, weight_ref, dy_ref, out_ref):
     dy = dy_ref[...]
-    scatter_half(dy, jnp.transpose(dy), weight_ref[...], z1_ref[...], pairs_ref, core_index() * (blocks * width), blocks, width, out_ref)
+    scatter_half(dy, weight_ref[...], z1_ref[...], pairs_ref, core_index() * (blocks * width), blocks, width, out_ref)
 
 
 def total_kernel(in_ref, out_ref):
@@ -199,17 +206,17 @@
     for j in range(out_ref.shape[0]):
         out_ref[j] = result
     if rest_ref:
-        rest_ref[0][...] = total[height:, :]
+        gram = total[height:, :]
+        rest_ref[0][: gram.shape[0], :] = gram
+        rest_ref[0][gram.shape[0] :, :] = total[width + 2 : width + 2 + TILE, :]
 
 
 def gather_kernel(blocks, width, x_ref, z_ref, means_ref, dy_ref, x_out, z_out):
-    dy = dy_ref[...]
-    x_new, z_new = gather_half(
-        dy, jnp.transpose(dy), means_ref, core_index() * (blocks * width), blocks, width, lambda a: x_ref[row_block(a), :], z_ref[...]
-    )
-    for a, value in enumerate(x_new):
-        x_out[row_block(a), :] = value
-    z_out[...] = z_new
+    def emit(a, picked):
+        x_out[row_block(a), :] = x_ref[row_block(a), :] - picked
+
+    base = core_index() * (blocks * width)
+    z_out[...] = gather_half(dy_ref[...], means_ref, base, blocks, width, z_ref[...], emit)
 
 
 def effect_kernel(
@@ -219,16 +226,17 @@
     dy = dy_ref[...]
     weight = weight_ref[...]
     weight_t = jnp.transpose(weight)
-    x_new, z2 = gather_half(
-        dy, jnp.transpose(dy), means_ref, (1 - core_index()) * (blocks * width), blocks, width, lambda a: x_ref[row_block(a), :], z_ref[...]
-    )
-    for a, value in enumerate(x_new):
-        x2_ref[row_block(a), :] = value
-        weighted_ref[row_block(a), :] = pair(value * weight_t[:, a : a + 1])
+
+    def emit(a, picked):
+        x2 = x_ref[row_block(a), :] - picked
+        x2_ref[row_block(a), :] = x2
+        weighted_ref[row_block(a), :] = pair(x2 * weight_t[:, a : a + 1])
+
+    z2 = gather_half(dy, means_ref, (1 - core_index()) * (blocks * width), blocks, width, z_ref[...], emit)
     z2_ref[...] = z2
     effect = owner_ref[...] * PD_DEV + local_ref[...]
     scatter_half(
-        effect, jnp.transpose(effect), weight, z2, weighted_ref, (1 - core_index()) * (blocks * pd_width), blocks, pd_width, send_ref
+        effect, weight, z2, weighted_ref, (1 - core_index()) * (blocks * pd_width), blocks, pd_width, send_ref
     )
 
 
@@ -241,13 +249,11 @@
     lines = z2.shape[0]
     effect = owner_ref[...] * PD_DEV + local_ref[...]
     scatter_half(
-        effect, jnp.transpose(effect), weight, z2, weighted_ref, core_index() * (blocks * pd_width), blocks, pd_width, keep_ref
+        effect, weight, z2, weighted_ref, core_index() * (blocks * pd_width), blocks, pd_width, keep_ref
     )
     for a in range(lines):
         plain_ref[row_block(a), :] = pair(x2_ref[row_block(a), :])
-    gram = lax.dot_general(
-        weighted_ref[...], plain_ref[...], (((0,), (0,)), ((), ())), preferred_element_type=F32
-    )
+    gram = dot_first(weighted_ref[...], plain_ref[...])
     gram = unpair(gram[:LANES, :] + gram[LANES:, :])
     left = [part.astype(F32) for part in pieces(weight * z2, 3)]
     none = jnp.zeros((TILE - 3, LANES), F32)
@@ -255,74 +261,77 @@
         [jnp.concatenate([part[a : a + 1, :] for part in left] + [none], axis=0) for a in range(lines)], axis=1
     )
     rhs = unpair(jnp.sum(dot(left.astype(BF16), plain_ref[...]), axis=0, keepdims=True))
-    spare = jnp.zeros((gram_ref.shape[1] - 4 * share - 1, LANES), F32)
+    keep_ref[:, pd_width + 2, :] = jnp.broadcast_to(rhs, (blocks, LANES))
     half = blocks * 2 * share
     for j in range(blocks):
         low = gram[2 * j * share : 2 * (j + 1) * share, :]
         high = gram[half + 2 * j * share : half + 2 * (j + 1) * share, :]
-        gram_ref[j] = jnp.concatenate([low, high, rhs, spare], axis=0)
-
-
-def gram_less(means_ref, blocks, width, first):
-    mean_x = means_ref[:, :width, :]
+        gram_ref[j, : 4 * share, :] = jnp.concatenate([low, high], axis=0)
+
+
+def gram_less(means_ref, blocks, width, first, share):
+    count = blocks * width
     diagonal = iota((blocks, width, LANES), 2) == iota((blocks, width, LANES), 1)
     sum_w = jnp.sum(jnp.where(diagonal, means_ref[:, width, :][:, None, :], 0.0), axis=2, keepdims=True)
     mean_z = jnp.sum(jnp.where(diagonal, means_ref[:, width + 1, :][:, None, :], 0.0), axis=2, keepdims=True)
-    sum_x = (sum_w * mean_x).reshape(blocks * width, LANES)
-    pick = jnp.where(iota((TILE, LANES), 1) == iota((TILE, LANES), 0) + first, 1.0, 0.0)
-    columns = lax.dot_general(
-        pick, sum_x, (((1,), (1,)), ((), ())), precision=lax.Precision.HIGHEST, preferred_element_type=F32
-    )
-    rhs = jnp.sum(sum_x * mean_z.reshape(blocks * width, 1), axis=0, keepdims=True)
-    return dot_exact(columns, mean_x.reshape(blocks * width, LANES)), rhs
-
-
-def own_kernel(
-    blocks, width, share, x_ref, z_ref, means_ref, owner_ref, local_ref, x_out, z_out, less_ref
+    mean_x = means_ref[:, :width, :].reshape(count, LANES)
+    sum_x = mean_x * sum_w.reshape(count, 1)
+    lane = iota((count, LANES), 1)
+    rows = []
+    for i in range(share):
+        column = jnp.sum(jnp.where(lane == first + i, sum_x, 0.0), axis=1, keepdims=True)
+        rows.append(jnp.sum(column * mean_x, axis=0, keepdims=True))
+    rows.append(jnp.sum(sum_x * mean_z.reshape(count, 1), axis=0, keepdims=True))
+    return jnp.concatenate(rows, axis=0)
+
+
+def own_kernel(blocks, width, share, x_ref, z_ref, means_ref, owner_ref, local_ref, x_out, z_out, less_ref):
+    effect = owner_ref[...] * PD_DEV + local_ref[...]
+
+    def emit(a, picked):
+        x_out[row_block(a), :] = x_ref[row_block(a), :] - picked
+
+    z_out[...] = gather_half(effect, means_ref, core_index() * (blocks * width), blocks, width, z_ref[...], emit)
+    less_ref[: share + 1, :] = gram_less(means_ref, blocks, width, lax.axis_index(AXIS) * share, share)
+
+
+def last_kernel(
+    blocks, width, share, total_rows, x_ref, z_ref, means_ref, less_ref, mine_ref, got_ref, owner_ref, local_ref,
+    x_hbm, z_hbm, gram_hbm, rhs_hbm, x_out, z_out, gram_out, rhs_out, sems,
 ):
-    effect = owner_ref[...] * PD_DEV + local_ref[...]
-    x_new, z_new = gather_half(
-        effect, jnp.transpose(effect), means_ref, core_index() * (blocks * width), blocks, width, lambda a: x_ref[row_block(a), :],
-        z_ref[...],
-    )
-    for a, value in enumerate(x_new):
-        x_out[row_block(a), :] = value
-    z_out[...] = z_new
-    gram, rhs = gram_less(means_ref, blocks, width, lax.axis_index(AXIS) * share)
-    less_ref[...] = jnp.concatenate([gram, rhs, jnp.zeros((TILE - 1, LANES), F32)], axis=0)
-
-
-def last_kernel(
-    blocks, width, share, total_rows, x_ref, z_ref, means_ref, less_ref, mine_ref, got_ref, owner_ref,
-    local_ref, x_hbm, z_out, gram_out, rhs_out, x_out, sems,
-):
-    effect = owner_ref[...] * PD_DEV + local_ref[...]
-    x_new, z_new = gather_half(
-        effect, jnp.transpose(effect), means_ref, (1 - core_index()) * (blocks * width), blocks, width, lambda a: x_ref[row_block(a), :],
-        z_ref[...],
-    )
-    copies = []
-    chunk = max(1, len(x_new) // 4)
-    for a, value in enumerate(x_new):
-        x_out[row_block(a), :] = value
-        if a % chunk == chunk - 1:
-            span = slice((a + 1 - chunk) * LANES, (a + 1) * LANES)
-            copies.append(pltpu.make_async_copy(x_out.at[span, :], x_hbm.at[span, :], sems.at[a // chunk]))
-            copies[-1].start()
-    z_out[...] = z_new
     me = lax.axis_index(AXIS)
     core, high = core_index(), lax.div(me, 2 * blocks)
     first = me * share
-    gram_part, rhs_part = gram_less(means_ref, blocks, width, first)
+    copies = []
+    effect = owner_ref[...] * PD_DEV + local_ref[...]
+    lines = effect.shape[0]
+    chunk = max(1, lines // 4)
+
+    def emit(a, picked):
+        x_out[row_block(a), :] = x_ref[row_block(a), :] - picked
+        if a % chunk == chunk - 1:
+            span = slice((a + 1 - chunk) * LANES, (a + 1) * LANES)
+            copies.append(pltpu.make_async_copy(x_out.at[span, :], x_hbm.at[span, :], sems.at[3 + a // chunk]))
+            copies[-1].start()
+
+    z_out[...] = gather_half(effect, means_ref, (1 - core) * (blocks * width), blocks, width, z_ref[...], emit)
+    copies.append(pltpu.make_async_copy(z_out, z_hbm, sems.at[2]))
+    copies[-1].start()
+    less = gram_less(means_ref, blocks, width, first, share) + less_ref[: share + 1, :]
     total = mine_ref[...] + got_ref[...]
+    high_rows = total.shape[0] - TILE
     gram = jnp.zeros((share, LANES), F32)
     for place in range(4):
         here = (high == place // 2) & (core == place % 2)
         gram = jnp.where(here, total[place * share : (place + 1) * share, :], gram)
     scale = 1.0 / total_rows
-    gram_out[...] = (gram - (gram_part[:share, :] + less_ref[:share, :])) * scale
-    rhs = (total[4 * share : 4 * share + 1, :] - (rhs_part + less_ref[TILE : TILE + 1, :])) * scale
+    gram_out[...] = (gram - less[:share, :]) * scale
+    rhs = (total[high_rows : high_rows + 1, :] - less[share:, :]) * scale
     rhs_out[...] = pltpu.roll(rhs, LANES - first, 1)[:, :share]
+    copies.append(pltpu.make_async_copy(gram_out, gram_hbm, sems.at[0]))
+    copies.append(pltpu.make_async_copy(rhs_out, rhs_hbm, sems.at[1]))
+    for copy in copies[-2:]:
+        copy.start()
     for copy in copies:
         copy.wait()
 
@@ -363,8 +372,8 @@
     share = width // devices
     total_rows = rows * devices
     dy_width, pd_width = DY // (2 * blocks), devices * PD_DEV // (2 * blocks)
-    dy_high, pd_high = rounded(dy_width + 2), rounded(pd_width + 2)
-    gram_high = rounded(4 * share + 1)
+    dy_high, pd_high = rounded(dy_width + 2), rounded(pd_width + 3)
+    gram_high = rounded(4 * share)
     lines = rows // LANES
     groups = [
         [half * (devices // 2) + core_of + 2 * chip for chip in range(blocks)]
@@ -454,7 +463,7 @@
     mine = total_of(across(jnp.concatenate([keep + got, gram], axis=1)))
     means, gram = call(
         functools.partial(means_kernel, pd_width),
-        (shaped(blocks, pd_high, LANES), shaped(gram_high, LANES)),
+        (shaped(blocks, pd_high, LANES), shaped(gram_high + TILE, LANES)),
         (mine, to_half(mine)),
     )
     got = to_core(gram)
@@ -462,7 +471,7 @@
     other = to_core(means)
     x3, z3, less = call(
         functools.partial(own_kernel, blocks, pd_width, share),
-        (shaped(rows, width), shaped(lines, LANES), shaped(2 * TILE, LANES)),
+        (shaped(rows, width), shaped(lines, LANES), shaped(rounded(share + 1), LANES)),
         (x2, z2, means, owner, local),
         flops=wide * pd_half,
     )
@@ -470,9 +479,15 @@
         functools.partial(last_kernel, blocks, pd_width, share, total_rows),
         (shaped(rows, width), shaped(lines, LANES), shaped(share, LANES), shaped(1, share)),
         (x3, z3, other, less, gram, got, owner, local),
-        scratch=(pltpu.VMEM((rows, width), F32), pltpu.SemaphoreType.DMA((count,))),
+        scratch=(
+            pltpu.VMEM((rows, width), F32),
+            pltpu.VMEM((lines, LANES), F32),
+            pltpu.VMEM((share, LANES), F32),
+            pltpu.VMEM((1, share), F32),
+            pltpu.SemaphoreType.DMA((3 + count,)),
+        ),
         flops=wide * pd_half,
-        out_specs=[HBM, VMEM, VMEM, VMEM],
+        out_specs=[HBM] * 4,
     )
     return x3, z3.reshape(rows), gram, rhs.reshape(share)
 

time: 73.3 us -> 71.9 us (0.981)
  Pallas kernels: 13.7 us -> 12.3 us
    pallas_call x11, Pallas kernels: 13.7 us -> 12.3 us  [call(): pl.pallas_call(kernel, out_shape=tuple(outs), in_specs=in_specs or [VMEM]...]
  transfers between devices with their start and end apart: 7 -> 7, of which waited for: 4 -> 6; matrix products, arithmetic and copies ran while one was open for 0% -> 0% of each run, Pallas kernels for 7% -> 6%
where the time goes in v4:
time: 71.9 us; the launch traced here: 71.5 us
  blocking collectives  45.1 us (63%)
  Pallas kernels  12.3 us (17%)
  starting transfers between devices  6.66 us (9%)
  waiting for transfers between devices  6.57 us (9%)
  between operations  0.72 us (1%)
    all_to_all x4, blocking collectives, across(): return lax.all_to_all(v, AXIS, 0, 0, axis_index_groups=groups)  45.1 us
    pallas_call x11, Pallas kernels, call(): pl.pallas_call(kernel, out_shape=tuple(outs), in_specs=in_specs or [VMEM]...  12.3 us
    ppermute x2, waiting for transfers between devices, to_half(): return lax.ppermute(v, AXIS, opposite)  5.45 us
    ppermute x2, starting transfers between devices, to_half(): return lax.ppermute(v, AXIS, opposite)  5.41 us
  transfers between devices with their start and end apart: 7, of which 6 were waited for; matrix products, arithmetic and copies ran while one was open for 0% of the time, Pallas kernels for 6%

profile of v4, /device:TPU:0, one launch (start us, length us, event | category | flops | bytes accessed | tf_op | source)
XLA Modules:
  0.0 71.5 jit_solution(18205788000495148701)
XLA Ops:
  0.6 4.1 %shard_map.102 = (f32[2048,128]{1,0:T(8,128)S(1)}, f32[16,128]{1,0:T(8,128)S(1)}, f32[16,128]{1,0:T(8,128)S(1)}, s32[16,128]{1,0:T(8,128)S(1)}, bf16[2048,256]{1...) custom-call(f32[2048,128]{1,0:T(8,128)} %x_hbm.1, f32[16,128]{1,0:T(8,128)} %bitcast.16, f32[16,128]{1,0:T(8,128)} %bitcast.17, ...), custom_call_target="tpu_custom_call" | custom-call | flops 1342177280 | bytes 3760128 | tf_op jit(solution)/shard_map/pallas_call | solution.py:345
  4.7 0.5 collective-permute-start
  5.2 1.4 %shard_map.103 = f32[8,136,128]{2,1,0:T(8,128)S(1)} custom-call(bf16[2048,256]{1,0:T(8,128)(2,1)S(1)} %get-tuple-element.29.pairs_ref, f32[16,128]{1,0:T(8,128)S(1)} %get-tuple-element.28.z1_ref.z_ref, f32[16,128]{1,0:T(8,128)S(1)} %get-tuple-element.30.weight_ref, s32[16,128]{1,0:T(8,128)S(1)} %get-tuple-element.31.dy_ref), custom_call_target="tpu_custom_call" | custom-call | flops 1073741824 | bytes 1630208 | tf_op jit(solution)/shard_map/pallas_call | solution.py:345
  6.7 0.1 collective-permute-done
  6.8 0.1 add.6
  6.9 16.3 %all_to_all.20.in_ref = f32[8,136,128]{2,1,0:T(8,128)S(1)} all-to-all(f32[8,136,128]{2,1,0:T(8,128)S(1)} %add.6), channel_id=1, replica_groups={{0,2,4,6,8,10,12,14},{1,3,5,7,9,11,13,15},{16,18,20,22,24,26,28,30},{17..., dimensions={0} | all-to-all | bytes 1114112 | tf_op jit(solution)/shard_map/all_to_all | solution.py:397
  23.2 2.7 %collective-permute-start.1 = (f32[136,128]{1,0:T(8,128)S(1)}, f32[136,128]{1,0:T(8,128)S(1)}, u32[]{:S(2)}, u32[]{:S(2)}) collective-permute-start(f32[136,128]{1,0:T(8,128)S(1)} %shard_map.104.mine_ref), channel_id=1, source_target_pairs={{0,16},{1,17},{2,18},{3,19},{4,20},{5,21},{6,22},{7,23},{8,24},{9,... | collective-permute-start | bytes 208904 | tf_op jit(solution)/shard_map/ppermute | solution.py:394
  25.8 3.4 %collective-permute-done.1.got_ref = f32[136,128]{1,0:T(8,128)S(1)} collective-permute-done((f32[136,128]{1,0:T(8,128)S(1)}, f32[136,128]{1,0:T(8,128)S(1)}, u32[]{:S(2)}, u32[]{:S(2)}) %collective-permute-start.1) | collective-permute-done | bytes 69664 | tf_op jit(solution)/shard_map/ppermute | solution.py:394
  29.2 0.1 shard_map.105
  29.3 10.9 %all_to_all.21.means_ref = f32[8,136,128]{2,1,0:T(8,128)S(1)} all-to-all(f32[8,136,128]{2,1,0:T(8,128)S(1)} %shard_map.105), channel_id=1, replica_groups={{0,2,4,6,8,10,12,14},{1,3,5,7,9,11,13,15},{16,18,20,22,24,26,28,30},{17..., dimensions={0} | all-to-all | bytes 1114112 | tf_op jit(solution)/shard_map/all_to_all | solution.py:397
  40.2 0.0 collective-permute-start.2
  40.2 0.0 copy-start
  40.2 0.0 copy-start.1
  40.2 1.6 %shard_map.106 = (f32[2048,128]{1,0:T(8,128)S(1)}, f32[16,128]{1,0:T(8,128)S(1)}) custom-call(f32[2048,128]{1,0:T(8,128)S(1)} %get-tuple-element.27.x_ref, f32[16,128]{1,0:T(8,128)S(1)} %get-tuple-element.28.z1_ref.z_ref, f32[8,136,128]{2,1,0:T(8,128)S(1)} %all_to_all.21.means_ref, s32[16,128]{1,0:T(8,128)S(1)} %get-tuple-element.31.dy_ref), custom_call_target="tpu_custom_call" | custom-call | flops 1073741824 | bytes 2678784 | tf_op jit(solution)/shard_map/pallas_call | solution.py:345
  41.8 0.4 collective-permute-done.2.means_ref
  42.2 0.0 copy-done
  42.2 0.0 copy-done.1
  42.2 2.0 %shard_map.107 = (f32[2048,128]{1,0:T(8,128)S(1)}, f32[16,128]{1,0:T(8,128)S(1)}, bf16[2048,256]{1,0:T(8,128)(2,1)S(1)}, f32[8,40,128]{2,1,0:T(8,128)S(1)}) custom-call(f32[2048,128]{1,0:T(8,128)S(1)} %get-tuple-element.33.x_ref, f32[16,128]{1,0:T(8,128)S(1)} %get-tuple-element.34.z_ref, f32[8,136,128]{2,1,0:T(8,128)S(1)} %collective-permute-done.2.means_ref, ...), custom_call_target="tpu_custom_call" | custom-call | flops 1342177280 | bytes 3915776 | tf_op jit(solution)/shard_map/pallas_call | solution.py:345
  44.2 0.2 collective-permute-start.3
  44.4 0.9 %shard_map.108 = (f32[8,40,128]{2,1,0:T(8,128)S(1)}, f32[8,16,128]{2,1,0:T(8,128)S(1)}) custom-call(f32[2048,128]{1,0:T(8,128)S(1)} %get-tuple-element.35.x2_ref.x_ref, f32[16,128]{1,0:T(8,128)S(1)} %get-tuple-element.36.z2_ref.z_ref, bf16[2048,256]{1,0:T(8,128)(2,1)S(1)} %get-tuple-element.37.weighted_ref, f32[16,128]{1,0:T(8,128)S(1)} %get-tuple-element.30.weight_ref, ...), custom_call_target="tpu_custom_call" | custom-call | flops 536870912 | bytes 2359296 | tf_op jit(solution)/shard_map/pallas_call | solution.py:345
  45.4 0.3 collective-permute-done.3
  45.7 9.3 %all_to_all.22.in_ref = f32[8,56,128]{2,1,0:T(8,128)S(1)} all-to-all(f32[8,56,128]{2,1,0:T(8,128)S(1)} %pad_maximum_fusion), channel_id=1, replica_groups={{0,2,4,6,8,10,12,14},{1,3,5,7,9,11,13,15},{16,18,20,22,24,26,28,30},{17..., dimensions={0} | all-to-all | bytes 458752 | tf_op jit(solution)/shard_map/all_to_all | solution.py:397
  55.1 2.8 %collective-permute-start.4 = (f32[56,128]{1,0:T(8,128)S(1)}, f32[56,128]{1,0:T(8,128)S(1)}, u32[]{:S(2)}, u32[]{:S(2)}) collective-permute-start(f32[56,128]{1,0:T(8,128)S(1)} %shard_map.109.mine_ref), channel_id=1, source_target_pairs={{0,16},{1,17},{2,18},{3,19},{4,20},{5,21},{6,22},{7,23},{8,24},{9,... | collective-permute-start | bytes 86024 | tf_op jit(solution)/shard_map/ppermute | solution.py:394
  57.8 2.1 %collective-permute-done.4.got_ref = f32[56,128]{1,0:T(8,128)S(1)} collective-permute-done((f32[56,128]{1,0:T(8,128)S(1)}, f32[56,128]{1,0:T(8,128)S(1)}, u32[]{:S(2)}, u32[]{:S(2)}) %collective-permute-start.4) | collective-permute-done | bytes 28704 | tf_op jit(solution)/shard_map/ppermute | solution.py:394
  59.9 0.1 shard_map.110
  60.0 8.6 %all_to_all.23.means_ref = f32[8,40,128]{2,1,0:T(8,128)S(1)} all-to-all(f32[8,40,128]{2,1,0:T(8,128)S(1)} %get-tuple-element.41), channel_id=1, replica_groups={{0,2,4,6,8,10,12,14},{1,3,5,7,9,11,13,15},{16,18,20,22,24,26,28,30},{17..., dimensions={0} | all-to-all | bytes 327680 | tf_op jit(solution)/shard_map/all_to_all | solution.py:397
  68.6 0.0 collective-permute-start.5
  68.6 0.5 collective-permute-start.6
  69.2 0.6 shard_map.111
  69.8 0.3 collective-permute-done.6.got_ref
  70.1 0.0 collective-permute-done.5.means_ref
  70.1 1.5 %shard_map.112 = (f32[2048,128]{1,0:T(8,128)}, f32[16,128]{1,0:T(8,128)}, f32[4,128]{1,0:T(4,128)}, f32[1,4]{1,0:T(1,128)}) custom-call(f32[2048,128]{1,0:T(8,128)S(1)} %get-tuple-element.42.x_ref, f32[16,128]{1,0:T(8,128)S(1)} %get-tuple-element.43.z_ref, f32[8,40,128]{2,1,0:T(8,128)S(1)} %collective-permute-done.5.means_ref, ...), custom_call_target="tpu_custom_call" | custom-call | flops 268435456 | bytes 2324496 | tf_op jit(solution)/shard_map/pallas_call | solution.py:345
  (4 shorter events, 0.1 us)
Async XLA Ops:
  4.7 2.1 %collective-permute-start = (f32[8,136,128]{2,1,0:T(8,128)S(1)}, f32[8,136,128]{2,1,0:T(8,128)S(1)}, u32[]{:S(2)}, u32[]{:S(2)}) collective-permute-start(f32[8,136,128]{2,1,0:T(8,128)S(1)} %get-tuple-element.32), channel_id=1, source_target_pairs={{0,1},{1,0},{2,3},{3,2},{4,5},{5,4},{6,7},{7,6},{8,9},{9,8},{10,11... | collective-permute-start | bytes 1671176 | tf_op jit(solution)/shard_map/ppermute | solution.py:391
  23.2 6.0 %collective-permute-start.1 = (f32[136,128]{1,0:T(8,128)S(1)}, f32[136,128]{1,0:T(8,128)S(1)}, u32[]{:S(2)}, u32[]{:S(2)}) collective-permute-start(f32[136,128]{1,0:T(8,128)S(1)} %shard_map.104.mine_ref), channel_id=1, source_target_pairs={{0,16},{1,17},{2,18},{3,19},{4,20},{5,21},{6,22},{7,23},{8,24},{9,... | collective-permute-start | bytes 208904 | tf_op jit(solution)/shard_map/ppermute | solution.py:394
  40.2 2.0 %collective-permute-start.2 = (f32[8,136,128]{2,1,0:T(8,128)S(1)}, f32[8,136,128]{2,1,0:T(8,128)S(1)}, u32[]{:S(2)}, u32[]{:S(2)}) collective-permute-start(f32[8,136,128]{2,1,0:T(8,128)S(1)} %all_to_all.21.means_ref), channel_id=1, source_target_pairs={{0,1},{1,0},{2,3},{3,2},{4,5},{5,4},{6,7},{7,6},{8,9},{9,8},{10,11... | collective-permute-start | bytes 1671176 | tf_op jit(solution)/shard_map/ppermute | solution.py:391
  40.2 2.0 %copy-start = (s32[2048,1]{0,1:T(1,128)S(1)}, s32[2048,1]{0,1:T(1,128)}, u32[]{:S(2)}) copy-start(s32[2048,1]{0,1:T(1,128)} %param.12) | copy-start | bytes 24580
  40.2 2.0 %copy-start.1 = (s32[2048]{0:T(1024)S(1)}, s32[2048]{0:T(1024)}, u32[]{:S(2)}) copy-start(s32[2048]{0:T(1024)} %param.13) | copy-start | bytes 24580
  44.2 1.5 %collective-permute-start.3 = (f32[8,40,128]{2,1,0:T(8,128)S(1)}, f32[8,40,128]{2,1,0:T(8,128)S(1)}, u32[]{:S(2)}, u32[]{:S(2)}) collective-permute-start(f32[8,40,128]{2,1,0:T(8,128)S(1)} %get-tuple-element.39), channel_id=1, source_target_pairs={{0,1},{1,0},{2,3},{3,2},{4,5},{5,4},{6,7},{7,6},{8,9},{9,8},{10,11... | collective-permute-start | bytes 491528 | tf_op jit(solution)/shard_map/ppermute | solution.py:391
  55.1 4.8 %collective-permute-start.4 = (f32[56,128]{1,0:T(8,128)S(1)}, f32[56,128]{1,0:T(8,128)S(1)}, u32[]{:S(2)}, u32[]{:S(2)}) collective-permute-start(f32[56,128]{1,0:T(8,128)S(1)} %shard_map.109.mine_ref), channel_id=1, source_target_pairs={{0,16},{1,17},{2,18},{3,19},{4,20},{5,21},{6,22},{7,23},{8,24},{9,... | collective-permute-start | bytes 86024 | tf_op jit(solution)/shard_map/ppermute | solution.py:394
  68.6 1.4 %collective-permute-start.5 = (f32[8,40,128]{2,1,0:T(8,128)S(1)}, f32[8,40,128]{2,1,0:T(8,128)S(1)}, u32[]{:S(2)}, u32[]{:S(2)}) collective-permute-start(f32[8,40,128]{2,1,0:T(8,128)S(1)} %all_to_all.23.means_ref), channel_id=1, source_target_pairs={{0,1},{1,0},{2,3},{3,2},{4,5},{5,4},{6,7},{7,6},{8,9},{9,8},{10,11... | collective-permute-start | bytes 491528 | tf_op jit(solution)/shard_map/ppermute | solution.py:391
  68.6 1.4 %collective-permute-start.6 = (f32[24,128]{1,0:T(8,128)S(1)}, f32[24,128]{1,0:T(8,128)S(1)}, u32[]{:S(2)}, u32[]{:S(2)}) collective-permute-start(f32[24,128]{1,0:T(8,128)S(1)} %get-tuple-element.45.mine_ref), channel_id=1, source_target_pairs={{0,1},{1,0},{2,3},{3,2},{4,5},{5,4},{6,7},{7,6},{8,9},{9,8},{10,11... | collective-permute-start | bytes 36872 | tf_op jit(solution)/shard_map/ppermute | solution.py:391

commit v5 on v4

--- a/solution.py
+++ b/solution.py
@@ -161,15 +161,17 @@
     for i, a in enumerate(starts):
         copies[len(small) + i].wait()
         span = slice(a * LANES, (a + chunk) * LANES)
+        if a == 0:
+            offset = jnp.sum(x_ref[row_block(0), :], axis=0, keepdims=True) * (1.0 / LANES)
         for b in range(a, a + chunk):
-            pairs_ref[row_block(b), :] = pair(x_ref[row_block(b), :] * weight_t[:, b : b + 1])
+            pairs_ref[row_block(b), :] = pair((x_ref[row_block(b), :] - offset) * weight_t[:, b : b + 1])
         sum_x += dot(table[:, span], pairs_ref[span, :])
     mean_x = pair(unpair(sum_x) / denominator)
     z1 = []
     for a in range(count):
         if a % group == 0:
             picked = unpair(dot_first(table[:, a * LANES : (a + group) * LANES], mean_x))
-        x1 = x_ref[row_block(a), :] - picked[row_block(a % group), :]
+        x1 = (x_ref[row_block(a), :] - offset) - picked[row_block(a % group), :]
         x1_ref[row_block(a), :] = x1
         pairs_ref[row_block(a), :] = pair(x1 * weight_t[:, a : a + 1])
         picked_z = jnp.sum(jnp.where(masks[a], mean_z, 0.0), axis=0, keepdims=True)

time: 71.9 us -> 71.9 us (level)
  no operation moved by 1% of the time
where the time goes in v5:
time: 71.9 us; the launch traced here: 71.5 us
  blocking collectives  45.1 us (63%)
  Pallas kernels  12.3 us (17%)
  starting transfers between devices  6.67 us (9%)
  waiting for transfers between devices  6.57 us (9%)
  between operations  0.72 us (1%)
    all_to_all x4, blocking collectives, across(): return lax.all_to_all(v, AXIS, 0, 0, axis_index_groups=groups)  45.1 us
    pallas_call x11, Pallas kernels, call(): pl.pallas_call(kernel, out_shape=tuple(outs), in_specs=in_specs or [VMEM]...  12.3 us
    ppermute x2, waiting for transfers between devices, to_half(): return lax.ppermute(v, AXIS, opposite)  5.45 us
    ppermute x2, starting transfers between devices, to_half(): return lax.ppermute(v, AXIS, opposite)  5.41 us
  transfers between devices with their start and end apart: 7, of which 6 were waited for; matrix products, arithmetic and copies ran while one was open for 0% of the time, Pallas kernels for 6%

profile of v5, /device:TPU:0, one launch (start us, length us, event | category | flops | bytes accessed | tf_op | source)
XLA Modules:
  0.0 71.5 jit_solution(7267937101081852502)
XLA Ops:
  0.6 4.1 %shard_map.102 = (f32[2048,128]{1,0:T(8,128)S(1)}, f32[16,128]{1,0:T(8,128)S(1)}, f32[16,128]{1,0:T(8,128)S(1)}, s32[16,128]{1,0:T(8,128)S(1)}, bf16[2048,256]{1...) custom-call(f32[2048,128]{1,0:T(8,128)} %x_hbm.1, f32[16,128]{1,0:T(8,128)} %bitcast.16, f32[16,128]{1,0:T(8,128)} %bitcast.17, ...), custom_call_target="tpu_custom_call" | custom-call | flops 1342177280 | bytes 3760128 | tf_op jit(solution)/shard_map/pallas_call | solution.py:347
  4.7 0.5 collective-permute-start
  5.2 1.4 %shard_map.103 = f32[8,136,128]{2,1,0:T(8,128)S(1)} custom-call(bf16[2048,256]{1,0:T(8,128)(2,1)S(1)} %get-tuple-element.29.pairs_ref, f32[16,128]{1,0:T(8,128)S(1)} %get-tuple-element.28.z1_ref.z_ref, f32[16,128]{1,0:T(8,128)S(1)} %get-tuple-element.30.weight_ref, s32[16,128]{1,0:T(8,128)S(1)} %get-tuple-element.31.dy_ref), custom_call_target="tpu_custom_call" | custom-call | flops 1073741824 | bytes 1630208 | tf_op jit(solution)/shard_map/pallas_call | solution.py:347
  6.7 0.1 collective-permute-done
  6.8 0.1 add.6
  6.9 16.3 %all_to_all.20.in_ref = f32[8,136,128]{2,1,0:T(8,128)S(1)} all-to-all(f32[8,136,128]{2,1,0:T(8,128)S(1)} %add.6), channel_id=1, replica_groups={{0,2,4,6,8,10,12,14},{1,3,5,7,9,11,13,15},{16,18,20,22,24,26,28,30},{17..., dimensions={0} | all-to-all | bytes 1114112 | tf_op jit(solution)/shard_map/all_to_all | solution.py:399
  23.2 2.7 %collective-permute-start.1 = (f32[136,128]{1,0:T(8,128)S(1)}, f32[136,128]{1,0:T(8,128)S(1)}, u32[]{:S(2)}, u32[]{:S(2)}) collective-permute-start(f32[136,128]{1,0:T(8,128)S(1)} %shard_map.104.mine_ref), channel_id=1, source_target_pairs={{0,16},{1,17},{2,18},{3,19},{4,20},{5,21},{6,22},{7,23},{8,24},{9,... | collective-permute-start | bytes 208904 | tf_op jit(solution)/shard_map/ppermute | solution.py:396
  25.9 3.4 %collective-permute-done.1.got_ref = f32[136,128]{1,0:T(8,128)S(1)} collective-permute-done((f32[136,128]{1,0:T(8,128)S(1)}, f32[136,128]{1,0:T(8,128)S(1)}, u32[]{:S(2)}, u32[]{:S(2)}) %collective-permute-start.1) | collective-permute-done | bytes 69664 | tf_op jit(solution)/shard_map/ppermute | solution.py:396
  29.2 0.1 shard_map.105
  29.4 10.9 %all_to_all.21.means_ref = f32[8,136,128]{2,1,0:T(8,128)S(1)} all-to-all(f32[8,136,128]{2,1,0:T(8,128)S(1)} %shard_map.105), channel_id=1, replica_groups={{0,2,4,6,8,10,12,14},{1,3,5,7,9,11,13,15},{16,18,20,22,24,26,28,30},{17..., dimensions={0} | all-to-all | bytes 1114112 | tf_op jit(solution)/shard_map/all_to_all | solution.py:399
  40.2 0.0 collective-permute-start.2
  40.2 0.0 copy-start
  40.2 0.0 copy-start.1
  40.2 1.6 %shard_map.106 = (f32[2048,128]{1,0:T(8,128)S(1)}, f32[16,128]{1,0:T(8,128)S(1)}) custom-call(f32[2048,128]{1,0:T(8,128)S(1)} %get-tuple-element.27.x_ref, f32[16,128]{1,0:T(8,128)S(1)} %get-tuple-element.28.z1_ref.z_ref, f32[8,136,128]{2,1,0:T(8,128)S(1)} %all_to_all.21.means_ref, s32[16,128]{1,0:T(8,128)S(1)} %get-tuple-element.31.dy_ref), custom_call_target="tpu_custom_call" | custom-call | flops 1073741824 | bytes 2678784 | tf_op jit(solution)/shard_map/pallas_call | solution.py:347
  41.8 0.4 collective-permute-done.2.means_ref
  42.2 0.0 copy-done
  42.2 0.0 copy-done.1
  42.2 2.0 %shard_map.107 = (f32[2048,128]{1,0:T(8,128)S(1)}, f32[16,128]{1,0:T(8,128)S(1)}, bf16[2048,256]{1,0:T(8,128)(2,1)S(1)}, f32[8,40,128]{2,1,0:T(8,128)S(1)}) custom-call(f32[2048,128]{1,0:T(8,128)S(1)} %get-tuple-element.33.x_ref, f32[16,128]{1,0:T(8,128)S(1)} %get-tuple-element.34.z_ref, f32[8,136,128]{2,1,0:T(8,128)S(1)} %collective-permute-done.2.means_ref, ...), custom_call_target="tpu_custom_call" | custom-call | flops 1342177280 | bytes 3915776 | tf_op jit(solution)/shard_map/pallas_call | solution.py:347
  44.2 0.2 collective-permute-start.3
  44.5 0.9 %shard_map.108 = (f32[8,40,128]{2,1,0:T(8,128)S(1)}, f32[8,16,128]{2,1,0:T(8,128)S(1)}) custom-call(f32[2048,128]{1,0:T(8,128)S(1)} %get-tuple-element.35.x2_ref.x_ref, f32[16,128]{1,0:T(8,128)S(1)} %get-tuple-element.36.z2_ref.z_ref, bf16[2048,256]{1,0:T(8,128)(2,1)S(1)} %get-tuple-element.37.weighted_ref, f32[16,128]{1,0:T(8,128)S(1)} %get-tuple-element.30.weight_ref, ...), custom_call_target="tpu_custom_call" | custom-call | flops 536870912 | bytes 2359296 | tf_op jit(solution)/shard_map/pallas_call | solution.py:347
  45.4 0.3 collective-permute-done.3
  45.7 9.3 %all_to_all.22.in_ref = f32[8,56,128]{2,1,0:T(8,128)S(1)} all-to-all(f32[8,56,128]{2,1,0:T(8,128)S(1)} %pad_maximum_fusion), channel_id=1, replica_groups={{0,2,4,6,8,10,12,14},{1,3,5,7,9,11,13,15},{16,18,20,22,24,26,28,30},{17..., dimensions={0} | all-to-all | bytes 458752 | tf_op jit(solution)/shard_map/all_to_all | solution.py:399
  55.1 2.8 %collective-permute-start.4 = (f32[56,128]{1,0:T(8,128)S(1)}, f32[56,128]{1,0:T(8,128)S(1)}, u32[]{:S(2)}, u32[]{:S(2)}) collective-permute-start(f32[56,128]{1,0:T(8,128)S(1)} %shard_map.109.mine_ref), channel_id=1, source_target_pairs={{0,16},{1,17},{2,18},{3,19},{4,20},{5,21},{6,22},{7,23},{8,24},{9,... | collective-permute-start | bytes 86024 | tf_op jit(solution)/shard_map/ppermute | solution.py:396
  57.8 2.1 %collective-permute-done.4.got_ref = f32[56,128]{1,0:T(8,128)S(1)} collective-permute-done((f32[56,128]{1,0:T(8,128)S(1)}, f32[56,128]{1,0:T(8,128)S(1)}, u32[]{:S(2)}, u32[]{:S(2)}) %collective-permute-start.4) | collective-permute-done | bytes 28704 | tf_op jit(solution)/shard_map/ppermute | solution.py:396
  59.9 0.1 shard_map.110
  60.0 8.6 %all_to_all.23.means_ref = f32[8,40,128]{2,1,0:T(8,128)S(1)} all-to-all(f32[8,40,128]{2,1,0:T(8,128)S(1)} %get-tuple-element.41), channel_id=1, replica_groups={{0,2,4,6,8,10,12,14},{1,3,5,7,9,11,13,15},{16,18,20,22,24,26,28,30},{17..., dimensions={0} | all-to-all | bytes 327680 | tf_op jit(solution)/shard_map/all_to_all | solution.py:399
  68.6 0.0 collective-permute-start.5
  68.7 0.5 collective-permute-start.6
  69.2 0.6 shard_map.111
  69.8 0.3 collective-permute-done.6.got_ref
  70.1 0.0 collective-permute-done.5.means_ref
  70.1 1.5 %shard_map.112 = (f32[2048,128]{1,0:T(8,128)}, f32[16,128]{1,0:T(8,128)}, f32[4,128]{1,0:T(4,128)}, f32[1,4]{1,0:T(1,128)}) custom-call(f32[2048,128]{1,0:T(8,128)S(1)} %get-tuple-element.42.x_ref, f32[16,128]{1,0:T(8,128)S(1)} %get-tuple-element.43.z_ref, f32[8,40,128]{2,1,0:T(8,128)S(1)} %collective-permute-done.5.means_ref, ...), custom_call_target="tpu_custom_call" | custom-call | flops 268435456 | bytes 2324496 | tf_op jit(solution)/shard_map/pallas_call | solution.py:347
  (4 shorter events, 0.1 us)
Async XLA Ops:
  4.7 2.1 %collective-permute-start = (f32[8,136,128]{2,1,0:T(8,128)S(1)}, f32[8,136,128]{2,1,0:T(8,128)S(1)}, u32[]{:S(2)}, u32[]{:S(2)}) collective-permute-start(f32[8,136,128]{2,1,0:T(8,128)S(1)} %get-tuple-element.32), channel_id=1, source_target_pairs={{0,1},{1,0},{2,3},{3,2},{4,5},{5,4},{6,7},{7,6},{8,9},{9,8},{10,11... | collective-permute-start | bytes 1671176 | tf_op jit(solution)/shard_map/ppermute | solution.py:393
  23.2 6.0 %collective-permute-start.1 = (f32[136,128]{1,0:T(8,128)S(1)}, f32[136,128]{1,0:T(8,128)S(1)}, u32[]{:S(2)}, u32[]{:S(2)}) collective-permute-start(f32[136,128]{1,0:T(8,128)S(1)} %shard_map.104.mine_ref), channel_id=1, source_target_pairs={{0,16},{1,17},{2,18},{3,19},{4,20},{5,21},{6,22},{7,23},{8,24},{9,... | collective-permute-start | bytes 208904 | tf_op jit(solution)/shard_map/ppermute | solution.py:396
  40.2 2.0 %collective-permute-start.2 = (f32[8,136,128]{2,1,0:T(8,128)S(1)}, f32[8,136,128]{2,1,0:T(8,128)S(1)}, u32[]{:S(2)}, u32[]{:S(2)}) collective-permute-start(f32[8,136,128]{2,1,0:T(8,128)S(1)} %all_to_all.21.means_ref), channel_id=1, source_target_pairs={{0,1},{1,0},{2,3},{3,2},{4,5},{5,4},{6,7},{7,6},{8,9},{9,8},{10,11... | collective-permute-start | bytes 1671176 | tf_op jit(solution)/shard_map/ppermute | solution.py:393
  40.2 2.0 %copy-start = (s32[2048,1]{0,1:T(1,128)S(1)}, s32[2048,1]{0,1:T(1,128)}, u32[]{:S(2)}) copy-start(s32[2048,1]{0,1:T(1,128)} %param.12) | copy-start | bytes 24580
  40.2 2.0 %copy-start.1 = (s32[2048]{0:T(1024)S(1)}, s32[2048]{0:T(1024)}, u32[]{:S(2)}) copy-start(s32[2048]{0:T(1024)} %param.13) | copy-start | bytes 24580
  44.2 1.5 %collective-permute-start.3 = (f32[8,40,128]{2,1,0:T(8,128)S(1)}, f32[8,40,128]{2,1,0:T(8,128)S(1)}, u32[]{:S(2)}, u32[]{:S(2)}) collective-permute-start(f32[8,40,128]{2,1,0:T(8,128)S(1)} %get-tuple-element.39), channel_id=1, source_target_pairs={{0,1},{1,0},{2,3},{3,2},{4,5},{5,4},{6,7},{7,6},{8,9},{9,8},{10,11... | collective-permute-start | bytes 491528 | tf_op jit(solution)/shard_map/ppermute | solution.py:393
  55.1 4.8 %collective-permute-start.4 = (f32[56,128]{1,0:T(8,128)S(1)}, f32[56,128]{1,0:T(8,128)S(1)}, u32[]{:S(2)}, u32[]{:S(2)}) collective-permute-start(f32[56,128]{1,0:T(8,128)S(1)} %shard_map.109.mine_ref), channel_id=1, source_target_pairs={{0,16},{1,17},{2,18},{3,19},{4,20},{5,21},{6,22},{7,23},{8,24},{9,... | collective-permute-start | bytes 86024 | tf_op jit(solution)/shard_map/ppermute | solution.py:396
  68.6 1.4 %collective-permute-start.5 = (f32[8,40,128]{2,1,0:T(8,128)S(1)}, f32[8,40,128]{2,1,0:T(8,128)S(1)}, u32[]{:S(2)}, u32[]{:S(2)}) collective-permute-start(f32[8,40,128]{2,1,0:T(8,128)S(1)} %all_to_all.23.means_ref), channel_id=1, source_target_pairs={{0,1},{1,0},{2,3},{3,2},{4,5},{5,4},{6,7},{7,6},{8,9},{9,8},{10,11... | collective-permute-start | bytes 491528 | tf_op jit(solution)/shard_map/ppermute | solution.py:393
  68.7 1.4 %collective-permute-start.6 = (f32[24,128]{1,0:T(8,128)S(1)}, f32[24,128]{1,0:T(8,128)S(1)}, u32[]{:S(2)}, u32[]{:S(2)}) collective-permute-start(f32[24,128]{1,0:T(8,128)S(1)} %get-tuple-element.45.mine_ref), channel_id=1, source_target_pairs={{0,1},{1,0},{2,3},{3,2},{4,5},{5,4},{6,7},{7,6},{8,9},{9,8},{10,11... | collective-permute-start | bytes 36872 | tf_op jit(solution)/shard_map/ppermute | solution.py:393

commit v6 on v5

--- a/solution.py
+++ b/solution.py
@@ -112,10 +112,11 @@
     labels = iota((count, LANES), 0) + base
     z_new = []
     for a in range(0, lines, group):
-        for b in range(a, a + group):
-            mask = onehot(iota((blocks, LANES), 0) == block[b : b + 1, :])
-            candidates = dot(left, jnp.concatenate([mask, mask, mask], axis=0))
-            chosen = jnp.where(iota((width, LANES), 0) == place[b : b + 1, :], candidates, 0.0)
+        span = range(a, a + group)
+        mask = jnp.concatenate([onehot(iota((blocks, LANES), 0) == block[b : b + 1, :]) for b in span], axis=1)
+        candidates = dot(left, jnp.concatenate([mask, mask, mask], axis=0))
+        for b in span:
+            chosen = jnp.where(iota((width, LANES), 0) == place[b : b + 1, :], candidates[:, row_block(b - a)], 0.0)
             z_new.append(z[b : b + 1, :] - jnp.sum(chosen, axis=0, keepdims=True))
         mask = jnp.concatenate([onehot(labels == ids[b : b + 1, :]) for b in range(a, a + group)], axis=1)
         picked = unpair(dot_first(mask, table))

time: 71.9 us -> 71.8 us (level)
  no operation moved by 1% of the time
where the time goes in v6:
time: 71.8 us; the launch traced here: 71.4 us
  blocking collectives  45.1 us (63%)
  Pallas kernels  12.2 us (17%)
  starting transfers between devices  6.65 us (9%)
  waiting for transfers between devices  6.61 us (9%)
  between operations  0.72 us (1%)
    all_to_all x4, blocking collectives, across(): return lax.all_to_all(v, AXIS, 0, 0, axis_index_groups=groups)  45.1 us
    pallas_call x11, Pallas kernels, call(): pl.pallas_call(kernel, out_shape=tuple(outs), in_specs=in_specs or [VMEM]...  12.2 us
    ppermute x2, waiting for transfers between devices, to_half(): return lax.ppermute(v, AXIS, opposite)  5.45 us
    ppermute x2, starting transfers between devices, to_half(): return lax.ppermute(v, AXIS, opposite)  5.41 us
  transfers between devices with their start and end apart: 7, of which 6 were waited for; matrix products, arithmetic and copies ran while one was open for 0% of the time, Pallas kernels for 6%

profile of v6, /device:TPU:0, one launch (start us, length us, event | category | flops | bytes accessed | tf_op | source)
XLA Modules:
  0.0 71.4 jit_solution(11144999823485977303)
XLA Ops:
  0.6 4.1 %shard_map.102 = (f32[2048,128]{1,0:T(8,128)S(1)}, f32[16,128]{1,0:T(8,128)S(1)}, f32[16,128]{1,0:T(8,128)S(1)}, s32[16,128]{1,0:T(8,128)S(1)}, bf16[2048,256]{1...) custom-call(f32[2048,128]{1,0:T(8,128)} %x_hbm.1, f32[16,128]{1,0:T(8,128)} %bitcast.16, f32[16,128]{1,0:T(8,128)} %bitcast.17, ...), custom_call_target="tpu_custom_call" | custom-call | flops 1342177280 | bytes 3760128 | tf_op jit(solution)/shard_map/pallas_call | solution.py:348
  4.7 0.5 collective-permute-start
  5.2 1.4 %shard_map.103 = f32[8,136,128]{2,1,0:T(8,128)S(1)} custom-call(bf16[2048,256]{1,0:T(8,128)(2,1)S(1)} %get-tuple-element.29.pairs_ref, f32[16,128]{1,0:T(8,128)S(1)} %get-tuple-element.28.z1_ref.z_ref, f32[16,128]{1,0:T(8,128)S(1)} %get-tuple-element.30.weight_ref, s32[16,128]{1,0:T(8,128)S(1)} %get-tuple-element.31.dy_ref), custom_call_target="tpu_custom_call" | custom-call | flops 1073741824 | bytes 1630208 | tf_op jit(solution)/shard_map/pallas_call | solution.py:348
  6.7 0.1 collective-permute-done
  6.8 0.1 add.6
  6.9 16.3 %all_to_all.20.in_ref = f32[8,136,128]{2,1,0:T(8,128)S(1)} all-to-all(f32[8,136,128]{2,1,0:T(8,128)S(1)} %add.6), channel_id=1, replica_groups={{0,2,4,6,8,10,12,14},{1,3,5,7,9,11,13,15},{16,18,20,22,24,26,28,30},{17..., dimensions={0} | all-to-all | bytes 1114112 | tf_op jit(solution)/shard_map/all_to_all | solution.py:400
  23.2 2.7 %collective-permute-start.1 = (f32[136,128]{1,0:T(8,128)S(1)}, f32[136,128]{1,0:T(8,128)S(1)}, u32[]{:S(2)}, u32[]{:S(2)}) collective-permute-start(f32[136,128]{1,0:T(8,128)S(1)} %shard_map.104.mine_ref), channel_id=1, source_target_pairs={{0,16},{1,17},{2,18},{3,19},{4,20},{5,21},{6,22},{7,23},{8,24},{9,... | collective-permute-start | bytes 208904 | tf_op jit(solution)/shard_map/ppermute | solution.py:397
  25.9 3.4 %collective-permute-done.1.got_ref = f32[136,128]{1,0:T(8,128)S(1)} collective-permute-done((f32[136,128]{1,0:T(8,128)S(1)}, f32[136,128]{1,0:T(8,128)S(1)}, u32[]{:S(2)}, u32[]{:S(2)}) %collective-permute-start.1) | collective-permute-done | bytes 69664 | tf_op jit(solution)/shard_map/ppermute | solution.py:397
  29.2 0.1 shard_map.105
  29.4 10.9 %all_to_all.21.means_ref = f32[8,136,128]{2,1,0:T(8,128)S(1)} all-to-all(f32[8,136,128]{2,1,0:T(8,128)S(1)} %shard_map.105), channel_id=1, replica_groups={{0,2,4,6,8,10,12,14},{1,3,5,7,9,11,13,15},{16,18,20,22,24,26,28,30},{17..., dimensions={0} | all-to-all | bytes 1114112 | tf_op jit(solution)/shard_map/all_to_all | solution.py:400
  40.2 0.0 collective-permute-start.2
  40.2 0.0 copy-start
  40.2 0.0 copy-start.1
  40.2 1.5 %shard_map.106 = (f32[2048,128]{1,0:T(8,128)S(1)}, f32[16,128]{1,0:T(8,128)S(1)}) custom-call(f32[2048,128]{1,0:T(8,128)S(1)} %get-tuple-element.27.x_ref, f32[16,128]{1,0:T(8,128)S(1)} %get-tuple-element.28.z1_ref.z_ref, f32[8,136,128]{2,1,0:T(8,128)S(1)} %all_to_all.21.means_ref, s32[16,128]{1,0:T(8,128)S(1)} %get-tuple-element.31.dy_ref), custom_call_target="tpu_custom_call" | custom-call | flops 1073741824 | bytes 2678784 | tf_op jit(solution)/shard_map/pallas_call | solution.py:348
  41.8 0.4 collective-permute-done.2.means_ref
  42.2 0.0 copy-done
  42.2 0.0 copy-done.1
  42.2 2.0 %shard_map.107 = (f32[2048,128]{1,0:T(8,128)S(1)}, f32[16,128]{1,0:T(8,128)S(1)}, bf16[2048,256]{1,0:T(8,128)(2,1)S(1)}, f32[8,40,128]{2,1,0:T(8,128)S(1)}) custom-call(f32[2048,128]{1,0:T(8,128)S(1)} %get-tuple-element.33.x_ref, f32[16,128]{1,0:T(8,128)S(1)} %get-tuple-element.34.z_ref, f32[8,136,128]{2,1,0:T(8,128)S(1)} %collective-permute-done.2.means_ref, ...), custom_call_target="tpu_custom_call" | custom-call | flops 1342177280 | bytes 3915776 | tf_op jit(solution)/shard_map/pallas_call | solution.py:348
  44.2 0.2 collective-permute-start.3
  44.4 0.9 %shard_map.108 = (f32[8,40,128]{2,1,0:T(8,128)S(1)}, f32[8,16,128]{2,1,0:T(8,128)S(1)}) custom-call(f32[2048,128]{1,0:T(8,128)S(1)} %get-tuple-element.35.x2_ref.x_ref, f32[16,128]{1,0:T(8,128)S(1)} %get-tuple-element.36.z2_ref.z_ref, bf16[2048,256]{1,0:T(8,128)(2,1)S(1)} %get-tuple-element.37.weighted_ref, f32[16,128]{1,0:T(8,128)S(1)} %get-tuple-element.30.weight_ref, ...), custom_call_target="tpu_custom_call" | custom-call | flops 536870912 | bytes 2359296 | tf_op jit(solution)/shard_map/pallas_call | solution.py:348
  45.3 0.3 collective-permute-done.3
  45.7 9.3 %all_to_all.22.in_ref = f32[8,56,128]{2,1,0:T(8,128)S(1)} all-to-all(f32[8,56,128]{2,1,0:T(8,128)S(1)} %pad_maximum_fusion), channel_id=1, replica_groups={{0,2,4,6,8,10,12,14},{1,3,5,7,9,11,13,15},{16,18,20,22,24,26,28,30},{17..., dimensions={0} | all-to-all | bytes 458752 | tf_op jit(solution)/shard_map/all_to_all | solution.py:400
  55.0 2.8 %collective-permute-start.4 = (f32[56,128]{1,0:T(8,128)S(1)}, f32[56,128]{1,0:T(8,128)S(1)}, u32[]{:S(2)}, u32[]{:S(2)}) collective-permute-start(f32[56,128]{1,0:T(8,128)S(1)} %shard_map.109.mine_ref), channel_id=1, source_target_pairs={{0,16},{1,17},{2,18},{3,19},{4,20},{5,21},{6,22},{7,23},{8,24},{9,... | collective-permute-start | bytes 86024 | tf_op jit(solution)/shard_map/ppermute | solution.py:397
  57.8 2.1 %collective-permute-done.4.got_ref = f32[56,128]{1,0:T(8,128)S(1)} collective-permute-done((f32[56,128]{1,0:T(8,128)S(1)}, f32[56,128]{1,0:T(8,128)S(1)}, u32[]{:S(2)}, u32[]{:S(2)}) %collective-permute-start.4) | collective-permute-done | bytes 28704 | tf_op jit(solution)/shard_map/ppermute | solution.py:397
  59.8 0.1 shard_map.110
  59.9 8.6 %all_to_all.23.means_ref = f32[8,40,128]{2,1,0:T(8,128)S(1)} all-to-all(f32[8,40,128]{2,1,0:T(8,128)S(1)} %get-tuple-element.41), channel_id=1, replica_groups={{0,2,4,6,8,10,12,14},{1,3,5,7,9,11,13,15},{16,18,20,22,24,26,28,30},{17..., dimensions={0} | all-to-all | bytes 327680 | tf_op jit(solution)/shard_map/all_to_all | solution.py:400
  68.6 0.0 collective-permute-start.5
  68.6 0.5 collective-permute-start.6
  69.1 0.6 shard_map.111
  69.7 0.3 collective-permute-done.6.got_ref
  70.0 0.0 collective-permute-done.5.means_ref
  70.0 1.4 %shard_map.112 = (f32[2048,128]{1,0:T(8,128)}, f32[16,128]{1,0:T(8,128)}, f32[4,128]{1,0:T(4,128)}, f32[1,4]{1,0:T(1,128)}) custom-call(f32[2048,128]{1,0:T(8,128)S(1)} %get-tuple-element.42.x_ref, f32[16,128]{1,0:T(8,128)S(1)} %get-tuple-element.43.z_ref, f32[8,40,128]{2,1,0:T(8,128)S(1)} %collective-permute-done.5.means_ref, ...), custom_call_target="tpu_custom_call" | custom-call | flops 268435456 | bytes 2324496 | tf_op jit(solution)/shard_map/pallas_call | solution.py:348
  (4 shorter events, 0.1 us)
Async XLA Ops:
  4.7 2.1 %collective-permute-start = (f32[8,136,128]{2,1,0:T(8,128)S(1)}, f32[8,136,128]{2,1,0:T(8,128)S(1)}, u32[]{:S(2)}, u32[]{:S(2)}) collective-permute-start(f32[8,136,128]{2,1,0:T(8,128)S(1)} %get-tuple-element.32), channel_id=1, source_target_pairs={{0,1},{1,0},{2,3},{3,2},{4,5},{5,4},{6,7},{7,6},{8,9},{9,8},{10,11... | collective-permute-start | bytes 1671176 | tf_op jit(solution)/shard_map/ppermute | solution.py:394
  23.2 6.0 %collective-permute-start.1 = (f32[136,128]{1,0:T(8,128)S(1)}, f32[136,128]{1,0:T(8,128)S(1)}, u32[]{:S(2)}, u32[]{:S(2)}) collective-permute-start(f32[136,128]{1,0:T(8,128)S(1)} %shard_map.104.mine_ref), channel_id=1, source_target_pairs={{0,16},{1,17},{2,18},{3,19},{4,20},{5,21},{6,22},{7,23},{8,24},{9,... | collective-permute-start | bytes 208904 | tf_op jit(solution)/shard_map/ppermute | solution.py:397
  40.2 2.0 %collective-permute-start.2 = (f32[8,136,128]{2,1,0:T(8,128)S(1)}, f32[8,136,128]{2,1,0:T(8,128)S(1)}, u32[]{:S(2)}, u32[]{:S(2)}) collective-permute-start(f32[8,136,128]{2,1,0:T(8,128)S(1)} %all_to_all.21.means_ref), channel_id=1, source_target_pairs={{0,1},{1,0},{2,3},{3,2},{4,5},{5,4},{6,7},{7,6},{8,9},{9,8},{10,11... | collective-permute-start | bytes 1671176 | tf_op jit(solution)/shard_map/ppermute | solution.py:394
  40.2 2.0 %copy-start = (s32[2048,1]{0,1:T(1,128)S(1)}, s32[2048,1]{0,1:T(1,128)}, u32[]{:S(2)}) copy-start(s32[2048,1]{0,1:T(1,128)} %param.12) | copy-start | bytes 24580
  40.2 2.0 %copy-start.1 = (s32[2048]{0:T(1024)S(1)}, s32[2048]{0:T(1024)}, u32[]{:S(2)}) copy-start(s32[2048]{0:T(1024)} %param.13) | copy-start | bytes 24580
  44.2 1.5 %collective-permute-start.3 = (f32[8,40,128]{2,1,0:T(8,128)S(1)}, f32[8,40,128]{2,1,0:T(8,128)S(1)}, u32[]{:S(2)}, u32[]{:S(2)}) collective-permute-start(f32[8,40,128]{2,1,0:T(8,128)S(1)} %get-tuple-element.39), channel_id=1, source_target_pairs={{0,1},{1,0},{2,3},{3,2},{4,5},{5,4},{6,7},{7,6},{8,9},{9,8},{10,11... | collective-permute-start | bytes 491528 | tf_op jit(solution)/shard_map/ppermute | solution.py:394
  55.0 4.8 %collective-permute-start.4 = (f32[56,128]{1,0:T(8,128)S(1)}, f32[56,128]{1,0:T(8,128)S(1)}, u32[]{:S(2)}, u32[]{:S(2)}) collective-permute-start(f32[56,128]{1,0:T(8,128)S(1)} %shard_map.109.mine_ref), channel_id=1, source_target_pairs={{0,16},{1,17},{2,18},{3,19},{4,20},{5,21},{6,22},{7,23},{8,24},{9,... | collective-permute-start | bytes 86024 | tf_op jit(solution)/shard_map/ppermute | solution.py:397
  68.6 1.4 %collective-permute-start.5 = (f32[8,40,128]{2,1,0:T(8,128)S(1)}, f32[8,40,128]{2,1,0:T(8,128)S(1)}, u32[]{:S(2)}, u32[]{:S(2)}) collective-permute-start(f32[8,40,128]{2,1,0:T(8,128)S(1)} %all_to_all.23.means_ref), channel_id=1, source_target_pairs={{0,1},{1,0},{2,3},{3,2},{4,5},{5,4},{6,7},{7,6},{8,9},{9,8},{10,11... | collective-permute-start | bytes 491528 | tf_op jit(solution)/shard_map/ppermute | solution.py:394
  68.6 1.4 %collective-permute-start.6 = (f32[24,128]{1,0:T(8,128)S(1)}, f32[24,128]{1,0:T(8,128)S(1)}, u32[]{:S(2)}, u32[]{:S(2)}) collective-permute-start(f32[24,128]{1,0:T(8,128)S(1)} %get-tuple-element.45.mine_ref), channel_id=1, source_target_pairs={{0,1},{1,0},{2,3},{3,2},{4,5},{5,4},{6,7},{7,6},{8,9},{9,8},{10,11... | collective-permute-start | bytes 36872 | tf_op jit(solution)/shard_map/ppermute | solution.py:394

commit v7 on v6

--- a/solution.py
+++ b/solution.py
@@ -158,16 +158,13 @@
     denominator = jnp.where(sum_w > 0.0, sum_w, 1.0)
     mean_z = sum_z / denominator
     table = jnp.concatenate([onehot(mask) for mask in masks], axis=1)
-    sum_x = jnp.zeros((FIRM_DEV, 2 * LANES), F32)
     for i, a in enumerate(starts):
         copies[len(small) + i].wait()
-        span = slice(a * LANES, (a + chunk) * LANES)
         if a == 0:
             offset = jnp.sum(x_ref[row_block(0), :], axis=0, keepdims=True) * (1.0 / LANES)
         for b in range(a, a + chunk):
             pairs_ref[row_block(b), :] = pair((x_ref[row_block(b), :] - offset) * weight_t[:, b : b + 1])
-        sum_x += dot(table[:, span], pairs_ref[span, :])
-    mean_x = pair(unpair(sum_x) / denominator)
+    mean_x = pair(unpair(dot(table, pairs_ref[...])) / denominator)
     z1 = []
     for a in range(count):
         if a % group == 0:
@@ -330,7 +327,7 @@
     scale = 1.0 / total_rows
     gram_out[...] = (gram - less[:share, :]) * scale
     rhs = (total[high_rows : high_rows + 1, :] - less[share:, :]) * scale
-    rhs_out[...] = pltpu.roll(rhs, LANES - first, 1)[:, :share]
+    rhs_out[...] = pltpu.roll(rhs, lax.rem(LANES - first, LANES), 1)[:, :share]
     copies.append(pltpu.make_async_copy(gram_out, gram_hbm, sems.at[0]))
     copies.append(pltpu.make_async_copy(rhs_out, rhs_hbm, sems.at[1]))
     for copy in copies[-2:]:

time: 71.8 us -> 71.8 us (level)
  no operation moved by 1% of the time
where the time goes in v7:
time: 71.8 us; the launch traced here: 71.5 us
  blocking collectives  45.1 us (63%)
  Pallas kernels  12.3 us (17%)
  starting transfers between devices  6.64 us (9%)
  waiting for transfers between devices  6.62 us (9%)
    all_to_all x4, blocking collectives, across(): return lax.all_to_all(v, AXIS, 0, 0, axis_index_groups=groups)  45.1 us
    pallas_call x11, Pallas kernels, call(): pl.pallas_call(kernel, out_shape=tuple(outs), in_specs=in_specs or [VMEM]...  12.3 us
    ppermute x2, waiting for transfers between devices, to_half(): return lax.ppermute(v, AXIS, opposite)  5.45 us
    ppermute x2, starting transfers between devices, to_half(): return lax.ppermute(v, AXIS, opposite)  5.41 us
  transfers between devices with their start and end apart: 7, of which 6 were waited for; matrix products, arithmetic and copies ran while one was open for 0% of the time, Pallas kernels for 6%

profile of v7, /device:TPU:0, one launch (start us, length us, event | category | flops | bytes accessed | tf_op | source)
XLA Modules:
  0.0 71.5 jit_solution(1646784252244268890)
XLA Ops:
  0.6 4.1 %shard_map.102 = (f32[2048,128]{1,0:T(8,128)S(1)}, f32[16,128]{1,0:T(8,128)S(1)}, f32[16,128]{1,0:T(8,128)S(1)}, s32[16,128]{1,0:T(8,128)S(1)}, bf16[2048,256]{1...) custom-call(f32[2048,128]{1,0:T(8,128)} %x_hbm.1, f32[16,128]{1,0:T(8,128)} %bitcast.16, f32[16,128]{1,0:T(8,128)} %bitcast.17, ...), custom_call_target="tpu_custom_call" | custom-call | flops 1342177280 | bytes 3760128 | tf_op jit(solution)/shard_map/pallas_call | solution.py:345
  4.7 0.5 collective-permute-start
  5.2 1.4 %shard_map.103 = f32[8,136,128]{2,1,0:T(8,128)S(1)} custom-call(bf16[2048,256]{1,0:T(8,128)(2,1)S(1)} %get-tuple-element.29.pairs_ref, f32[16,128]{1,0:T(8,128)S(1)} %get-tuple-element.28.z1_ref.z_ref, f32[16,128]{1,0:T(8,128)S(1)} %get-tuple-element.30.weight_ref, s32[16,128]{1,0:T(8,128)S(1)} %get-tuple-element.31.dy_ref), custom_call_target="tpu_custom_call" | custom-call | flops 1073741824 | bytes 1630208 | tf_op jit(solution)/shard_map/pallas_call | solution.py:345
  6.7 0.1 collective-permute-done
  6.8 0.1 add.6
  6.9 16.3 %all_to_all.20.in_ref = f32[8,136,128]{2,1,0:T(8,128)S(1)} all-to-all(f32[8,136,128]{2,1,0:T(8,128)S(1)} %add.6), channel_id=1, replica_groups={{0,2,4,6,8,10,12,14},{1,3,5,7,9,11,13,15},{16,18,20,22,24,26,28,30},{17..., dimensions={0} | all-to-all | bytes 1114112 | tf_op jit(solution)/shard_map/all_to_all | solution.py:397
  23.2 2.7 %collective-permute-start.1 = (f32[136,128]{1,0:T(8,128)S(1)}, f32[136,128]{1,0:T(8,128)S(1)}, u32[]{:S(2)}, u32[]{:S(2)}) collective-permute-start(f32[136,128]{1,0:T(8,128)S(1)} %shard_map.104.mine_ref), channel_id=1, source_target_pairs={{0,16},{1,17},{2,18},{3,19},{4,20},{5,21},{6,22},{7,23},{8,24},{9,... | collective-permute-start | bytes 208904 | tf_op jit(solution)/shard_map/ppermute | solution.py:394
  25.9 3.4 %collective-permute-done.1.got_ref = f32[136,128]{1,0:T(8,128)S(1)} collective-permute-done((f32[136,128]{1,0:T(8,128)S(1)}, f32[136,128]{1,0:T(8,128)S(1)}, u32[]{:S(2)}, u32[]{:S(2)}) %collective-permute-start.1) | collective-permute-done | bytes 69664 | tf_op jit(solution)/shard_map/ppermute | solution.py:394
  29.2 0.1 shard_map.105
  29.4 10.9 %all_to_all.21.means_ref = f32[8,136,128]{2,1,0:T(8,128)S(1)} all-to-all(f32[8,136,128]{2,1,0:T(8,128)S(1)} %shard_map.105), channel_id=1, replica_groups={{0,2,4,6,8,10,12,14},{1,3,5,7,9,11,13,15},{16,18,20,22,24,26,28,30},{17..., dimensions={0} | all-to-all | bytes 1114112 | tf_op jit(solution)/shard_map/all_to_all | solution.py:397
  40.3 0.0 collective-permute-start.2
  40.3 0.0 copy-start
  40.3 0.0 copy-start.1
  40.3 1.5 %shard_map.106 = (f32[2048,128]{1,0:T(8,128)S(1)}, f32[16,128]{1,0:T(8,128)S(1)}) custom-call(f32[2048,128]{1,0:T(8,128)S(1)} %get-tuple-element.27.x_ref, f32[16,128]{1,0:T(8,128)S(1)} %get-tuple-element.28.z1_ref.z_ref, f32[8,136,128]{2,1,0:T(8,128)S(1)} %all_to_all.21.means_ref, s32[16,128]{1,0:T(8,128)S(1)} %get-tuple-element.31.dy_ref), custom_call_target="tpu_custom_call" | custom-call | flops 1073741824 | bytes 2678784 | tf_op jit(solution)/shard_map/pallas_call | solution.py:345
  41.8 0.4 collective-permute-done.2.means_ref
  42.2 0.0 copy-done
  42.2 0.0 copy-done.1
  42.2 2.0 %shard_map.107 = (f32[2048,128]{1,0:T(8,128)S(1)}, f32[16,128]{1,0:T(8,128)S(1)}, bf16[2048,256]{1,0:T(8,128)(2,1)S(1)}, f32[8,40,128]{2,1,0:T(8,128)S(1)}) custom-call(f32[2048,128]{1,0:T(8,128)S(1)} %get-tuple-element.33.x_ref, f32[16,128]{1,0:T(8,128)S(1)} %get-tuple-element.34.z_ref, f32[8,136,128]{2,1,0:T(8,128)S(1)} %collective-permute-done.2.means_ref, ...), custom_call_target="tpu_custom_call" | custom-call | flops 1342177280 | bytes 3915776 | tf_op jit(solution)/shard_map/pallas_call | solution.py:345
  44.2 0.2 collective-permute-start.3
  44.4 0.9 %shard_map.108 = (f32[8,40,128]{2,1,0:T(8,128)S(1)}, f32[8,16,128]{2,1,0:T(8,128)S(1)}) custom-call(f32[2048,128]{1,0:T(8,128)S(1)} %get-tuple-element.35.x2_ref.x_ref, f32[16,128]{1,0:T(8,128)S(1)} %get-tuple-element.36.z2_ref.z_ref, bf16[2048,256]{1,0:T(8,128)(2,1)S(1)} %get-tuple-element.37.weighted_ref, f32[16,128]{1,0:T(8,128)S(1)} %get-tuple-element.30.weight_ref, ...), custom_call_target="tpu_custom_call" | custom-call | flops 536870912 | bytes 2359296 | tf_op jit(solution)/shard_map/pallas_call | solution.py:345
  45.3 0.3 collective-permute-done.3
  45.7 9.3 %all_to_all.22.in_ref = f32[8,56,128]{2,1,0:T(8,128)S(1)} all-to-all(f32[8,56,128]{2,1,0:T(8,128)S(1)} %pad_maximum_fusion), channel_id=1, replica_groups={{0,2,4,6,8,10,12,14},{1,3,5,7,9,11,13,15},{16,18,20,22,24,26,28,30},{17..., dimensions={0} | all-to-all | bytes 458752 | tf_op jit(solution)/shard_map/all_to_all | solution.py:397
  55.0 2.8 %collective-permute-start.4 = (f32[56,128]{1,0:T(8,128)S(1)}, f32[56,128]{1,0:T(8,128)S(1)}, u32[]{:S(2)}, u32[]{:S(2)}) collective-permute-start(f32[56,128]{1,0:T(8,128)S(1)} %shard_map.109.mine_ref), channel_id=1, source_target_pairs={{0,16},{1,17},{2,18},{3,19},{4,20},{5,21},{6,22},{7,23},{8,24},{9,... | collective-permute-start | bytes 86024 | tf_op jit(solution)/shard_map/ppermute | solution.py:394
  57.8 2.1 %collective-permute-done.4.got_ref = f32[56,128]{1,0:T(8,128)S(1)} collective-permute-done((f32[56,128]{1,0:T(8,128)S(1)}, f32[56,128]{1,0:T(8,128)S(1)}, u32[]{:S(2)}, u32[]{:S(2)}) %collective-permute-start.4) | collective-permute-done | bytes 28704 | tf_op jit(solution)/shard_map/ppermute | solution.py:394
  59.9 0.1 shard_map.110
  60.0 8.6 %all_to_all.23.means_ref = f32[8,40,128]{2,1,0:T(8,128)S(1)} all-to-all(f32[8,40,128]{2,1,0:T(8,128)S(1)} %get-tuple-element.41), channel_id=1, replica_groups={{0,2,4,6,8,10,12,14},{1,3,5,7,9,11,13,15},{16,18,20,22,24,26,28,30},{17..., dimensions={0} | all-to-all | bytes 327680 | tf_op jit(solution)/shard_map/all_to_all | solution.py:397
  68.6 0.0 collective-permute-start.5
  68.6 0.5 collective-permute-start.6
  69.1 0.6 shard_map.111
  69.7 0.3 collective-permute-done.6.got_ref
  70.0 0.0 collective-permute-done.5.means_ref
  70.0 1.4 %shard_map.112 = (f32[2048,128]{1,0:T(8,128)}, f32[16,128]{1,0:T(8,128)}, f32[4,128]{1,0:T(4,128)}, f32[1,4]{1,0:T(1,128)}) custom-call(f32[2048,128]{1,0:T(8,128)S(1)} %get-tuple-element.42.x_ref, f32[16,128]{1,0:T(8,128)S(1)} %get-tuple-element.43.z_ref, f32[8,40,128]{2,1,0:T(8,128)S(1)} %collective-permute-done.5.means_ref, ...), custom_call_target="tpu_custom_call" | custom-call | flops 268435456 | bytes 2324496 | tf_op jit(solution)/shard_map/pallas_call | solution.py:345
  (4 shorter events, 0.1 us)
Async XLA Ops:
  4.7 2.1 %collective-permute-start = (f32[8,136,128]{2,1,0:T(8,128)S(1)}, f32[8,136,128]{2,1,0:T(8,128)S(1)}, u32[]{:S(2)}, u32[]{:S(2)}) collective-permute-start(f32[8,136,128]{2,1,0:T(8,128)S(1)} %get-tuple-element.32), channel_id=1, source_target_pairs={{0,1},{1,0},{2,3},{3,2},{4,5},{5,4},{6,7},{7,6},{8,9},{9,8},{10,11... | collective-permute-start | bytes 1671176 | tf_op jit(solution)/shard_map/ppermute | solution.py:391
  23.2 6.0 %collective-permute-start.1 = (f32[136,128]{1,0:T(8,128)S(1)}, f32[136,128]{1,0:T(8,128)S(1)}, u32[]{:S(2)}, u32[]{:S(2)}) collective-permute-start(f32[136,128]{1,0:T(8,128)S(1)} %shard_map.104.mine_ref), channel_id=1, source_target_pairs={{0,16},{1,17},{2,18},{3,19},{4,20},{5,21},{6,22},{7,23},{8,24},{9,... | collective-permute-start | bytes 208904 | tf_op jit(solution)/shard_map/ppermute | solution.py:394
  40.3 2.0 %collective-permute-start.2 = (f32[8,136,128]{2,1,0:T(8,128)S(1)}, f32[8,136,128]{2,1,0:T(8,128)S(1)}, u32[]{:S(2)}, u32[]{:S(2)}) collective-permute-start(f32[8,136,128]{2,1,0:T(8,128)S(1)} %all_to_all.21.means_ref), channel_id=1, source_target_pairs={{0,1},{1,0},{2,3},{3,2},{4,5},{5,4},{6,7},{7,6},{8,9},{9,8},{10,11... | collective-permute-start | bytes 1671176 | tf_op jit(solution)/shard_map/ppermute | solution.py:391
  40.3 2.0 %copy-start = (s32[2048,1]{0,1:T(1,128)S(1)}, s32[2048,1]{0,1:T(1,128)}, u32[]{:S(2)}) copy-start(s32[2048,1]{0,1:T(1,128)} %param.12) | copy-start | bytes 24580
  40.3 2.0 %copy-start.1 = (s32[2048]{0:T(1024)S(1)}, s32[2048]{0:T(1024)}, u32[]{:S(2)}) copy-start(s32[2048]{0:T(1024)} %param.13) | copy-start | bytes 24580
  44.2 1.5 %collective-permute-start.3 = (f32[8,40,128]{2,1,0:T(8,128)S(1)}, f32[8,40,128]{2,1,0:T(8,128)S(1)}, u32[]{:S(2)}, u32[]{:S(2)}) collective-permute-start(f32[8,40,128]{2,1,0:T(8,128)S(1)} %get-tuple-element.39), channel_id=1, source_target_pairs={{0,1},{1,0},{2,3},{3,2},{4,5},{5,4},{6,7},{7,6},{8,9},{9,8},{10,11... | collective-permute-start | bytes 491528 | tf_op jit(solution)/shard_map/ppermute | solution.py:391
  55.0 4.8 %collective-permute-start.4 = (f32[56,128]{1,0:T(8,128)S(1)}, f32[56,128]{1,0:T(8,128)S(1)}, u32[]{:S(2)}, u32[]{:S(2)}) collective-permute-start(f32[56,128]{1,0:T(8,128)S(1)} %shard_map.109.mine_ref), channel_id=1, source_target_pairs={{0,16},{1,17},{2,18},{3,19},{4,20},{5,21},{6,22},{7,23},{8,24},{9,... | collective-permute-start | bytes 86024 | tf_op jit(solution)/shard_map/ppermute | solution.py:394
  68.6 1.4 %collective-permute-start.5 = (f32[8,40,128]{2,1,0:T(8,128)S(1)}, f32[8,40,128]{2,1,0:T(8,128)S(1)}, u32[]{:S(2)}, u32[]{:S(2)}) collective-permute-start(f32[8,40,128]{2,1,0:T(8,128)S(1)} %all_to_all.23.means_ref), channel_id=1, source_target_pairs={{0,1},{1,0},{2,3},{3,2},{4,5},{5,4},{6,7},{7,6},{8,9},{9,8},{10,11... | collective-permute-start | bytes 491528 | tf_op jit(solution)/shard_map/ppermute | solution.py:391
  68.6 1.4 %collective-permute-start.6 = (f32[24,128]{1,0:T(8,128)S(1)}, f32[24,128]{1,0:T(8,128)S(1)}, u32[]{:S(2)}, u32[]{:S(2)}) collective-permute-start(f32[24,128]{1,0:T(8,128)S(1)} %get-tuple-element.45.mine_ref), channel_id=1, source_target_pairs={{0,1},{1,0},{2,3},{3,2},{4,5},{5,4},{6,7},{7,6},{8,9},{9,8},{10,11... | collective-permute-start | bytes 36872 | tf_op jit(solution)/shard_map/ppermute | solution.py:391

commit v8 on v7

--- a/solution.py
+++ b/solution.py
@@ -23,6 +23,11 @@
 
 def core_index():
     return lax.rem(lax.axis_index(AXIS), 2)
+
+
+def effect_half(blocks):
+    me = lax.axis_index(AXIS)
+    return lax.rem(me + lax.div(me, 2 * blocks), 2)
 
 
 def iota(shape, dim):
@@ -236,7 +241,7 @@
     z2_ref[...] = z2
     effect = owner_ref[...] * PD_DEV + local_ref[...]
     scatter_half(
-        effect, weight, z2, weighted_ref, (1 - core_index()) * (blocks * pd_width), blocks, pd_width, send_ref
+        effect, weight, z2, weighted_ref, (1 - effect_half(blocks)) * (blocks * pd_width), blocks, pd_width, send_ref
     )
 
 
@@ -249,7 +254,7 @@
     lines = z2.shape[0]
     effect = owner_ref[...] * PD_DEV + local_ref[...]
     scatter_half(
-        effect, weight, z2, weighted_ref, core_index() * (blocks * pd_width), blocks, pd_width, keep_ref
+        effect, weight, z2, weighted_ref, effect_half(blocks) * (blocks * pd_width), blocks, pd_width, keep_ref
     )
     for a in range(lines):
         plain_ref[row_block(a), :] = pair(x2_ref[row_block(a), :])
@@ -291,7 +296,7 @@
     def emit(a, picked):
         x_out[row_block(a), :] = x_ref[row_block(a), :] - picked
 
-    z_out[...] = gather_half(effect, means_ref, core_index() * (blocks * width), blocks, width, z_ref[...], emit)
+    z_out[...] = gather_half(effect, means_ref, effect_half(blocks) * (blocks * width), blocks, width, z_ref[...], emit)
     less_ref[: share + 1, :] = gram_less(means_ref, blocks, width, lax.axis_index(AXIS) * share, share)
 
 
@@ -314,7 +319,7 @@
             copies.append(pltpu.make_async_copy(x_out.at[span, :], x_hbm.at[span, :], sems.at[3 + a // chunk]))
             copies[-1].start()
 
-    z_out[...] = gather_half(effect, means_ref, (1 - core) * (blocks * width), blocks, width, z_ref[...], emit)
+    z_out[...] = gather_half(effect, means_ref, (1 - effect_half(blocks)) * (blocks * width), blocks, width, z_ref[...], emit)
     copies.append(pltpu.make_async_copy(z_out, z_hbm, sems.at[2]))
     copies[-1].start()
     less = gram_less(means_ref, blocks, width, first, share) + less_ref[: share + 1, :]
@@ -382,6 +387,7 @@
     ]
     partner = [(i, i ^ 1) for i in range(devices)]
     opposite = [(i, (i + devices // 2) % devices) for i in range(devices)]
+    crossed = [(i, (i + devices // 2) % devices ^ 1) for i in range(devices)]
     outcome, predictor, firm, dy, owner, local = (
         v.reshape(lines, LANES) for v in (outcome, predictor, firm_id, dy_id, pd_owner, pd_local)
     )
@@ -390,8 +396,8 @@
     def to_core(v):
         return lax.ppermute(v, AXIS, partner)
 
-    def to_half(v):
-        return lax.ppermute(v, AXIS, opposite)
+    def to_half(v, pairs):
+        return lax.ppermute(v, AXIS, pairs)
 
     def across(v):
         return lax.all_to_all(v, AXIS, 0, 0, axis_index_groups=groups)
@@ -431,7 +437,7 @@
     )
     mine = total_of(across(keep + got))
     (means,) = call(
-        functools.partial(means_kernel, dy_width), (shaped(blocks, dy_high, LANES),), (mine, to_half(mine))
+        functools.partial(means_kernel, dy_width), (shaped(blocks, dy_high, LANES),), (mine, to_half(mine, opposite))
     )
     means = across(means)
     other = to_core(means)
@@ -464,7 +470,7 @@
     means, gram = call(
         functools.partial(means_kernel, pd_width),
         (shaped(blocks, pd_high, LANES), shaped(gram_high + TILE, LANES)),
-        (mine, to_half(mine)),
+        (mine, to_half(mine, crossed)),
     )
     got = to_core(gram)
     means = across(means)

time: 71.8 us -> 71.8 us (level)
  starting transfers between devices: 6.64 us -> 5.14 us
  waiting for transfers between devices: 6.62 us -> 7.53 us
    ppermute x2, starting transfers between devices: 5.41 us -> 3.91 us  [to_half(): return lax.ppermute(v, AXIS, pairs)]
    ppermute x2, waiting for transfers between devices: 5.45 us -> 6.38 us  [to_half(): return lax.ppermute(v, AXIS, pairs)]
where the time goes in v8:
time: 71.8 us; the launch traced here: 71.5 us
  blocking collectives  45.7 us (64%)
  Pallas kernels  12.3 us (17%)
  waiting for transfers between devices  7.53 us (10%)
  starting transfers between devices  5.14 us (7%)
  between operations  0.72 us (1%)
    all_to_all x4, blocking collectives, across(): return lax.all_to_all(v, AXIS, 0, 0, axis_index_groups=groups)  45.7 us
    pallas_call x11, Pallas kernels, call(): pl.pallas_call(kernel, out_shape=tuple(outs), in_specs=in_specs or [VMEM]...  12.3 us
    ppermute x2, waiting for transfers between devices, to_half(): return lax.ppermute(v, AXIS, pairs)  6.38 us
    ppermute x2, starting transfers between devices, to_half(): return lax.ppermute(v, AXIS, pairs)  3.91 us
  transfers between devices with their start and end apart: 7, of which 6 were waited for; matrix products, arithmetic and copies ran while one was open for 0% of the time, Pallas kernels for 6%

profile of v8, /device:TPU:0, one launch (start us, length us, event | category | flops | bytes accessed | tf_op | source)
XLA Modules:
  0.0 71.5 jit_solution(11893331589182104689)
XLA Ops:
  0.6 4.1 %shard_map.102 = (f32[2048,128]{1,0:T(8,128)S(1)}, f32[16,128]{1,0:T(8,128)S(1)}, f32[16,128]{1,0:T(8,128)S(1)}, s32[16,128]{1,0:T(8,128)S(1)}, bf16[2048,256]{1...) custom-call(f32[2048,128]{1,0:T(8,128)} %x_hbm.1, f32[16,128]{1,0:T(8,128)} %bitcast.16, f32[16,128]{1,0:T(8,128)} %bitcast.17, ...), custom_call_target="tpu_custom_call" | custom-call | flops 1342177280 | bytes 3760128 | tf_op jit(solution)/shard_map/pallas_call | solution.py:350
  4.7 0.5 collective-permute-start
  5.2 1.4 %shard_map.103 = f32[8,136,128]{2,1,0:T(8,128)S(1)} custom-call(bf16[2048,256]{1,0:T(8,128)(2,1)S(1)} %get-tuple-element.29.pairs_ref, f32[16,128]{1,0:T(8,128)S(1)} %get-tuple-element.28.z1_ref.z_ref, f32[16,128]{1,0:T(8,128)S(1)} %get-tuple-element.30.weight_ref, s32[16,128]{1,0:T(8,128)S(1)} %get-tuple-element.31.dy_ref), custom_call_target="tpu_custom_call" | custom-call | flops 1073741824 | bytes 1630208 | tf_op jit(solution)/shard_map/pallas_call | solution.py:350
  6.7 0.1 collective-permute-done
  6.8 0.1 add.6
  6.9 16.3 %all_to_all.20.in_ref = f32[8,136,128]{2,1,0:T(8,128)S(1)} all-to-all(f32[8,136,128]{2,1,0:T(8,128)S(1)} %add.6), channel_id=1, replica_groups={{0,2,4,6,8,10,12,14},{1,3,5,7,9,11,13,15},{16,18,20,22,24,26,28,30},{17..., dimensions={0} | all-to-all | bytes 1114112 | tf_op jit(solution)/shard_map/all_to_all | solution.py:403
  23.2 2.7 %collective-permute-start.1 = (f32[136,128]{1,0:T(8,128)S(1)}, f32[136,128]{1,0:T(8,128)S(1)}, u32[]{:S(2)}, u32[]{:S(2)}) collective-permute-start(f32[136,128]{1,0:T(8,128)S(1)} %shard_map.104.mine_ref), channel_id=1, source_target_pairs={{0,16},{1,17},{2,18},{3,19},{4,20},{5,21},{6,22},{7,23},{8,24},{9,... | collective-permute-start | bytes 208904 | tf_op jit(solution)/shard_map/ppermute | solution.py:400
  25.9 3.4 %collective-permute-done.1.got_ref = f32[136,128]{1,0:T(8,128)S(1)} collective-permute-done((f32[136,128]{1,0:T(8,128)S(1)}, f32[136,128]{1,0:T(8,128)S(1)}, u32[]{:S(2)}, u32[]{:S(2)}) %collective-permute-start.1) | collective-permute-done | bytes 69664 | tf_op jit(solution)/shard_map/ppermute | solution.py:400
  29.2 0.1 shard_map.105
  29.4 10.9 %all_to_all.21.means_ref = f32[8,136,128]{2,1,0:T(8,128)S(1)} all-to-all(f32[8,136,128]{2,1,0:T(8,128)S(1)} %shard_map.105), channel_id=1, replica_groups={{0,2,4,6,8,10,12,14},{1,3,5,7,9,11,13,15},{16,18,20,22,24,26,28,30},{17..., dimensions={0} | all-to-all | bytes 1114112 | tf_op jit(solution)/shard_map/all_to_all | solution.py:403
  40.3 0.0 collective-permute-start.2
  40.3 0.0 copy-start
  40.3 0.0 copy-start.1
  40.3 1.5 %shard_map.106 = (f32[2048,128]{1,0:T(8,128)S(1)}, f32[16,128]{1,0:T(8,128)S(1)}) custom-call(f32[2048,128]{1,0:T(8,128)S(1)} %get-tuple-element.27.x_ref, f32[16,128]{1,0:T(8,128)S(1)} %get-tuple-element.28.z1_ref.z_ref, f32[8,136,128]{2,1,0:T(8,128)S(1)} %all_to_all.21.means_ref, s32[16,128]{1,0:T(8,128)S(1)} %get-tuple-element.31.dy_ref), custom_call_target="tpu_custom_call" | custom-call | flops 1073741824 | bytes 2678784 | tf_op jit(solution)/shard_map/pallas_call | solution.py:350
  41.8 0.4 collective-permute-done.2.means_ref
  42.2 0.0 copy-done
  42.2 0.0 copy-done.1
  42.2 2.0 %shard_map.107 = (f32[2048,128]{1,0:T(8,128)S(1)}, f32[16,128]{1,0:T(8,128)S(1)}, bf16[2048,256]{1,0:T(8,128)(2,1)S(1)}, f32[8,40,128]{2,1,0:T(8,128)S(1)}) custom-call(f32[2048,128]{1,0:T(8,128)S(1)} %get-tuple-element.33.x_ref, f32[16,128]{1,0:T(8,128)S(1)} %get-tuple-element.34.z_ref, f32[8,136,128]{2,1,0:T(8,128)S(1)} %collective-permute-done.2.means_ref, ...), custom_call_target="tpu_custom_call" | custom-call | flops 1342177280 | bytes 3915776 | tf_op jit(solution)/shard_map/pallas_call | solution.py:350
  44.2 0.2 collective-permute-start.3
  44.4 0.9 %shard_map.108 = (f32[8,40,128]{2,1,0:T(8,128)S(1)}, f32[8,16,128]{2,1,0:T(8,128)S(1)}) custom-call(f32[2048,128]{1,0:T(8,128)S(1)} %get-tuple-element.35.x2_ref.x_ref, f32[16,128]{1,0:T(8,128)S(1)} %get-tuple-element.36.z2_ref.z_ref, bf16[2048,256]{1,0:T(8,128)(2,1)S(1)} %get-tuple-element.37.weighted_ref, f32[16,128]{1,0:T(8,128)S(1)} %get-tuple-element.30.weight_ref, ...), custom_call_target="tpu_custom_call" | custom-call | flops 536870912 | bytes 2359296 | tf_op jit(solution)/shard_map/pallas_call | solution.py:350
  45.3 0.3 collective-permute-done.3
  45.7 9.3 %all_to_all.22.in_ref = f32[8,56,128]{2,1,0:T(8,128)S(1)} all-to-all(f32[8,56,128]{2,1,0:T(8,128)S(1)} %pad_maximum_fusion), channel_id=1, replica_groups={{0,2,4,6,8,10,12,14},{1,3,5,7,9,11,13,15},{16,18,20,22,24,26,28,30},{17..., dimensions={0} | all-to-all | bytes 458752 | tf_op jit(solution)/shard_map/all_to_all | solution.py:403
  55.0 1.3 %collective-permute-start.4 = (f32[56,128]{1,0:T(8,128)S(1)}, f32[56,128]{1,0:T(8,128)S(1)}, u32[]{:S(2)}, u32[]{:S(2)}) collective-permute-start(f32[56,128]{1,0:T(8,128)S(1)} %shard_map.109.mine_ref), channel_id=1, source_target_pairs={{0,17},{1,16},{2,19},{3,18},{4,21},{5,20},{6,23},{7,22},{8,25},{9,... | collective-permute-start | bytes 86024 | tf_op jit(solution)/shard_map/ppermute | solution.py:400
  56.3 3.0 %collective-permute-done.4.got_ref = f32[56,128]{1,0:T(8,128)S(1)} collective-permute-done((f32[56,128]{1,0:T(8,128)S(1)}, f32[56,128]{1,0:T(8,128)S(1)}, u32[]{:S(2)}, u32[]{:S(2)}) %collective-permute-start.4) | collective-permute-done | bytes 28704 | tf_op jit(solution)/shard_map/ppermute | solution.py:400
  59.3 0.1 shard_map.110
  59.4 9.3 %all_to_all.23.means_ref = f32[8,40,128]{2,1,0:T(8,128)S(1)} all-to-all(f32[8,40,128]{2,1,0:T(8,128)S(1)} %get-tuple-element.41), channel_id=1, replica_groups={{0,2,4,6,8,10,12,14},{1,3,5,7,9,11,13,15},{16,18,20,22,24,26,28,30},{17..., dimensions={0} | all-to-all | bytes 327680 | tf_op jit(solution)/shard_map/all_to_all | solution.py:403
  68.6 0.0 collective-permute-start.5
  68.6 0.5 collective-permute-start.6
  69.2 0.6 shard_map.111
  69.8 0.3 collective-permute-done.6.got_ref
  70.1 0.0 collective-permute-done.5.means_ref
  70.1 1.4 %shard_map.112 = (f32[2048,128]{1,0:T(8,128)}, f32[16,128]{1,0:T(8,128)}, f32[4,128]{1,0:T(4,128)}, f32[1,4]{1,0:T(1,128)}) custom-call(f32[2048,128]{1,0:T(8,128)S(1)} %get-tuple-element.42.x_ref, f32[16,128]{1,0:T(8,128)S(1)} %get-tuple-element.43.z_ref, f32[8,40,128]{2,1,0:T(8,128)S(1)} %collective-permute-done.5.means_ref, ...), custom_call_target="tpu_custom_call" | custom-call | flops 268435456 | bytes 2324496 | tf_op jit(solution)/shard_map/pallas_call | solution.py:350
  (4 shorter events, 0.1 us)
Async XLA Ops:
  4.7 2.1 %collective-permute-start = (f32[8,136,128]{2,1,0:T(8,128)S(1)}, f32[8,136,128]{2,1,0:T(8,128)S(1)}, u32[]{:S(2)}, u32[]{:S(2)}) collective-permute-start(f32[8,136,128]{2,1,0:T(8,128)S(1)} %get-tuple-element.32), channel_id=1, source_target_pairs={{0,1},{1,0},{2,3},{3,2},{4,5},{5,4},{6,7},{7,6},{8,9},{9,8},{10,11... | collective-permute-start | bytes 1671176 | tf_op jit(solution)/shard_map/ppermute | solution.py:397
  23.2 6.0 %collective-permute-start.1 = (f32[136,128]{1,0:T(8,128)S(1)}, f32[136,128]{1,0:T(8,128)S(1)}, u32[]{:S(2)}, u32[]{:S(2)}) collective-permute-start(f32[136,128]{1,0:T(8,128)S(1)} %shard_map.104.mine_ref), channel_id=1, source_target_pairs={{0,16},{1,17},{2,18},{3,19},{4,20},{5,21},{6,22},{7,23},{8,24},{9,... | collective-permute-start | bytes 208904 | tf_op jit(solution)/shard_map/ppermute | solution.py:400
  40.3 2.0 %collective-permute-start.2 = (f32[8,136,128]{2,1,0:T(8,128)S(1)}, f32[8,136,128]{2,1,0:T(8,128)S(1)}, u32[]{:S(2)}, u32[]{:S(2)}) collective-permute-start(f32[8,136,128]{2,1,0:T(8,128)S(1)} %all_to_all.21.means_ref), channel_id=1, source_target_pairs={{0,1},{1,0},{2,3},{3,2},{4,5},{5,4},{6,7},{7,6},{8,9},{9,8},{10,11... | collective-permute-start | bytes 1671176 | tf_op jit(solution)/shard_map/ppermute | solution.py:397
  40.3 2.0 %copy-start = (s32[2048,1]{0,1:T(1,128)S(1)}, s32[2048,1]{0,1:T(1,128)}, u32[]{:S(2)}) copy-start(s32[2048,1]{0,1:T(1,128)} %param.12) | copy-start | bytes 24580
  40.3 2.0 %copy-start.1 = (s32[2048]{0:T(1024)S(1)}, s32[2048]{0:T(1024)}, u32[]{:S(2)}) copy-start(s32[2048]{0:T(1024)} %param.13) | copy-start | bytes 24580
  44.2 1.5 %collective-permute-start.3 = (f32[8,40,128]{2,1,0:T(8,128)S(1)}, f32[8,40,128]{2,1,0:T(8,128)S(1)}, u32[]{:S(2)}, u32[]{:S(2)}) collective-permute-start(f32[8,40,128]{2,1,0:T(8,128)S(1)} %get-tuple-element.39), channel_id=1, source_target_pairs={{0,1},{1,0},{2,3},{3,2},{4,5},{5,4},{6,7},{7,6},{8,9},{9,8},{10,11... | collective-permute-start | bytes 491528 | tf_op jit(solution)/shard_map/ppermute | solution.py:397
  55.0 4.3 %collective-permute-start.4 = (f32[56,128]{1,0:T(8,128)S(1)}, f32[56,128]{1,0:T(8,128)S(1)}, u32[]{:S(2)}, u32[]{:S(2)}) collective-permute-start(f32[56,128]{1,0:T(8,128)S(1)} %shard_map.109.mine_ref), channel_id=1, source_target_pairs={{0,17},{1,16},{2,19},{3,18},{4,21},{5,20},{6,23},{7,22},{8,25},{9,... | collective-permute-start | bytes 86024 | tf_op jit(solution)/shard_map/ppermute | solution.py:400
  68.6 1.4 %collective-permute-start.5 = (f32[8,40,128]{2,1,0:T(8,128)S(1)}, f32[8,40,128]{2,1,0:T(8,128)S(1)}, u32[]{:S(2)}, u32[]{:S(2)}) collective-permute-start(f32[8,40,128]{2,1,0:T(8,128)S(1)} %all_to_all.23.means_ref), channel_id=1, source_target_pairs={{0,1},{1,0},{2,3},{3,2},{4,5},{5,4},{6,7},{7,6},{8,9},{9,8},{10,11... | collective-permute-start | bytes 491528 | tf_op jit(solution)/shard_map/ppermute | solution.py:397
  68.6 1.4 %collective-permute-start.6 = (f32[24,128]{1,0:T(8,128)S(1)}, f32[24,128]{1,0:T(8,128)S(1)}, u32[]{:S(2)}, u32[]{:S(2)}) collective-permute-start(f32[24,128]{1,0:T(8,128)S(1)} %get-tuple-element.45.mine_ref), channel_id=1, source_target_pairs={{0,1},{1,0},{2,3},{3,2},{4,5},{5,4},{6,7},{7,6},{8,9},{9,8},{10,11... | collective-permute-start | bytes 36872 | tf_op jit(solution)/shard_map/ppermute | solution.py:397

commit v9 on v8

--- a/solution.py
+++ b/solution.py
@@ -197,7 +197,7 @@
     out_ref[...] = total
 
 
-def means_kernel(width, mine_ref, got_ref, out_ref, *rest_ref):
+def means_kernel(width, share, mine_ref, got_ref, out_ref, *rest_ref):
     total = mine_ref[...] + got_ref[...]
     line_w = total[width : width + 1, :]
     line_z = total[width + 1 : width + 2, :]
@@ -207,13 +207,20 @@
     mean_z = line_z / jnp.where(line_w > 0.0, line_w, 1.0)
     height = out_ref.shape[1]
     rest = jnp.zeros((height - width - 2, LANES), F32)
+    if rest_ref:
+        core, high = core_index(), lax.div(lax.axis_index(AXIS), 2 * out_ref.shape[0])
+        own = jnp.zeros((share, LANES), F32)
+        other = jnp.zeros((share, LANES), F32)
+        for place in range(4):
+            rows = total[height + place * share : height + (place + 1) * share, :]
+            own = jnp.where((high == place // 2) & (core == place % 2), rows, own)
+            other = jnp.where((high == place // 2) & (core != place % 2), rows, other)
+        rhs = total[width + 2 : width + 3, :]
+        rest_ref[0][: share + 1, :] = jnp.concatenate([own, rhs], axis=0)
+        rest = jnp.concatenate([other, rhs, rest[share + 1 :, :]], axis=0)
     result = jnp.concatenate([mean_x, line_w, mean_z, rest], axis=0)
     for j in range(out_ref.shape[0]):
         out_ref[j] = result
-    if rest_ref:
-        gram = total[height:, :]
-        rest_ref[0][: gram.shape[0], :] = gram
-        rest_ref[0][gram.shape[0] :, :] = total[width + 2 : width + 2 + TILE, :]
 
 
 def gather_kernel(blocks, width, x_ref, z_ref, means_ref, dy_ref, x_out, z_out):
@@ -301,11 +308,10 @@
 
 
 def last_kernel(
-    blocks, width, share, total_rows, x_ref, z_ref, means_ref, less_ref, mine_ref, got_ref, owner_ref, local_ref,
+    blocks, width, share, total_rows, x_ref, z_ref, means_ref, less_ref, mine_ref, owner_ref, local_ref,
     x_hbm, z_hbm, gram_hbm, rhs_hbm, x_out, z_out, gram_out, rhs_out, sems,
 ):
     me = lax.axis_index(AXIS)
-    core, high = core_index(), lax.div(me, 2 * blocks)
     first = me * share
     copies = []
     effect = owner_ref[...] * PD_DEV + local_ref[...]
@@ -323,15 +329,12 @@
     copies.append(pltpu.make_async_copy(z_out, z_hbm, sems.at[2]))
     copies[-1].start()
     less = gram_less(means_ref, blocks, width, first, share) + less_ref[: share + 1, :]
-    total = mine_ref[...] + got_ref[...]
-    high_rows = total.shape[0] - TILE
-    gram = jnp.zeros((share, LANES), F32)
-    for place in range(4):
-        here = (high == place // 2) & (core == place % 2)
-        gram = jnp.where(here, total[place * share : (place + 1) * share, :], gram)
+    chip = lax.rem(lax.div(me, 2), blocks)
+    got = means_ref[pl.ds(chip, 1), width + 2 : width + 3 + share, :].reshape(share + 1, LANES)
+    total = mine_ref[: share + 1, :] + got
     scale = 1.0 / total_rows
-    gram_out[...] = (gram - less[:share, :]) * scale
-    rhs = (total[high_rows : high_rows + 1, :] - less[share:, :]) * scale
+    gram_out[...] = (total[:share, :] - less[:share, :]) * scale
+    rhs = (total[share:, :] - less[share:, :]) * scale
     rhs_out[...] = pltpu.roll(rhs, lax.rem(LANES - first, LANES), 1)[:, :share]
     copies.append(pltpu.make_async_copy(gram_out, gram_hbm, sems.at[0]))
     copies.append(pltpu.make_async_copy(rhs_out, rhs_hbm, sems.at[1]))
@@ -377,7 +380,7 @@
     share = width // devices
     total_rows = rows * devices
     dy_width, pd_width = DY // (2 * blocks), devices * PD_DEV // (2 * blocks)
-    dy_high, pd_high = rounded(dy_width + 2), rounded(pd_width + 3)
+    dy_high, pd_high = rounded(dy_width + 2), rounded(pd_width + 3 + share)
     gram_high = rounded(4 * share)
     lines = rows // LANES
     groups = [
@@ -437,7 +440,7 @@
     )
     mine = total_of(across(keep + got))
     (means,) = call(
-        functools.partial(means_kernel, dy_width), (shaped(blocks, dy_high, LANES),), (mine, to_half(mine, opposite))
+        functools.partial(means_kernel, dy_width, share), (shaped(blocks, dy_high, LANES),), (mine, to_half(mine, opposite))
     )
     means = across(means)
     other = to_core(means)
@@ -468,11 +471,10 @@
     )
     mine = total_of(across(jnp.concatenate([keep + got, gram], axis=1)))
     means, gram = call(
-        functools.partial(means_kernel, pd_width),
-        (shaped(blocks, pd_high, LANES), shaped(gram_high + TILE, LANES)),
+        functools.partial(means_kernel, pd_width, share),
+        (shaped(blocks, pd_high, LANES), shaped(rounded(share + 1), LANES)),
         (mine, to_half(mine, crossed)),
     )
-    got = to_core(gram)
     means = across(means)
     other = to_core(means)
     x3, z3, less = call(
@@ -484,7 +486,7 @@
     x3, z3, gram, rhs = call(
         functools.partial(last_kernel, blocks, pd_width, share, total_rows),
         (shaped(rows, width), shaped(lines, LANES), shaped(share, LANES), shaped(1, share)),
-        (x3, z3, other, less, gram, got, owner, local),
+        (x3, z3, other, less, gram, owner, local),
         scratch=(
             pltpu.VMEM((rows, width), F32),
             pltpu.VMEM((lines, LANES), F32),

time: 71.8 us -> 71.8 us (level)
    ppermute x5 -> x4, waiting for transfers between devices: 1.15 us -> 1.64 us  [to_core(): return lax.ppermute(v, AXIS, partner)]
  transfers between devices with their start and end apart: 7 -> 6, of which waited for: 6 -> 6; matrix products, arithmetic and copies ran while one was open for 0% -> 0% of each run, Pallas kernels for 6% -> 6%
where the time goes in v9:
time: 71.8 us; the launch traced here: 71.5 us
  blocking collectives  45.7 us (64%)
  Pallas kernels  12.3 us (17%)
  waiting for transfers between devices  8.02 us (11%)
  starting transfers between devices  4.63 us (6%)
  between operations  0.72 us (1%)
    all_to_all x4, blocking collectives, across(): return lax.all_to_all(v, AXIS, 0, 0, axis_index_groups=groups)  45.7 us
    pallas_call x11, Pallas kernels, call(): pl.pallas_call(kernel, out_shape=tuple(outs), in_specs=in_specs or [VMEM]...  12.3 us
    ppermute x2, waiting for transfers between devices, to_half(): return lax.ppermute(v, AXIS, pairs)  6.38 us
    ppermute x2, starting transfers between devices, to_half(): return lax.ppermute(v, AXIS, pairs)  3.91 us
    ppermute x4, waiting for transfers between devices, to_core(): return lax.ppermute(v, AXIS, partner)  1.64 us
  transfers between devices with their start and end apart: 6, of which 6 were waited for; matrix products, arithmetic and copies ran while one was open for 0% of the time, Pallas kernels for 6%

profile of v9, /device:TPU:0, one launch (start us, length us, event | category | flops | bytes accessed | tf_op | source)
XLA Modules:
  0.0 71.5 jit_solution(3993249704677151587)
XLA Ops:
  0.6 4.1 %shard_map.102 = (f32[2048,128]{1,0:T(8,128)S(1)}, f32[16,128]{1,0:T(8,128)S(1)}, f32[16,128]{1,0:T(8,128)S(1)}, s32[16,128]{1,0:T(8,128)S(1)}, bf16[2048,256]{1...) custom-call(f32[2048,128]{1,0:T(8,128)} %x_hbm.1, f32[16,128]{1,0:T(8,128)} %bitcast.16, f32[16,128]{1,0:T(8,128)} %bitcast.17, ...), custom_call_target="tpu_custom_call" | custom-call | flops 1342177280 | bytes 3760128 | tf_op jit(solution)/shard_map/pallas_call | solution.py:353
  4.7 0.5 collective-permute-start
  5.2 1.4 %shard_map.103 = f32[8,136,128]{2,1,0:T(8,128)S(1)} custom-call(bf16[2048,256]{1,0:T(8,128)(2,1)S(1)} %get-tuple-element.29.pairs_ref, f32[16,128]{1,0:T(8,128)S(1)} %get-tuple-element.28.z1_ref.z_ref, f32[16,128]{1,0:T(8,128)S(1)} %get-tuple-element.30.weight_ref, s32[16,128]{1,0:T(8,128)S(1)} %get-tuple-element.31.dy_ref), custom_call_target="tpu_custom_call" | custom-call | flops 1073741824 | bytes 1630208 | tf_op jit(solution)/shard_map/pallas_call | solution.py:353
  6.7 0.1 collective-permute-done
  6.8 0.1 add.6
  6.9 16.3 %all_to_all.20.in_ref = f32[8,136,128]{2,1,0:T(8,128)S(1)} all-to-all(f32[8,136,128]{2,1,0:T(8,128)S(1)} %add.6), channel_id=1, replica_groups={{0,2,4,6,8,10,12,14},{1,3,5,7,9,11,13,15},{16,18,20,22,24,26,28,30},{17..., dimensions={0} | all-to-all | bytes 1114112 | tf_op jit(solution)/shard_map/all_to_all | solution.py:406
  23.2 2.7 %collective-permute-start.1 = (f32[136,128]{1,0:T(8,128)S(1)}, f32[136,128]{1,0:T(8,128)S(1)}, u32[]{:S(2)}, u32[]{:S(2)}) collective-permute-start(f32[136,128]{1,0:T(8,128)S(1)} %shard_map.104.mine_ref), channel_id=1, source_target_pairs={{0,16},{1,17},{2,18},{3,19},{4,20},{5,21},{6,22},{7,23},{8,24},{9,... | collective-permute-start | bytes 208904 | tf_op jit(solution)/shard_map/ppermute | solution.py:403
  25.9 3.4 %collective-permute-done.1.got_ref = f32[136,128]{1,0:T(8,128)S(1)} collective-permute-done((f32[136,128]{1,0:T(8,128)S(1)}, f32[136,128]{1,0:T(8,128)S(1)}, u32[]{:S(2)}, u32[]{:S(2)}) %collective-permute-start.1) | collective-permute-done | bytes 69664 | tf_op jit(solution)/shard_map/ppermute | solution.py:403
  29.2 0.1 shard_map.105
  29.4 10.9 %all_to_all.21.means_ref = f32[8,136,128]{2,1,0:T(8,128)S(1)} all-to-all(f32[8,136,128]{2,1,0:T(8,128)S(1)} %shard_map.105), channel_id=1, replica_groups={{0,2,4,6,8,10,12,14},{1,3,5,7,9,11,13,15},{16,18,20,22,24,26,28,30},{17..., dimensions={0} | all-to-all | bytes 1114112 | tf_op jit(solution)/shard_map/all_to_all | solution.py:406
  40.3 0.0 collective-permute-start.2
  40.3 0.0 copy-start
  40.3 0.0 copy-start.1
  40.3 1.5 %shard_map.106 = (f32[2048,128]{1,0:T(8,128)S(1)}, f32[16,128]{1,0:T(8,128)S(1)}) custom-call(f32[2048,128]{1,0:T(8,128)S(1)} %get-tuple-element.27.x_ref, f32[16,128]{1,0:T(8,128)S(1)} %get-tuple-element.28.z1_ref.z_ref, f32[8,136,128]{2,1,0:T(8,128)S(1)} %all_to_all.21.means_ref, s32[16,128]{1,0:T(8,128)S(1)} %get-tuple-element.31.dy_ref), custom_call_target="tpu_custom_call" | custom-call | flops 1073741824 | bytes 2678784 | tf_op jit(solution)/shard_map/pallas_call | solution.py:353
  41.8 0.4 collective-permute-done.2.means_ref
  42.2 0.0 copy-done
  42.2 0.0 copy-done.1
  42.2 2.0 %shard_map.107 = (f32[2048,128]{1,0:T(8,128)S(1)}, f32[16,128]{1,0:T(8,128)S(1)}, bf16[2048,256]{1,0:T(8,128)(2,1)S(1)}, f32[8,40,128]{2,1,0:T(8,128)S(1)}) custom-call(f32[2048,128]{1,0:T(8,128)S(1)} %get-tuple-element.33.x_ref, f32[16,128]{1,0:T(8,128)S(1)} %get-tuple-element.34.z_ref, f32[8,136,128]{2,1,0:T(8,128)S(1)} %collective-permute-done.2.means_ref, ...), custom_call_target="tpu_custom_call" | custom-call | flops 1342177280 | bytes 3915776 | tf_op jit(solution)/shard_map/pallas_call | solution.py:353
  44.2 0.2 collective-permute-start.3
  44.4 0.9 %shard_map.108 = (f32[8,40,128]{2,1,0:T(8,128)S(1)}, f32[8,16,128]{2,1,0:T(8,128)S(1)}) custom-call(f32[2048,128]{1,0:T(8,128)S(1)} %get-tuple-element.35.x2_ref.x_ref, f32[16,128]{1,0:T(8,128)S(1)} %get-tuple-element.36.z2_ref.z_ref, bf16[2048,256]{1,0:T(8,128)(2,1)S(1)} %get-tuple-element.37.weighted_ref, f32[16,128]{1,0:T(8,128)S(1)} %get-tuple-element.30.weight_ref, ...), custom_call_target="tpu_custom_call" | custom-call | flops 536870912 | bytes 2359296 | tf_op jit(solution)/shard_map/pallas_call | solution.py:353
  45.3 0.3 collective-permute-done.3
  45.7 9.3 %all_to_all.22.in_ref = f32[8,56,128]{2,1,0:T(8,128)S(1)} all-to-all(f32[8,56,128]{2,1,0:T(8,128)S(1)} %pad_maximum_fusion), channel_id=1, replica_groups={{0,2,4,6,8,10,12,14},{1,3,5,7,9,11,13,15},{16,18,20,22,24,26,28,30},{17..., dimensions={0} | all-to-all | bytes 458752 | tf_op jit(solution)/shard_map/all_to_all | solution.py:406
  55.0 1.3 %collective-permute-start.4 = (f32[56,128]{1,0:T(8,128)S(1)}, f32[56,128]{1,0:T(8,128)S(1)}, u32[]{:S(2)}, u32[]{:S(2)}) collective-permute-start(f32[56,128]{1,0:T(8,128)S(1)} %shard_map.109.mine_ref), channel_id=1, source_target_pairs={{0,17},{1,16},{2,19},{3,18},{4,21},{5,20},{6,23},{7,22},{8,25},{9,... | collective-permute-start | bytes 86024 | tf_op jit(solution)/shard_map/ppermute | solution.py:403
  56.3 3.0 %collective-permute-done.4.got_ref = f32[56,128]{1,0:T(8,128)S(1)} collective-permute-done((f32[56,128]{1,0:T(8,128)S(1)}, f32[56,128]{1,0:T(8,128)S(1)}, u32[]{:S(2)}, u32[]{:S(2)}) %collective-permute-start.4) | collective-permute-done | bytes 28704 | tf_op jit(solution)/shard_map/ppermute | solution.py:403
  59.3 0.1 shard_map.110
  59.4 9.3 %all_to_all.23.means_ref = f32[8,40,128]{2,1,0:T(8,128)S(1)} all-to-all(f32[8,40,128]{2,1,0:T(8,128)S(1)} %get-tuple-element.41), channel_id=1, replica_groups={{0,2,4,6,8,10,12,14},{1,3,5,7,9,11,13,15},{16,18,20,22,24,26,28,30},{17..., dimensions={0} | all-to-all | bytes 327680 | tf_op jit(solution)/shard_map/all_to_all | solution.py:406
  68.6 0.0 collective-permute-start.5
  68.6 0.6 shard_map.111
  69.3 0.7 %collective-permute-done.5.means_ref = f32[8,40,128]{2,1,0:T(8,128)S(1)} collective-permute-done((f32[8,40,128]{2,1,0:T(8,128)S(1)}, f32[8,40,128]{2,1,0:T(8,128)S(1)}, u32[]{:S(2)}, u32[]{:S(2)}) %collective-permute-start.5) | collective-permute-done | bytes 163872 | tf_op jit(solution)/shard_map/ppermute | solution.py:400
  70.0 1.4 %shard_map.112 = (f32[2048,128]{1,0:T(8,128)}, f32[16,128]{1,0:T(8,128)}, f32[4,128]{1,0:T(4,128)}, f32[1,4]{1,0:T(1,128)}) custom-call(f32[2048,128]{1,0:T(8,128)S(1)} %get-tuple-element.42.x_ref, f32[16,128]{1,0:T(8,128)S(1)} %get-tuple-element.43.z_ref, f32[8,40,128]{2,1,0:T(8,128)S(1)} %collective-permute-done.5.means_ref, ...), custom_call_target="tpu_custom_call" | custom-call | flops 268435456 | bytes 2304016 | tf_op jit(solution)/shard_map/pallas_call | solution.py:353
  (4 shorter events, 0.1 us)
Async XLA Ops:
  4.7 2.1 %collective-permute-start = (f32[8,136,128]{2,1,0:T(8,128)S(1)}, f32[8,136,128]{2,1,0:T(8,128)S(1)}, u32[]{:S(2)}, u32[]{:S(2)}) collective-permute-start(f32[8,136,128]{2,1,0:T(8,128)S(1)} %get-tuple-element.32), channel_id=1, source_target_pairs={{0,1},{1,0},{2,3},{3,2},{4,5},{5,4},{6,7},{7,6},{8,9},{9,8},{10,11... | collective-permute-start | bytes 1671176 | tf_op jit(solution)/shard_map/ppermute | solution.py:400
  23.2 6.0 %collective-permute-start.1 = (f32[136,128]{1,0:T(8,128)S(1)}, f32[136,128]{1,0:T(8,128)S(1)}, u32[]{:S(2)}, u32[]{:S(2)}) collective-permute-start(f32[136,128]{1,0:T(8,128)S(1)} %shard_map.104.mine_ref), channel_id=1, source_target_pairs={{0,16},{1,17},{2,18},{3,19},{4,20},{5,21},{6,22},{7,23},{8,24},{9,... | collective-permute-start | bytes 208904 | tf_op jit(solution)/shard_map/ppermute | solution.py:403
  40.3 2.0 %collective-permute-start.2 = (f32[8,136,128]{2,1,0:T(8,128)S(1)}, f32[8,136,128]{2,1,0:T(8,128)S(1)}, u32[]{:S(2)}, u32[]{:S(2)}) collective-permute-start(f32[8,136,128]{2,1,0:T(8,128)S(1)} %all_to_all.21.means_ref), channel_id=1, source_target_pairs={{0,1},{1,0},{2,3},{3,2},{4,5},{5,4},{6,7},{7,6},{8,9},{9,8},{10,11... | collective-permute-start | bytes 1671176 | tf_op jit(solution)/shard_map/ppermute | solution.py:400
  40.3 2.0 %copy-start = (s32[2048,1]{0,1:T(1,128)S(1)}, s32[2048,1]{0,1:T(1,128)}, u32[]{:S(2)}) copy-start(s32[2048,1]{0,1:T(1,128)} %param.12) | copy-start | bytes 24580
  40.3 2.0 %copy-start.1 = (s32[2048]{0:T(1024)S(1)}, s32[2048]{0:T(1024)}, u32[]{:S(2)}) copy-start(s32[2048]{0:T(1024)} %param.13) | copy-start | bytes 24580
  44.2 1.5 %collective-permute-start.3 = (f32[8,40,128]{2,1,0:T(8,128)S(1)}, f32[8,40,128]{2,1,0:T(8,128)S(1)}, u32[]{:S(2)}, u32[]{:S(2)}) collective-permute-start(f32[8,40,128]{2,1,0:T(8,128)S(1)} %get-tuple-element.39), channel_id=1, source_target_pairs={{0,1},{1,0},{2,3},{3,2},{4,5},{5,4},{6,7},{7,6},{8,9},{9,8},{10,11... | collective-permute-start | bytes 491528 | tf_op jit(solution)/shard_map/ppermute | solution.py:400
  55.0 4.3 %collective-permute-start.4 = (f32[56,128]{1,0:T(8,128)S(1)}, f32[56,128]{1,0:T(8,128)S(1)}, u32[]{:S(2)}, u32[]{:S(2)}) collective-permute-start(f32[56,128]{1,0:T(8,128)S(1)} %shard_map.109.mine_ref), channel_id=1, source_target_pairs={{0,17},{1,16},{2,19},{3,18},{4,21},{5,20},{6,23},{7,22},{8,25},{9,... | collective-permute-start | bytes 86024 | tf_op jit(solution)/shard_map/ppermute | solution.py:403
  68.6 1.4 %collective-permute-start.5 = (f32[8,40,128]{2,1,0:T(8,128)S(1)}, f32[8,40,128]{2,1,0:T(8,128)S(1)}, u32[]{:S(2)}, u32[]{:S(2)}) collective-permute-start(f32[8,40,128]{2,1,0:T(8,128)S(1)} %all_to_all.23.means_ref), channel_id=1, source_target_pairs={{0,1},{1,0},{2,3},{3,2},{4,5},{5,4},{6,7},{7,6},{8,9},{9,8},{10,11... | collective-permute-start | bytes 491528 | tf_op jit(solution)/shard_map/ppermute | solution.py:400

commit v10 on v9

--- a/solution.py
+++ b/solution.py
@@ -137,7 +137,7 @@
     small = [(firm_hbm, firm_ref), (predictor_hbm, predictor_ref), (outcome_hbm, outcome_ref), (dy_hbm, dy_ref)]
     copies = [pltpu.make_async_copy(src, dst, sems.at[i]) for i, (src, dst) in enumerate(small)]
     count = firm_ref.shape[0]
-    chunk = max(1, count // 4)
+    chunk = max(1, count // 2)
     starts = list(range(0, count, chunk))
     for i, a in enumerate(starts):
         span = slice(a * LANES, (a + chunk) * LANES)

time: 71.8 us -> 71.6 us (level)
  no operation moved by 1% of the time
where the time goes in v10:
time: 71.6 us; the launch traced here: 71.3 us
  blocking collectives  45.7 us (64%)
  Pallas kernels  12 us (17%)
  waiting for transfers between devices  8.02 us (11%)
  starting transfers between devices  4.63 us (6%)
  between operations  0.72 us (1%)
    all_to_all x4, blocking collectives, across(): return lax.all_to_all(v, AXIS, 0, 0, axis_index_groups=groups)  45.7 us
    pallas_call x11, Pallas kernels, call(): pl.pallas_call(kernel, out_shape=tuple(outs), in_specs=in_specs or [VMEM]...  12 us
    ppermute x2, waiting for transfers between devices, to_half(): return lax.ppermute(v, AXIS, pairs)  6.38 us
    ppermute x2, starting transfers between devices, to_half(): return lax.ppermute(v, AXIS, pairs)  3.91 us
    ppermute x4, waiting for transfers between devices, to_core(): return lax.ppermute(v, AXIS, partner)  1.64 us
  transfers between devices with their start and end apart: 6, of which 6 were waited for; matrix products, arithmetic and copies ran while one was open for 0% of the time, Pallas kernels for 6%

profile of v10, /device:TPU:0, one launch (start us, length us, event | category | flops | bytes accessed | tf_op | source)
XLA Modules:
  0.0 71.3 jit_solution(12389266600530846304)
XLA Ops:
  0.6 3.9 %shard_map.102 = (f32[2048,128]{1,0:T(8,128)S(1)}, f32[16,128]{1,0:T(8,128)S(1)}, f32[16,128]{1,0:T(8,128)S(1)}, s32[16,128]{1,0:T(8,128)S(1)}, bf16[2048,256]{1...) custom-call(f32[2048,128]{1,0:T(8,128)} %x_hbm.1, f32[16,128]{1,0:T(8,128)} %bitcast.16, f32[16,128]{1,0:T(8,128)} %bitcast.17, ...), custom_call_target="tpu_custom_call" | custom-call | flops 1342177280 | bytes 3760128 | tf_op jit(solution)/shard_map/pallas_call | solution.py:353
  4.5 0.5 collective-permute-start
  5.0 1.4 %shard_map.103 = f32[8,136,128]{2,1,0:T(8,128)S(1)} custom-call(bf16[2048,256]{1,0:T(8,128)(2,1)S(1)} %get-tuple-element.29.pairs_ref, f32[16,128]{1,0:T(8,128)S(1)} %get-tuple-element.28.z1_ref.z_ref, f32[16,128]{1,0:T(8,128)S(1)} %get-tuple-element.30.weight_ref, s32[16,128]{1,0:T(8,128)S(1)} %get-tuple-element.31.dy_ref), custom_call_target="tpu_custom_call" | custom-call | flops 1073741824 | bytes 1630208 | tf_op jit(solution)/shard_map/pallas_call | solution.py:353
  6.4 0.1 collective-permute-done
  6.6 0.1 add.6
  6.7 16.3 %all_to_all.20.in_ref = f32[8,136,128]{2,1,0:T(8,128)S(1)} all-to-all(f32[8,136,128]{2,1,0:T(8,128)S(1)} %add.6), channel_id=1, replica_groups={{0,2,4,6,8,10,12,14},{1,3,5,7,9,11,13,15},{16,18,20,22,24,26,28,30},{17..., dimensions={0} | all-to-all | bytes 1114112 | tf_op jit(solution)/shard_map/all_to_all | solution.py:406
  23.0 2.7 %collective-permute-start.1 = (f32[136,128]{1,0:T(8,128)S(1)}, f32[136,128]{1,0:T(8,128)S(1)}, u32[]{:S(2)}, u32[]{:S(2)}) collective-permute-start(f32[136,128]{1,0:T(8,128)S(1)} %shard_map.104.mine_ref), channel_id=1, source_target_pairs={{0,16},{1,17},{2,18},{3,19},{4,20},{5,21},{6,22},{7,23},{8,24},{9,... | collective-permute-start | bytes 208904 | tf_op jit(solution)/shard_map/ppermute | solution.py:403
  25.6 3.4 %collective-permute-done.1.got_ref = f32[136,128]{1,0:T(8,128)S(1)} collective-permute-done((f32[136,128]{1,0:T(8,128)S(1)}, f32[136,128]{1,0:T(8,128)S(1)}, u32[]{:S(2)}, u32[]{:S(2)}) %collective-permute-start.1) | collective-permute-done | bytes 69664 | tf_op jit(solution)/shard_map/ppermute | solution.py:403
  29.0 0.1 shard_map.105
  29.1 10.9 %all_to_all.21.means_ref = f32[8,136,128]{2,1,0:T(8,128)S(1)} all-to-all(f32[8,136,128]{2,1,0:T(8,128)S(1)} %shard_map.105), channel_id=1, replica_groups={{0,2,4,6,8,10,12,14},{1,3,5,7,9,11,13,15},{16,18,20,22,24,26,28,30},{17..., dimensions={0} | all-to-all | bytes 1114112 | tf_op jit(solution)/shard_map/all_to_all | solution.py:406
  40.0 0.0 collective-permute-start.2
  40.0 0.0 copy-start
  40.0 0.0 copy-start.1
  40.0 1.5 %shard_map.106 = (f32[2048,128]{1,0:T(8,128)S(1)}, f32[16,128]{1,0:T(8,128)S(1)}) custom-call(f32[2048,128]{1,0:T(8,128)S(1)} %get-tuple-element.27.x_ref, f32[16,128]{1,0:T(8,128)S(1)} %get-tuple-element.28.z1_ref.z_ref, f32[8,136,128]{2,1,0:T(8,128)S(1)} %all_to_all.21.means_ref, s32[16,128]{1,0:T(8,128)S(1)} %get-tuple-element.31.dy_ref), custom_call_target="tpu_custom_call" | custom-call | flops 1073741824 | bytes 2678784 | tf_op jit(solution)/shard_map/pallas_call | solution.py:353
  41.6 0.4 collective-permute-done.2.means_ref
  42.0 0.0 copy-done
  42.0 0.0 copy-done.1
  42.0 2.0 %shard_map.107 = (f32[2048,128]{1,0:T(8,128)S(1)}, f32[16,128]{1,0:T(8,128)S(1)}, bf16[2048,256]{1,0:T(8,128)(2,1)S(1)}, f32[8,40,128]{2,1,0:T(8,128)S(1)}) custom-call(f32[2048,128]{1,0:T(8,128)S(1)} %get-tuple-element.33.x_ref, f32[16,128]{1,0:T(8,128)S(1)} %get-tuple-element.34.z_ref, f32[8,136,128]{2,1,0:T(8,128)S(1)} %collective-permute-done.2.means_ref, ...), custom_call_target="tpu_custom_call" | custom-call | flops 1342177280 | bytes 3915776 | tf_op jit(solution)/shard_map/pallas_call | solution.py:353
  43.9 0.2 collective-permute-start.3
  44.1 0.9 %shard_map.108 = (f32[8,40,128]{2,1,0:T(8,128)S(1)}, f32[8,16,128]{2,1,0:T(8,128)S(1)}) custom-call(f32[2048,128]{1,0:T(8,128)S(1)} %get-tuple-element.35.x2_ref.x_ref, f32[16,128]{1,0:T(8,128)S(1)} %get-tuple-element.36.z2_ref.z_ref, bf16[2048,256]{1,0:T(8,128)(2,1)S(1)} %get-tuple-element.37.weighted_ref, f32[16,128]{1,0:T(8,128)S(1)} %get-tuple-element.30.weight_ref, ...), custom_call_target="tpu_custom_call" | custom-call | flops 536870912 | bytes 2359296 | tf_op jit(solution)/shard_map/pallas_call | solution.py:353
  45.1 0.3 collective-permute-done.3
  45.5 9.3 %all_to_all.22.in_ref = f32[8,56,128]{2,1,0:T(8,128)S(1)} all-to-all(f32[8,56,128]{2,1,0:T(8,128)S(1)} %pad_maximum_fusion), channel_id=1, replica_groups={{0,2,4,6,8,10,12,14},{1,3,5,7,9,11,13,15},{16,18,20,22,24,26,28,30},{17..., dimensions={0} | all-to-all | bytes 458752 | tf_op jit(solution)/shard_map/all_to_all | solution.py:406
  54.8 1.3 %collective-permute-start.4 = (f32[56,128]{1,0:T(8,128)S(1)}, f32[56,128]{1,0:T(8,128)S(1)}, u32[]{:S(2)}, u32[]{:S(2)}) collective-permute-start(f32[56,128]{1,0:T(8,128)S(1)} %shard_map.109.mine_ref), channel_id=1, source_target_pairs={{0,17},{1,16},{2,19},{3,18},{4,21},{5,20},{6,23},{7,22},{8,25},{9,... | collective-permute-start | bytes 86024 | tf_op jit(solution)/shard_map/ppermute | solution.py:403
  56.0 3.0 %collective-permute-done.4.got_ref = f32[56,128]{1,0:T(8,128)S(1)} collective-permute-done((f32[56,128]{1,0:T(8,128)S(1)}, f32[56,128]{1,0:T(8,128)S(1)}, u32[]{:S(2)}, u32[]{:S(2)}) %collective-permute-start.4) | collective-permute-done | bytes 28704 | tf_op jit(solution)/shard_map/ppermute | solution.py:403
  59.0 0.1 shard_map.110
  59.1 9.3 %all_to_all.23.means_ref = f32[8,40,128]{2,1,0:T(8,128)S(1)} all-to-all(f32[8,40,128]{2,1,0:T(8,128)S(1)} %get-tuple-element.41), channel_id=1, replica_groups={{0,2,4,6,8,10,12,14},{1,3,5,7,9,11,13,15},{16,18,20,22,24,26,28,30},{17..., dimensions={0} | all-to-all | bytes 327680 | tf_op jit(solution)/shard_map/all_to_all | solution.py:406
  68.4 0.0 collective-permute-start.5
  68.4 0.6 shard_map.111
  69.1 0.7 %collective-permute-done.5.means_ref = f32[8,40,128]{2,1,0:T(8,128)S(1)} collective-permute-done((f32[8,40,128]{2,1,0:T(8,128)S(1)}, f32[8,40,128]{2,1,0:T(8,128)S(1)}, u32[]{:S(2)}, u32[]{:S(2)}) %collective-permute-start.5) | collective-permute-done | bytes 163872 | tf_op jit(solution)/shard_map/ppermute | solution.py:400
  69.8 1.4 %shard_map.112 = (f32[2048,128]{1,0:T(8,128)}, f32[16,128]{1,0:T(8,128)}, f32[4,128]{1,0:T(4,128)}, f32[1,4]{1,0:T(1,128)}) custom-call(f32[2048,128]{1,0:T(8,128)S(1)} %get-tuple-element.42.x_ref, f32[16,128]{1,0:T(8,128)S(1)} %get-tuple-element.43.z_ref, f32[8,40,128]{2,1,0:T(8,128)S(1)} %collective-permute-done.5.means_ref, ...), custom_call_target="tpu_custom_call" | custom-call | flops 268435456 | bytes 2304016 | tf_op jit(solution)/shard_map/pallas_call | solution.py:353
  (4 shorter events, 0.1 us)
Async XLA Ops:
  4.5 2.1 %collective-permute-start = (f32[8,136,128]{2,1,0:T(8,128)S(1)}, f32[8,136,128]{2,1,0:T(8,128)S(1)}, u32[]{:S(2)}, u32[]{:S(2)}) collective-permute-start(f32[8,136,128]{2,1,0:T(8,128)S(1)} %get-tuple-element.32), channel_id=1, source_target_pairs={{0,1},{1,0},{2,3},{3,2},{4,5},{5,4},{6,7},{7,6},{8,9},{9,8},{10,11... | collective-permute-start | bytes 1671176 | tf_op jit(solution)/shard_map/ppermute | solution.py:400
  23.0 6.0 %collective-permute-start.1 = (f32[136,128]{1,0:T(8,128)S(1)}, f32[136,128]{1,0:T(8,128)S(1)}, u32[]{:S(2)}, u32[]{:S(2)}) collective-permute-start(f32[136,128]{1,0:T(8,128)S(1)} %shard_map.104.mine_ref), channel_id=1, source_target_pairs={{0,16},{1,17},{2,18},{3,19},{4,20},{5,21},{6,22},{7,23},{8,24},{9,... | collective-permute-start | bytes 208904 | tf_op jit(solution)/shard_map/ppermute | solution.py:403
  40.0 2.0 %collective-permute-start.2 = (f32[8,136,128]{2,1,0:T(8,128)S(1)}, f32[8,136,128]{2,1,0:T(8,128)S(1)}, u32[]{:S(2)}, u32[]{:S(2)}) collective-permute-start(f32[8,136,128]{2,1,0:T(8,128)S(1)} %all_to_all.21.means_ref), channel_id=1, source_target_pairs={{0,1},{1,0},{2,3},{3,2},{4,5},{5,4},{6,7},{7,6},{8,9},{9,8},{10,11... | collective-permute-start | bytes 1671176 | tf_op jit(solution)/shard_map/ppermute | solution.py:400
  40.0 2.0 %copy-start = (s32[2048,1]{0,1:T(1,128)S(1)}, s32[2048,1]{0,1:T(1,128)}, u32[]{:S(2)}) copy-start(s32[2048,1]{0,1:T(1,128)} %param.12) | copy-start | bytes 24580
  40.0 2.0 %copy-start.1 = (s32[2048]{0:T(1024)S(1)}, s32[2048]{0:T(1024)}, u32[]{:S(2)}) copy-start(s32[2048]{0:T(1024)} %param.13) | copy-start | bytes 24580
  43.9 1.5 %collective-permute-start.3 = (f32[8,40,128]{2,1,0:T(8,128)S(1)}, f32[8,40,128]{2,1,0:T(8,128)S(1)}, u32[]{:S(2)}, u32[]{:S(2)}) collective-permute-start(f32[8,40,128]{2,1,0:T(8,128)S(1)} %get-tuple-element.39), channel_id=1, source_target_pairs={{0,1},{1,0},{2,3},{3,2},{4,5},{5,4},{6,7},{7,6},{8,9},{9,8},{10,11... | collective-permute-start | bytes 491528 | tf_op jit(solution)/shard_map/ppermute | solution.py:400
  54.8 4.3 %collective-permute-start.4 = (f32[56,128]{1,0:T(8,128)S(1)}, f32[56,128]{1,0:T(8,128)S(1)}, u32[]{:S(2)}, u32[]{:S(2)}) collective-permute-start(f32[56,128]{1,0:T(8,128)S(1)} %shard_map.109.mine_ref), channel_id=1, source_target_pairs={{0,17},{1,16},{2,19},{3,18},{4,21},{5,20},{6,23},{7,22},{8,25},{9,... | collective-permute-start | bytes 86024 | tf_op jit(solution)/shard_map/ppermute | solution.py:403
  68.4 1.4 %collective-permute-start.5 = (f32[8,40,128]{2,1,0:T(8,128)S(1)}, f32[8,40,128]{2,1,0:T(8,128)S(1)}, u32[]{:S(2)}, u32[]{:S(2)}) collective-permute-start(f32[8,40,128]{2,1,0:T(8,128)S(1)} %all_to_all.23.means_ref), channel_id=1, source_target_pairs={{0,1},{1,0},{2,3},{3,2},{4,5},{5,4},{6,7},{7,6},{8,9},{9,8},{10,11... | collective-permute-start | bytes 491528 | tf_op jit(solution)/shard_map/ppermute | solution.py:400
